TPU v7x, 32 devices: a whole 2x2x4 slice. The times are simulated.
32 devices in a mesh: wide: 8 (over z, y), narrow: 4 (over x, core).
Axes of the slice: x: 2, y: 2, z: 4, core: 2. Of those that a mesh axis runs over, the one named last changes fastest.
Arguments:
- frames: bfloat16 [128, 8, 5, 32, 32, 3], P(('wide', 'narrow')), may hold values from -11 to 11
- tokens: bfloat16 [50176, 2048], P(('wide', 'narrow')), may hold values from -11 to 11
- stem_cotangent: bfloat16 [262144, 64], P(('wide', 'narrow')), may hold values from -6 to 6
- crop_counts: int32 [64], replicated, may hold values from 1 to 5, 128 in all
- labels: int32 [64], replicated, may hold values from 0 to 173
- stem_weight: bfloat16 [588, 64], P(None, 'wide'), may hold values from -0.25 to 0.25
- stem_gain: bfloat16 [64], P('wide'), may hold values from 0.099609375 to 1.8984375
- stem_shift: bfloat16 [64], P('wide'), may hold values from -2 to 2
- w_squeeze: bfloat16 [2048, 512], P('wide'), may hold values from -0.125 to 0.125
- next_kernel: bfloat16 [9, 512], P(None, 'wide'), may hold values from -2 to 2
- scale_kernel: bfloat16 [9, 512], P(None, 'wide'), may hold values from -2 to 2
- w_expand: bfloat16 [512, 2048], P(None, 'wide'), may hold values from -0.25 to 0.25
- w_reduce: bfloat16 [2048, 512], P('wide'), may hold values from -0.125 to 0.125
- gain_one: bfloat16 [512], P('wide'), may hold values from 0.099609375 to 1.8984375
- shift_one: bfloat16 [512], P('wide'), may hold values from -2 to 2
- w_spatial: bfloat16 [9, 512, 512], P(None, 'wide'), may hold values from -0.09375 to 0.09375
- gain_two: bfloat16 [512], P('wide'), may hold values from 0.099609375 to 1.8984375
- shift_two: bfloat16 [512], P('wide'), may hold values from -2 to 2
- w_restore: bfloat16 [512, 2048], P('wide'), may hold values from -0.25 to 0.25
- gain_three: bfloat16 [2048], P('wide'), may hold values from 0.099609375 to 1.8984375
- shift_three: bfloat16 [2048], P('wide'), may hold values from -2 to 2
- w_class: bfloat16 [2048, 174], P('wide'), may hold values from -0.5 to 0.5
- class_bias: bfloat16 [174], replicated, may hold values from -3 to 3
Outputs:
- activations: bfloat16 [50176, 2048], P(('wide', 'narrow'))
- stem_features: bfloat16 [262144, 64], P(('wide', 'narrow'))
- tokens_grad: bfloat16 [50176, 2048], P(('wide', 'narrow'))
- stem_weight_grad: float32 [588, 64], P(None, 'wide')
- stem_gain_grad: float32 [64], P('wide')
- stem_shift_grad: float32 [64], P('wide')
- squeeze_grad: float32 [2048, 512], P('wide')
- next_kernel_grad: float32 [9, 512], P(None, 'wide')
- scale_kernel_grad: float32 [9, 512], P(None, 'wide')
- expand_grad: float32 [512, 2048], P(None, 'wide')
- reduce_grad: float32 [2048, 512], P('wide')
- gain_one_grad: float32 [512], P('wide')
- shift_one_grad: float32 [512], P('wide')
- spatial_grad: float32 [9, 512, 512], P(None, 'wide')
- gain_two_grad: float32 [512], P('wide')
- shift_two_grad: float32 [512], P('wide')
- restore_grad: float32 [512, 2048], P('wide')
- gain_three_grad: float32 [2048], P('wide')
- shift_three_grad: float32 [2048], P('wide')
- class_grad: float32 [2048, 174], P('wide')
- class_bias_grad: float32 [174], replicated
- loss: float32 [], replicated
Inputs may be any that keep to these rules, and one draw needn't show every extreme that they name: `crop_counts`: the counts sum to 128, and some video has 5 views.
All inputs are finite; a program needn't handle non-finite values.
Results may differ from a plain program's by a relative error of at most 0.015.
Values may be sent and summed in bfloat16 or wider, within the bound.
No kernel may reach another device: no remote copies, remote signals or barrier semaphores. Data moves between devices by JAX's collectives and lax.ppermute only.
A program may use at most 320 MiB of HBM per device.

v0:
```python
import functools

import jax
import jax.numpy as jnp
from jax import lax
from jax.experimental import pallas as pl
from jax.experimental.pallas import tpu as pltpu
from jax.sharding import PartitionSpec as P

C = 2048
B = 512
R = 512
CLASSES = 174
SEG = 8
SIDE = 7
PER_VIEW = SEG * SIDE * SIDE

epsilon = 1e-05
loss_scale = 1024.0

AXES = ("wide", "narrow")
f32 = jnp.float32
bf16 = jnp.bfloat16


def product(first_operand, second_operand):
    return jnp.dot(first_operand, second_operand, preferred_element_type=f32)


def product_left(first_operand, second_operand):
    return lax.dot_general(
        first_operand, second_operand, (((0,), (0,)), ((), ())), preferred_element_type=f32
    )


def product_right(first_operand, second_operand):
    return lax.dot_general(
        first_operand, second_operand, (((1,), (1,)), ((), ())), preferred_element_type=f32
    )


def exchange(values, mask):
    size = lax.axis_size(AXES)
    return lax.ppermute(values, AXES, [(index, index ^ mask) for index in range(size)])


def own_bit(bit):
    return (lax.axis_index(AXES) >> bit) & 1


def total(values):
    bits = lax.axis_size(AXES).bit_length() - 1
    values = values + exchange(values, 1)
    for bit in range(1, bits, 2):
        masks = [1 << bit]
        if bit + 1 < bits:
            masks += [2 << bit, 3 << bit]
        parts = [exchange(values, mask) for mask in masks]
        for part in parts:
            values = values + part
    return values


def swap_total(values):
    size = lax.axis_size(AXES)
    copies = jnp.broadcast_to(values[None], (size,) + values.shape)
    return jnp.sum(lax.all_to_all(copies, AXES, 0, 0, tiled=True), 0)


def beside(run, inputs, sends, more=()):
    inputs, arrays = lax.optimization_barrier((tuple(inputs), [array for array, _ in sends]))
    came = [exchange(array, mask) for array, (_, mask) in zip(arrays, sends)]
    return lax.optimization_barrier((run(*inputs), came, tuple(more)))


def launch(run, inputs, sends):
    inputs, arrays = lax.optimization_barrier((tuple(inputs), [array for array, _ in sends]))
    came = [exchange(array, mask) for array, (_, mask) in zip(arrays, sends)]
    return lax.optimization_barrier(run(*inputs)), came


class Gather:
    def __init__(self, block):
        self.block = block

    def depth(self):
        return [(self.block, mask) for mask in (8, 16, 24)]

    def take_depth(self, came):
        self.four = join([part[None] for part in (self.block, *came)])

    def second(self):
        return [(self.four, 4)]

    def take_second(self, came):
        self.eight = join([self.four, came[0]])

    def third(self):
        return [(self.eight, 2)]

    def take_third(self, came):
        self.other = came[0]

    def core(self):
        return [(self.eight, 1), (self.other, 1)]

    def take_core(self, came):
        self.arrays = (self.eight, self.other) + tuple(came)


class Sum:
    def __init__(self, half, shape, lead):
        self.keep, self.send = half
        self.shape, self.lead, self.axes = shape, lead, "zyx"

    def core(self):
        return [(self.send, 1)]

    def take_core(self, came):
        self.values = (self.keep + came[0].astype(f32)).reshape(self.shape)

    def split(self, letter):
        place = self.lead + self.axes.index(letter)
        self.axes = self.axes.replace(letter, "")
        bit = {"x": 1, "y": 2, "z": 3}[letter]
        span = 3 if letter == "z" else 1
        mine = (lax.axis_index(AXES) >> bit) & span
        found = []
        for mask in range(1, span + 1):
            part = lax.dynamic_index_in_dim(self.values, mine ^ mask, place, keepdims=False)
            found.append((part.astype(bf16), mask << bit))
        self.values = lax.dynamic_index_in_dim(self.values, mine, place, keepdims=False)
        return found

    def split_parts(self, letter, at):
        ((send, mask),) = self.split(letter)
        return [(send[:at], mask)], [(send[at:], mask)]

    def take_parts(self, first, second):
        self.take([jnp.concatenate([first[0], second[0]])])

    def take(self, came):
        for part in came:
            self.values = self.values + part.astype(f32)

    def spread(self):
        self.part = self.values.astype(bf16)
        return [(self.part, mask) for mask in (1, 2, 3)]

    def take_spread(self, came):
        own, (core, over_x, both) = self.part, came
        odd, far = own_bit(0) == 1, own_bit(1) == 1
        near = [jnp.where(odd, core, own), jnp.where(odd, own, core)]
        away = [jnp.where(odd, both, over_x), jnp.where(odd, over_x, both)]
        self.whole = jnp.stack(
            [jnp.where(far, away[0], near[0]), jnp.where(far, away[1], near[1]),
             jnp.where(far, near[0], away[0]), jnp.where(far, near[1], away[1])]
        ).astype(f32)


def gathered(w_squeeze, w_expand, w_reduce, w_spatial, w_restore, w_class):
    def whole(weight, axis):
        return lax.all_gather(weight, "wide", axis=axis, tiled=True)

    def as_blocks(blocks):
        ordered = blocks.reshape((4, 2, 2, 2) + blocks.shape[1:])
        return [
            ordered[:, :, far, core].swapaxes(0, 1).reshape((8,) + blocks.shape[1:])
            for core in range(2)
            for far in range(2)
        ]

    squeeze = whole(w_squeeze, 0).reshape(32, -1, R)
    expand = whole(w_expand, 1).reshape(4, 2, PAIR_ROWS, 8, TILE).transpose(3, 0, 2, 1, 4)
    expand = expand.reshape(32, PAIR_ROWS, 2 * TILE)
    reduce = whole(w_reduce, 0).reshape(32, -1, B)
    spatial = whole(w_spatial, 1).reshape(9, 32, 16, B).swapaxes(0, 1).reshape(32, -1, B)
    restore = whole(w_restore, 0).reshape(8, 64, 4, B).swapaxes(1, 2).reshape(32, 64, B)
    classes = jnp.pad(whole(w_class, 0), ((0, 0), (0, TILE - CLASSES)))
    classes = classes.reshape(32, 2, CLASS_ROWS, TILE).swapaxes(1, 2).reshape(32, CLASS_ROWS, B)
    late = jnp.concatenate([restore, classes], axis=1)
    pair = jnp.concatenate([reduce, expand], axis=1)
    return as_blocks(squeeze), as_blocks(pair), as_blocks(spatial), late


def reduced(buffer, reduce_half, expand_half, squeeze_half):
    def whole(half, grain):
        keep, send = (part.astype(bf16) for part in half)
        shape = keep.shape[:1] + (-1, grain) + keep.shape[2:]
        both = jnp.stack([keep.reshape(shape), send.reshape(shape)], axis=2)
        return both.reshape(keep.shape[:1] + (-1,) + keep.shape[2:])

    def scattered(grad, axis):
        part = lax.psum_scatter(grad, "wide", scatter_dimension=axis, tiled=True)
        return lax.psum(part, "narrow").astype(f32)

    def columns(tiles):
        return tiles.swapaxes(0, 1).reshape(tiles.shape[1], -1)

    restore = buffer[:, :RESTORE_ROWS].reshape(8, 4, RESTORE_ROWS, WIDE).swapaxes(1, 2).reshape(B, C)
    spatial = buffer[:, RESTORE_ROWS:].reshape(32, 9, 16, B).swapaxes(0, 1).reshape(9, B, B)
    return (
        scattered(restore, 0),
        scattered(spatial, 1),
        scattered(columns(whole(reduce_half, 128)), 1).T,
        scattered(columns(whole(expand_half, 128)), 1),
        scattered(columns(whole(squeeze_half, 128)), 1).T,
    )


CELLS = SIDE * SIDE
HALF = 2 * PER_VIEW
PADDED = SIDE + 2
MIB = 1 << 20
LANES = 128
TILE = 256


def cell_place(cell):
    return (cell // SIDE + 1) * PADDED + cell % SIDE + 1


def tap_place(cell, tap):
    return cell_place(cell) + (tap // 3 - 1) * PADDED + tap % 3 - 1


def dot_nt(first_operand, second_operand):
    return lax.dot_general(
        first_operand, second_operand, (((1,), (1,)), ((), ())), preferred_element_type=f32
    )


def dot_tn(first_operand, second_operand):
    return lax.dot_general(
        first_operand, second_operand, (((0,), (0,)), ((), ())), preferred_element_type=f32
    )


def sigmoid(values):
    return 0.5 * jnp.tanh(0.5 * values) + 0.5


def constants(sums, affine, count):
    mean = sums[0:1] / count
    inverse = lax.rsqrt(sums[1:2] / count - mean * mean + epsilon)
    return mean, inverse, affine[0:1], affine[1:2]


def spread(row, rows=16):
    return jnp.broadcast_to(row, (rows, row.shape[1]))


def lanes(index, width):
    return pl.ds(pl.multiple_of(index * width, width), width)


def clear_border(ref):
    zero = jnp.zeros(ref.shape[1:], ref.dtype)
    for place in range(PADDED * PADDED):
        if place // PADDED in (0, PADDED - 1) or place % PADDED in (0, PADDED - 1):
            ref[place] = zero


def fold(values):
    return values[0:8] + values[8:16]


def half_spec(width):
    return pl.BlockSpec((HALF, width), lambda step, *_: (step, 0))


def whole_spec(shape):
    return pl.BlockSpec(shape, lambda *_: (0,) * len(shape), pipeline_mode=pl.Buffered(1))


def whole_out(shape):
    return pl.BlockSpec(shape, lambda *_: (0,) * len(shape))


WIDE = 512
GROUPS = C // WIDE


def group_spec():
    return pl.BlockSpec((HALF, WIDE), lambda half, group: (half, group))


def row_spec(rows):
    return pl.BlockSpec((rows, WIDE), lambda half, group: (0, group))


def view_spec(rows):
    return pl.BlockSpec((1, rows, WIDE), lambda half, group: (half, 0, group))


def first_group():
    return pl.program_id(1) == 0


def last_group():
    return pl.program_id(1) == GROUPS - 1


ANY = pl.BlockSpec(memory_space=pl.ANY)
SCALAR = pl.BlockSpec(memory_space=pltpu.SMEM)


def kernel_call(kernel, steps, in_specs, out_specs, out_shapes, scratch, flops,
                transcendentals=0, after=(), vmem=60, aliases=None):
    known = len(in_specs)
    grid = steps if isinstance(steps, tuple) else (steps,)

    def body(*refs):
        kernel(*refs[:known], *refs[known + len(after) :])

    call = pl.pallas_call(
        body,
        grid=grid,
        in_specs=list(in_specs) + [ANY] * len(after),
        out_specs=out_specs,
        out_shape=out_shapes,
        scratch_shapes=scratch,
        input_output_aliases=aliases or {},
        compiler_params=pltpu.CompilerParams(
            dimension_semantics=("arbitrary",) * len(grid), vmem_limit_bytes=vmem * MIB
        ),
        cost_estimate=pl.CostEstimate(
            flops=2 * flops, bytes_accessed=16 * MIB, transcendentals=transcendentals
        ),
    )
    return lambda *operands: call(*operands, *after)


def block_copies(me, sources, target, semaphores, rows=None, lanes_at=None, target_rows=None):
    copies = []
    for low_mask, source in zip((0, 2, 1, 3), sources):
        for entry in range(8):
            mask = low_mask | ((entry // 4) * 4) | ((entry % 4) << 3)
            taken, place = source.at[entry], target.at[me ^ mask]
            if rows is not None:
                taken = taken.at[rows] if lanes_at is None else taken.at[rows, lanes_at]
            if target_rows is not None:
                place = place.at[target_rows]
            copies.append(pltpu.make_async_copy(taken, place, semaphores.at[len(copies)]))
    return copies


PAIR_ROWS = 64


def reduce_copies(me, sources, target, semaphores):
    return block_copies(me, sources, target, semaphores, slice(0, PAIR_ROWS))


def expand_copies(me, sources, target, semaphores):
    rows = slice(PAIR_ROWS, 2 * PAIR_ROWS)
    found = []
    for part in range(2):
        found += block_copies(
            me, sources, target, semaphores.at[part], rows,
            slice(part * TILE, (part + 1) * TILE),
            slice(part * PAIR_ROWS, (part + 1) * PAIR_ROWS),
        )
    return found


def start(copies):
    for copy in copies:
        copy.start()


def wait(copies):
    for copy in copies:
        copy.wait()


def join_kernel(*refs):
    *sources, out_ref, semaphores = refs
    copies, top = [], 0
    for source in sources:
        count = source.shape[0]
        copies.append(
            pltpu.make_async_copy(
                source, out_ref.at[top : top + count], semaphores.at[len(copies)]
            )
        )
        top += count
    start(copies)
    wait(copies)


def join(arrays):
    count = sum(array.shape[0] for array in arrays)
    return kernel_call(
        join_kernel,
        1,
        [ANY] * len(arrays),
        ANY,
        jax.ShapeDtypeStruct((count,) + arrays[0].shape[1:], arrays[0].dtype),
        [pltpu.SemaphoreType.DMA((len(arrays),))],
        1000000,
        vmem=16,
    )(*arrays)


def first_step():
    return pl.program_id(0) == 0


def very_first():
    return (pl.program_id(0) == 0) & (pl.program_id(1) == 0)


def add_moments(sums_ref, where, first, second):
    sums_ref[0:1, where] += jnp.sum(first, 0, keepdims=True)
    sums_ref[1:2, where] += jnp.sum(second, 0, keepdims=True)


def mixing_kernel(
    me_ref, block_a, block_b, block_c, block_d, tokens_ref, next_ref, scale_ref,
    upcoming_ref, differ_ref, mixed_ref, natural, ahead, padded, squeeze_ref, semaphores,
):
    @pl.when(first_step())
    def _():
        copies = block_copies(
            me_ref[0], (block_a, block_b, block_c, block_d), squeeze_ref, semaphores, slice(0, 64)
        )
        start(copies)
        natural[:, HALF:] = jnp.zeros((4, natural.shape[1] - HALF, LANES), f32)
        clear_border(ahead)
        clear_border(padded)
        wait(copies)

    def squeeze_step(step, carry):
        squeezed = product(
            tokens_ref[...], squeeze_ref[:, :, lanes(step, TILE)].reshape(C, TILE)
        )
        natural[2 * step, 0:HALF] = squeezed[:, 0:LANES]
        natural[2 * step + 1, 0:HALF] = squeezed[:, LANES:TILE]
        return carry

    lax.fori_loop(0, 2, squeeze_step, 0)
    segment = lax.broadcasted_iota(jnp.int32, (16, LANES), 0) % SEG
    not_last = (segment != SEG - 1).astype(f32)

    def mixing_step(step, carry):
        where = lanes(step, LANES)
        next_rows = [spread(next_ref[tap : tap + 1, where]) for tap in range(9)]
        for cell in range(CELLS):
            upcoming = natural[step, pl.ds(cell + CELLS, 16, stride=CELLS)] * not_last
            ahead[cell_place(cell)] = upcoming
            upcoming_ref[cell * 16 : cell * 16 + 16, where] = upcoming
        mean = jnp.zeros((16, LANES), f32)
        for cell in range(CELLS):
            differ = -natural[step, pl.ds(cell, 16, stride=CELLS)]
            for tap in range(9):
                differ = differ + ahead[tap_place(cell, tap)] * next_rows[tap]
            padded[cell_place(cell)] = differ
            differ_ref[cell * 16 : cell * 16 + 16, where] = differ
            mean = mean + differ
        mean = mean * (1.0 / CELLS)
        scale_rows = [spread(scale_ref[tap : tap + 1, where]) for tap in range(9)]
        for cell in range(CELLS):
            mixed = padded[cell_place(cell)] + mean
            for tap in range(9):
                mixed = mixed + padded[tap_place(cell, tap)] * scale_rows[tap]
            natural[step, pl.ds(cell, 16, stride=CELLS)] = mixed
        mixed_ref[:, where] = natural[step, 0:HALF].astype(bf16)
        return carry

    lax.fori_loop(0, 4, mixing_step, 0)


def mixing_block(me, squeeze, tokens, next_kernel, scale_kernel, after=()):
    rows = tokens.shape[0]
    return kernel_call(
        mixing_kernel,
        rows // HALF,
        [SCALAR, ANY, ANY, ANY, ANY, half_spec(C), whole_spec((9, R)), whole_spec((9, R))],
        [half_spec(R), half_spec(R), half_spec(R)],
        [jax.ShapeDtypeStruct((rows, R), f32), jax.ShapeDtypeStruct((rows, R), f32),
         jax.ShapeDtypeStruct((rows, R), bf16)],
        [pltpu.VMEM((4, HALF + CELLS + 7, LANES), f32),
         pltpu.VMEM((PADDED * PADDED, 16, LANES), f32),
         pltpu.VMEM((PADDED * PADDED, 16, LANES), f32),
         pltpu.VMEM((32, C // 32, R), bf16), pltpu.SemaphoreType.DMA((32,))],
        2 * rows * C * R,
        after=after,
    )(me, *squeeze, tokens, next_kernel, scale_kernel)


def gate_kernel(
    me_ref, block_a, block_b, block_c, block_d, tokens_ref, mixed_ref,
    logit_ref, gated_ref, pre_ref, sums_ref,
    tile, found, expand_ref, reduce_ref, expand_semaphores, reduce_semaphores,
):
    blocks = (block_a, block_b, block_c, block_d)
    for_expand = expand_copies(me_ref[0], blocks, expand_ref, expand_semaphores)
    for_reduce = reduce_copies(me_ref[0], blocks, reduce_ref, reduce_semaphores)
    group = pl.program_id(1)

    @pl.when(very_first())
    def _():
        start(for_expand)
        start(for_reduce)
        sums_ref[...] = jnp.zeros_like(sums_ref)
        wait(for_expand)

    for part in range(2):
        columns = expand_ref[pl.ds(8 * group + 4 * part, 4)].reshape(R, TILE)
        tile[:, part * TILE : (part + 1) * TILE] = product(mixed_ref[...], columns)
    for chunk in range(HALF // 16):
        rows = slice(chunk * 16, chunk * 16 + 16)
        logit = tile[rows]
        token = tokens_ref[rows].astype(f32)
        logit_ref[rows] = logit.astype(bf16)
        gated_ref[rows] = (token + token * sigmoid(logit)).astype(bf16)

    @pl.when(very_first())
    def _():
        wait(for_reduce)

    part = product(gated_ref[...], reduce_ref[pl.ds(8 * group, 8)].reshape(WIDE, B))

    @pl.when(first_group())
    def _():
        found[...] = part

    @pl.when(group > 0)
    def _():
        found[...] += part

    @pl.when(last_group())
    def _():
        first = jnp.zeros((8, B), f32)
        second = jnp.zeros((8, B), f32)
        for chunk in range(HALF // 16):
            rows = slice(chunk * 16, chunk * 16 + 16)
            value = found[rows]
            pre_ref[rows] = value
            first = first + fold(value)
            second = second + fold(value * value)
        add_moments(sums_ref, slice(0, B), first, second)


def gate_block(me, pair, tokens, mixed):
    rows = tokens.shape[0]
    return kernel_call(
        gate_kernel,
        (rows // HALF, GROUPS),
        [SCALAR] + [ANY] * 4 + [group_spec(), half_spec(R)],
        [group_spec(), group_spec(), half_spec(B), whole_out((2, B))],
        [jax.ShapeDtypeStruct((rows, C), bf16), jax.ShapeDtypeStruct((rows, C), bf16),
         jax.ShapeDtypeStruct((rows, B), f32), jax.ShapeDtypeStruct((2, B), f32)],
        [pltpu.VMEM((HALF, WIDE), f32), pltpu.VMEM((HALF, B), f32),
         pltpu.VMEM((32, R // 4, TILE), bf16), pltpu.VMEM((32, C // 32, B), bf16),
         pltpu.SemaphoreType.DMA((2, 32)), pltpu.SemaphoreType.DMA((32,))],
        4 * rows * C * R,
        2 * rows * C,
    )(me, *pair, tokens, mixed)


SPATIAL_ROWS = 9 * 16
RESTORE_ROWS = 64
CLASS_ROWS = 32
LATE_ROWS = RESTORE_ROWS + CLASS_ROWS


def restore_copy(late_ref, target, semaphore):
    return pltpu.make_async_copy(late_ref.at[:, 0:RESTORE_ROWS], target, semaphore)


def second_kernel(count, me_ref, block_a, block_b, block_c, block_d,
                  pre_ref, in_sums_ref, affine_ref,
                  hidden_ref, out_ref, sums_ref, natural, padded, tile, spatial_ref, semaphores):
    copies = block_copies(me_ref[0], (block_a, block_b, block_c, block_d), spatial_ref, semaphores)

    @pl.when(first_step())
    def _():
        start(copies)
        sums_ref[...] = jnp.zeros_like(sums_ref)
        clear_border(padded)

    border = SIDE * 16
    hidden_ref[0, 0:border] = jnp.zeros((border, 3 * B), bf16)
    hidden_ref[0, border + HALF :] = jnp.zeros((border, 3 * B), bf16)

    def hidden_step(step, carry):
        where = lanes(step, LANES)
        mean, inverse, gain, shift = (
            spread(row) for row in constants(in_sums_ref[:, where], affine_ref[:, where], count)
        )
        for chunk in range(HALF // 16):
            rows = slice(chunk * 16, chunk * 16 + 16)
            norm = (pre_ref[rows, where] - mean) * inverse * gain + shift
            natural[rows] = norm * sigmoid(norm)
        for cell in range(CELLS):
            padded[cell_place(cell)] = natural[pl.ds(cell, 16, stride=CELLS)].astype(bf16)
        for side in range(3):
            at = lanes(side * 4 + step, LANES)
            for cell in range(CELLS):
                hidden_ref[0, border + cell * 16 : border + cell * 16 + 16, at] = padded[
                    tap_place(cell, 3 + side)
                ]
        return carry

    lax.fori_loop(0, 4, hidden_step, 0)

    @pl.when(first_step())
    def _():
        wait(copies)

    def product_step(step, carry):
        where = lanes(step, TILE)
        found = None
        for row in range(3):
            taps = [
                spatial_ref[:, tap * 16 : tap * 16 + 16, where].reshape(B, TILE)
                for tap in range(3 * row, 3 * row + 3)
            ]
            part = product(
                hidden_ref[0, row * border : row * border + HALF], jnp.concatenate(taps, axis=0)
            )
            found = part if found is None else found + part
        tile[...] = found
        first = jnp.zeros((8, TILE), f32)
        second = jnp.zeros((8, TILE), f32)
        for chunk in range(HALF // 16):
            rows = slice(chunk * 16, chunk * 16 + 16)
            value = tile[rows]
            out_ref[rows, where] = value
            first = first + fold(value)
            second = second + fold(value * value)
        add_moments(sums_ref, where, first, second)
        return carry

    lax.fori_loop(0, B // TILE, product_step, 0)


def second_block(me, spatial, pre_one, sums, affine, count):
    rows = pre_one.shape[0]
    steps = rows // HALF
    deep = HALF + 2 * SIDE * 16
    return kernel_call(
        functools.partial(second_kernel, count),
        steps,
        [SCALAR, ANY, ANY, ANY, ANY, half_spec(B), whole_spec(sums.shape), whole_spec((2, B))],
        [pl.BlockSpec((1, deep, 3 * B), lambda step: (step, 0, 0)), half_spec(B),
         whole_out((2, B))],
        [jax.ShapeDtypeStruct((steps, deep, 3 * B), bf16), jax.ShapeDtypeStruct((rows, B), f32),
         jax.ShapeDtypeStruct((2, B), f32)],
        [pltpu.VMEM((HALF, LANES), f32), pltpu.VMEM((PADDED * PADDED, 16, LANES), bf16),
         pltpu.VMEM((HALF, TILE), f32), pltpu.VMEM((32, SPATIAL_ROWS, B), bf16),
         pltpu.SemaphoreType.DMA((32,))],
        18 * rows * B * B,
        2 * rows * B,
    )(me, *spatial, pre_one, sums, affine)


def third_kernel(count, pre_ref, in_sums_ref, affine_ref, late_ref,
                 hidden_ref, out_ref, sums_ref, natural, tile, restore_ref, semaphore):
    copy = restore_copy(late_ref, restore_ref, semaphore)
    group = pl.program_id(1)

    @pl.when(very_first())
    def _():
        copy.start()
        sums_ref[...] = jnp.zeros_like(sums_ref)

    @pl.when(first_group())
    def _():
        def hidden_step(step, carry):
            where = lanes(step, LANES)
            mean, inverse, gain, shift = (
                spread(row)
                for row in constants(in_sums_ref[:, where], affine_ref[:, where], count)
            )
            for cell in range(CELLS):
                rows = slice(cell * 16, cell * 16 + 16)
                norm = (pre_ref[rows, where] - mean) * inverse * gain + shift
                natural[pl.ds(cell, 16, stride=CELLS)] = norm * sigmoid(norm)
            hidden_ref[:, where] = natural[...].astype(bf16)
            return carry

        lax.fori_loop(0, 4, hidden_step, 0)

    @pl.when(very_first())
    def _():
        copy.wait()

    columns = restore_ref.reshape(8, 4, RESTORE_ROWS, B)[:, group].reshape(B, WIDE)
    tile[...] = product(hidden_ref[...], columns)
    first = jnp.zeros((8, WIDE), f32)
    second = jnp.zeros((8, WIDE), f32)
    for chunk in range(HALF // 16):
        rows = slice(chunk * 16, chunk * 16 + 16)
        value = tile[rows]
        out_ref[rows] = value.astype(bf16)
        first = first + fold(value)
        second = second + fold(value * value)
    add_moments(sums_ref, lanes(group, WIDE), first, second)


def third_block(pre_two, sums, affine, late, count):
    rows = pre_two.shape[0]
    return kernel_call(
        functools.partial(third_kernel, count),
        (rows // HALF, GROUPS),
        [half_spec(B), whole_spec(sums.shape), whole_spec((2, B)), ANY],
        [half_spec(B), group_spec(), whole_out((2, C))],
        [jax.ShapeDtypeStruct((rows, B), bf16), jax.ShapeDtypeStruct((rows, C), bf16),
         jax.ShapeDtypeStruct((2, C), f32)],
        [pltpu.VMEM((HALF, LANES), f32), pltpu.VMEM((HALF, WIDE), f32),
         pltpu.VMEM((32, RESTORE_ROWS, B), bf16), pltpu.SemaphoreType.DMA(())],
        2 * rows * B * C,
        2 * rows * B,
    )(pre_two, sums, affine, late)


def view_rows(chunk):
    return (chunk * 16) // PER_VIEW, (chunk * 16 + 8) // PER_VIEW


def fourth_kernel(count, pre_ref, gated_ref, in_sums_ref, affine_ref,
                  out_ref, slope_ref, views_ref):
    for part in range(WIDE // TILE):
        where = slice(part * TILE, (part + 1) * TILE)
        mean, inverse, gain, shift = (
            spread(row) for row in constants(in_sums_ref[:, where], affine_ref[:, where], count)
        )
        totals = [[jnp.zeros((8, TILE), f32) for _ in range(2)] for _ in range(3)]
        for chunk in range(HALF // 16):
            rows = slice(chunk * 16, chunk * 16 + 16)
            unit = (pre_ref[rows, where].astype(f32) - mean) * inverse
            summed = unit * gain + shift + gated_ref[rows, where].astype(f32)
            sigma = sigmoid(summed)
            output = summed * sigma
            slope = sigma + output * (1.0 - sigma)
            out_ref[rows, where] = output.astype(bf16)
            slope_ref[rows, where] = slope.astype(bf16)
            low, high = view_rows(chunk)
            for kind, value in enumerate((output, slope, slope * unit)):
                if low == high:
                    totals[kind][low] = totals[kind][low] + fold(value)
                else:
                    totals[kind][low] = totals[kind][low] + value[0:8]
                    totals[kind][high] = totals[kind][high] + value[8:16]
        for kind in range(3):
            for view in range(2):
                at = 2 * kind + view
                views_ref[0, at : at + 1, where] = jnp.sum(totals[kind][view], 0, keepdims=True)
        views_ref[0, 6:8, where] = jnp.zeros((2, TILE), f32)


def fourth_block(pre_three, gated, sums, affine, count):
    rows = pre_three.shape[0]
    steps = rows // HALF
    return kernel_call(
        functools.partial(fourth_kernel, count),
        (steps, GROUPS),
        [group_spec(), group_spec(), row_spec(sums.shape[0]), row_spec(2)],
        [group_spec(), group_spec(), view_spec(8)],
        [jax.ShapeDtypeStruct((rows, C), bf16), jax.ShapeDtypeStruct((rows, C), bf16),
         jax.ShapeDtypeStruct((steps, 8, C), f32)],
        [],
        20 * rows * C,
        2 * rows * C,
    )(pre_three, gated, sums, affine)


def view_scale(pooled_ref, view, where):
    return spread(pooled_ref[0, view : view + 1, where], 8)


def view_grad_rows(slope, pooled, chunk):
    low, high = view_rows(chunk)
    return slope * jnp.concatenate([pooled[low], pooled[high]], axis=0)


def fifth_kernel(count, slope_ref, pre_three_ref, pooled_ref, sums_three_ref, affine_three_ref,
                 grads_three_ref, late_ref, pre_two_ref, sums_two_ref, affine_two_ref,
                 low_ref, out_ref, sums_ref, natural, restore_ref, semaphore):
    copy = restore_copy(late_ref, restore_ref, semaphore)

    @pl.when(first_step())
    def _():
        copy.start()
        sums_ref[...] = jnp.zeros_like(sums_ref)

    def low_step(step, carry):
        where = lanes(step, TILE)
        mean, inverse, gain, _ = constants(
            sums_three_ref[:, where], affine_three_ref[:, where], count
        )
        scale = spread(gain * inverse)
        offset = spread(grads_three_ref[0:1, where] / count)
        along = spread(grads_three_ref[1:2, where] / count * inverse)
        mean = spread(mean)
        pooled = [view_scale(pooled_ref, view, where) for view in range(2)]
        for chunk in range(HALF // 16):
            rows = slice(chunk * 16, chunk * 16 + 16)
            grad = view_grad_rows(slope_ref[rows, where].astype(f32), pooled, chunk)
            centred = pre_three_ref[rows, where].astype(f32) - mean
            low_ref[rows, where] = (scale * (grad - offset - centred * along)).astype(bf16)
        return carry

    lax.fori_loop(0, C // TILE, low_step, 0)

    @pl.when(first_step())
    def _():
        copy.wait()

    blocks = restore_ref.reshape(8, 4, RESTORE_ROWS, B)

    def product_step(step, carry):
        grad = None
        for quarter in range(4):
            rows = blocks[pl.ds(4 * step, 4), quarter].reshape(TILE, B)
            part = dot_nt(low_ref[:, quarter * B : (quarter + 1) * B], rows)
            grad = part if grad is None else grad + part
        natural[2 * step] = grad[:, 0:LANES]
        natural[2 * step + 1] = grad[:, LANES:TILE]
        return carry

    lax.fori_loop(0, B // TILE, product_step, 0)

    def slope_step(step, carry):
        where = lanes(step, LANES)
        mean, inverse, gain, shift = (
            spread(row) for row in constants(sums_two_ref[:, where], affine_two_ref[:, where], count)
        )
        first = jnp.zeros((16, LANES), f32)
        second = jnp.zeros((16, LANES), f32)
        for cell in range(CELLS):
            rows = slice(cell * 16, cell * 16 + 16)
            unit = (pre_two_ref[rows, where] - mean) * inverse
            norm = unit * gain + shift
            sigma = sigmoid(norm)
            grad = natural[step, pl.ds(cell, 16, stride=CELLS)]
            grad = grad * (sigma * (1.0 + norm * (1.0 - sigma)))
            out_ref[rows, where] = grad
            first = first + grad
            second = second + grad * unit
        add_moments(sums_ref, where, first, second)
        return carry

    lax.fori_loop(0, 4, slope_step, 0)


def fifth_block(slope, pre_three, pooled, sums_three, affine_three, grads_three, late,
                pre_two, sums_two, affine_two, count, after=()):
    rows = slope.shape[0]
    return kernel_call(
        functools.partial(fifth_kernel, count),
        rows // HALF,
        [half_spec(C), half_spec(C), pl.BlockSpec((1, 2, C), lambda step: (step, 0, 0)),
         whole_spec(sums_three.shape), whole_spec((2, C)), whole_spec(grads_three.shape), ANY,
         half_spec(B), whole_spec(sums_two.shape), whole_spec((2, B))],
        [half_spec(C), half_spec(B), whole_out((2, B))],
        [jax.ShapeDtypeStruct((rows, C), bf16), jax.ShapeDtypeStruct((rows, B), f32),
         jax.ShapeDtypeStruct((2, B), f32)],
        [pltpu.VMEM((4, HALF, LANES), f32), pltpu.VMEM((32, RESTORE_ROWS, B), bf16),
         pltpu.SemaphoreType.DMA(())],
        2 * rows * B * C,
        2 * rows * B,
        after=after,
    )(slope, pre_three, pooled, sums_three, affine_three, grads_three, late,
      pre_two, sums_two, affine_two)


def sixth_kernel(count, me_ref, block_a, block_b, block_c, block_d, grad_ref, pre_two_ref, sums_two_ref, affine_two_ref, grads_two_ref,
                 pre_one_ref, sums_one_ref, affine_one_ref,
                 low_ref, out_ref, sums_ref, padded, shifted, tile, natural, spatial_ref,
                 semaphores):
    border = SIDE * 16
    copies = block_copies(me_ref[0], (block_a, block_b, block_c, block_d), spatial_ref, semaphores)

    @pl.when(first_step())
    def _():
        start(copies)
        sums_ref[...] = jnp.zeros_like(sums_ref)
        clear_border(padded)
        shifted[0:border] = jnp.zeros((border, 3 * B), bf16)
        shifted[border + HALF :] = jnp.zeros((border, 3 * B), bf16)

    def low_step(step, carry):
        where = lanes(step, LANES)
        mean, inverse, gain, _ = constants(sums_two_ref[:, where], affine_two_ref[:, where], count)
        scale = spread(gain * inverse)
        offset = spread(grads_two_ref[0:1, where] / count)
        along = spread(grads_two_ref[1:2, where] / count * inverse)
        mean = spread(mean)
        for cell in range(CELLS):
            rows = slice(cell * 16, cell * 16 + 16)
            centred = pre_two_ref[rows, where] - mean
            low = (scale * (grad_ref[rows, where] - offset - centred * along)).astype(bf16)
            low_ref[rows, where] = low
            padded[cell_place(cell)] = low
        for side in range(3):
            at = lanes(side * 4 + step, LANES)
            for cell in range(CELLS):
                shifted[border + cell * 16 : border + cell * 16 + 16, at] = padded[
                    tap_place(cell, 3 + side)
                ]
        return carry

    lax.fori_loop(0, 4, low_step, 0)

    @pl.when(first_step())
    def _():
        wait(copies)

    def product_step(step, carry):
        grad = None
        for tap in range(9):
            top = (tap // 3) * border
            at = (tap % 3) * B
            back = (8 - tap) * 16
            rows = spatial_ref[pl.ds(16 * step, 16), back : back + 16].reshape(TILE, B)
            part = dot_nt(shifted[top : top + HALF, at : at + B], rows)
            grad = part if grad is None else grad + part
        tile[...] = grad
        for half in range(2):
            for cell in range(CELLS):
                natural[2 * step + half, pl.ds(cell, 16, stride=CELLS)] = tile[
                    cell * 16 : cell * 16 + 16, half * LANES : (half + 1) * LANES
                ]
        return carry

    lax.fori_loop(0, B // TILE, product_step, 0)

    def slope_step(step, carry):
        where = lanes(step, LANES)
        mean, inverse, gain, shift = (
            spread(row) for row in constants(sums_one_ref[:, where], affine_one_ref[:, where], count)
        )
        first = jnp.zeros((16, LANES), f32)
        second = jnp.zeros((16, LANES), f32)
        for chunk in range(HALF // 16):
            rows = slice(chunk * 16, chunk * 16 + 16)
            unit = (pre_one_ref[rows, where] - mean) * inverse
            norm = unit * gain + shift
            sigma = sigmoid(norm)
            grad = natural[step, rows] * (sigma * (1.0 + norm * (1.0 - sigma)))
            out_ref[rows, where] = grad
            first = first + grad
            second = second + grad * unit
        add_moments(sums_ref, where, first, second)
        return carry

    lax.fori_loop(0, 4, slope_step, 0)


def sixth_block(me, spatial, grad, pre_two, sums_two, affine_two, grads_two, pre_one, sums_one,
                affine_one, count):
    rows = grad.shape[0]
    deep = HALF + 2 * SIDE * 16
    return kernel_call(
        functools.partial(sixth_kernel, count),
        rows // HALF,
        [SCALAR, ANY, ANY, ANY, ANY, half_spec(B), half_spec(B), whole_spec(sums_two.shape),
         whole_spec((2, B)), whole_spec(grads_two.shape), half_spec(B), whole_spec(sums_one.shape),
         whole_spec((2, B))],
        [half_spec(B), half_spec(B), whole_out((2, B))],
        [jax.ShapeDtypeStruct((rows, B), bf16), jax.ShapeDtypeStruct((rows, B), f32),
         jax.ShapeDtypeStruct((2, B), f32)],
        [pltpu.VMEM((PADDED * PADDED, 16, LANES), bf16), pltpu.VMEM((deep, 3 * B), bf16),
         pltpu.VMEM((HALF, TILE), f32), pltpu.VMEM((4, HALF, LANES), f32),
         pltpu.VMEM((32, SPATIAL_ROWS, B), bf16), pltpu.SemaphoreType.DMA((32,))],
        18 * rows * B * B,
        2 * rows * B,
    )(me, *spatial, grad, pre_two, sums_two, affine_two, grads_two, pre_one, sums_one,
      affine_one)


def low_kernel(count, grad_ref, pre_ref, sums_ref, affine_ref, grads_ref, low_ref):
    def low_step(step, carry):
        where = lanes(step, LANES)
        mean, inverse, gain, _ = constants(sums_ref[:, where], affine_ref[:, where], count)
        scale = spread(gain * inverse)
        offset = spread(grads_ref[0:1, where] / count)
        along = spread(grads_ref[1:2, where] / count * inverse)
        mean = spread(mean)
        for chunk in range(HALF // 16):
            rows = slice(chunk * 16, chunk * 16 + 16)
            centred = pre_ref[rows, where] - mean
            low_ref[rows, where] = (
                scale * (grad_ref[rows, where] - offset - centred * along)
            ).astype(bf16)
        return carry

    lax.fori_loop(0, 4, low_step, 0)


def low_block(grad, pre, sums, affine, grads, count):
    return kernel_call(
        functools.partial(low_kernel, count),
        grad.shape[0] // HALF,
        [half_spec(B), half_spec(B), whole_spec(sums.shape), whole_spec((2, B)),
         whole_spec(grads.shape)],
        half_spec(B),
        jax.ShapeDtypeStruct(grad.shape, bf16),
        [],
        100 * grad.size,
    )(grad, pre, sums, affine, grads)


def gate_back_kernel(me_ref, block_a, block_b, block_c, block_d, low_ref,
                     slope_ref, pooled_ref, tokens_ref, logit_ref,
                     logit_grad_ref, part_ref, tile, reduce_ref, semaphores):
    copies = reduce_copies(me_ref[0], (block_a, block_b, block_c, block_d), reduce_ref, semaphores)
    group = pl.program_id(1)

    @pl.when(very_first())
    def _():
        start(copies)
        wait(copies)

    tile[...] = dot_nt(low_ref[...], reduce_ref[pl.ds(8 * group, 8)].reshape(WIDE, B))
    pooled = [view_scale(pooled_ref, view, slice(0, WIDE)) for view in range(2)]
    for chunk in range(HALF // 16):
        rows = slice(chunk * 16, chunk * 16 + 16)
        grad = tile[rows] + view_grad_rows(slope_ref[rows].astype(f32), pooled, chunk)
        gate = sigmoid(logit_ref[rows].astype(f32))
        token = tokens_ref[rows].astype(f32)
        part = grad * gate
        part_ref[rows] = (grad + part).astype(bf16)
        logit_grad_ref[rows] = (part * (1.0 - gate) * token).astype(bf16)


def gate_back_block(me, pair, low_one, slope, pooled, tokens, logit):
    rows = low_one.shape[0]
    return kernel_call(
        gate_back_kernel,
        (rows // HALF, GROUPS),
        [SCALAR, ANY, ANY, ANY, ANY, half_spec(B), group_spec(), view_spec(2),
         group_spec(), group_spec()],
        [group_spec(), group_spec()],
        [jax.ShapeDtypeStruct((rows, C), bf16), jax.ShapeDtypeStruct((rows, C), bf16)],
        [pltpu.VMEM((HALF, WIDE), f32), pltpu.VMEM((32, C // 32, B), bf16),
         pltpu.SemaphoreType.DMA((32,))],
        2 * rows * C * R,
        2 * rows * C,
    )(me, *pair, low_one, slope, pooled, tokens, logit)


def mixing_back_kernel(me_ref, block_a, block_b, block_c, block_d, logit_grad_ref,
                       upcoming_ref, differ_ref, next_ref, scale_ref, squeezed_ref, kernels_ref,
                       natural, later, ahead, padded, expand_ref, semaphores):
    @pl.when(first_step())
    def _():
        copies = expand_copies(
            me_ref[0], (block_a, block_b, block_c, block_d), expand_ref, semaphores
        )
        start(copies)
        kernels_ref[...] = jnp.zeros_like(kernels_ref)
        clear_border(ahead)
        clear_border(padded)
        later[0:CELLS] = jnp.zeros((CELLS, LANES), f32)
        wait(copies)

    quarters = expand_ref.reshape(8, 4, R // 4, TILE)

    def mixed_step(step, carry):
        grad = None
        for block in range(C // TILE):
            at = slice(block * TILE, (block + 1) * TILE)
            rows = quarters[block, pl.ds(2 * step, 2)].reshape(TILE, TILE)
            part = dot_nt(logit_grad_ref[:, at], rows)
            grad = part if grad is None else grad + part
        natural[2 * step] = grad[:, 0:LANES]
        natural[2 * step + 1] = grad[:, LANES:TILE]
        return carry

    lax.fori_loop(0, R // TILE, mixed_step, 0)
    segment = lax.broadcasted_iota(jnp.int32, (16, LANES), 0) % SEG
    not_last = (segment != SEG - 1).astype(f32)

    def mixing_step(step, carry):
        where = lanes(step, LANES)
        scale_rows = [spread(scale_ref[tap : tap + 1, where]) for tap in range(9)]
        mean = jnp.zeros((16, LANES), f32)
        for cell in range(CELLS):
            grad = natural[step, pl.ds(cell, 16, stride=CELLS)]
            padded[cell_place(cell)] = grad
            mean = mean + grad
            ahead[cell_place(cell)] = differ_ref[cell * 16 : cell * 16 + 16, where]
        mean = mean * (1.0 / CELLS)
        sums = [jnp.zeros((16, LANES), f32) for _ in range(9)]
        for cell in range(CELLS):
            grad = padded[cell_place(cell)]
            for tap in range(9):
                sums[tap] = sums[tap] + ahead[tap_place(cell, tap)] * grad
        for tap in range(9):
            kernels_ref[9 + tap : 10 + tap, where] += jnp.sum(sums[tap], 0, keepdims=True)
        for cell in range(CELLS):
            grad = padded[cell_place(cell)] + mean
            for tap in range(9):
                grad = grad + padded[tap_place(cell, tap)] * scale_rows[8 - tap]
            ahead[cell_place(cell)] = grad
        next_rows = [spread(next_ref[tap : tap + 1, where]) for tap in range(9)]
        for cell in range(CELLS):
            padded[cell_place(cell)] = upcoming_ref[cell * 16 : cell * 16 + 16, where]
        sums = [jnp.zeros((16, LANES), f32) for _ in range(9)]
        for cell in range(CELLS):
            grad = ahead[cell_place(cell)]
            for tap in range(9):
                sums[tap] = sums[tap] + padded[tap_place(cell, tap)] * grad
        for tap in range(9):
            kernels_ref[tap : tap + 1, where] += jnp.sum(sums[tap], 0, keepdims=True)
        for cell in range(CELLS):
            back = ahead[tap_place(cell, 0)] * next_rows[8]
            for tap in range(1, 9):
                back = back + ahead[tap_place(cell, tap)] * next_rows[8 - tap]
            later[pl.ds(cell + CELLS, 16, stride=CELLS)] = back * not_last
            natural[step, pl.ds(cell, 16, stride=CELLS)] = -ahead[cell_place(cell)]
        for chunk in range(HALF // 16):
            rows = slice(chunk * 16, chunk * 16 + 16)
            squeezed_ref[rows, where] = (natural[step, rows] + later[rows]).astype(bf16)
        return carry

    lax.fori_loop(0, 4, mixing_step, 0)


def mixing_back_block(me, pair, logit_grad, upcoming, differ, next_kernel, scale_kernel,
                      after=()):
    rows = logit_grad.shape[0]
    return kernel_call(
        mixing_back_kernel,
        rows // HALF,
        [SCALAR, ANY, ANY, ANY, ANY, half_spec(C), half_spec(R), half_spec(R),
         whole_spec((9, R)), whole_spec((9, R))],
        [half_spec(R), whole_out((18, R))],
        [jax.ShapeDtypeStruct((rows, R), bf16), jax.ShapeDtypeStruct((18, R), f32)],
        [pltpu.VMEM((4, HALF, LANES), f32), pltpu.VMEM((HALF + CELLS + 7, LANES), f32),
         pltpu.VMEM((PADDED * PADDED, 16, LANES), f32),
         pltpu.VMEM((PADDED * PADDED, 16, LANES), f32), pltpu.VMEM((32, R // 4, TILE), bf16),
         pltpu.SemaphoreType.DMA((2, 32))],
        2 * rows * C * R,
        after=after,
    )(me, *pair, logit_grad, upcoming, differ, next_kernel, scale_kernel)


def tokens_kernel(me_ref, block_a, block_b, block_c, block_d, part_ref, squeezed_ref, out_ref,
                  tile, squeeze_ref, semaphores):
    @pl.when(very_first())
    def _():
        copies = block_copies(
            me_ref[0], (block_a, block_b, block_c, block_d), squeeze_ref, semaphores, slice(0, 64)
        )
        start(copies)
        wait(copies)

    tile[...] = dot_nt(
        squeezed_ref[...], squeeze_ref[pl.ds(8 * pl.program_id(1), 8)].reshape(WIDE, R)
    )
    for chunk in range(HALF // 16):
        rows = slice(chunk * 16, chunk * 16 + 16)
        out_ref[rows] = (tile[rows] + part_ref[rows].astype(f32)).astype(bf16)


def tokens_block(me, squeeze, part, squeezed_grad):
    rows = part.shape[0]
    return kernel_call(
        tokens_kernel,
        (rows // HALF, GROUPS),
        [SCALAR, ANY, ANY, ANY, ANY, group_spec(), half_spec(R)],
        group_spec(),
        jax.ShapeDtypeStruct((rows, C), bf16),
        [pltpu.VMEM((HALF, WIDE), f32), pltpu.VMEM((32, C // 32, R), bf16),
         pltpu.SemaphoreType.DMA((32,))],
        2 * rows * C * R,
    )(me, *squeeze, part, squeezed_grad)


def turn(me, values, grain, plain, turned):
    core = me & 1
    plain[...] = values.T
    half = turned.shape[0] // 2
    for group in range(half // grain):
        mine = pl.multiple_of((2 * group + core) * grain, grain)
        other = pl.multiple_of((2 * group + 1 - core) * grain, grain)
        turned[group * grain : (group + 1) * grain] = plain[pl.ds(mine, grain)]
        turned[half + group * grain : half + (group + 1) * grain] = plain[pl.ds(other, grain)]


def store_tiles(found, keep_ref, send_ref):
    half = found.shape[0] // 2
    for tile in range(2):
        at = slice(tile * TILE, (tile + 1) * TILE)
        keep_ref[tile, 0:half] = found[0:half, at]
        send_ref[tile, 0:half] = found[half:, at].astype(bf16)


def outer_kernel(grain, me_ref, narrow_ref, wide_ref, keep_ref, send_ref, plain, turned):
    @pl.when(first_step())
    def _():
        turn(me_ref[0], narrow_ref[...], grain, plain, turned)

    store_tiles(product(turned[...], wide_ref[...]), keep_ref, send_ref)


def outer_block(me, narrow_values, wide_values, grain):
    rows, inner = narrow_values.shape
    blocks = wide_values.shape[1] // TILE
    half = pl.BlockSpec((2, inner // 2, TILE), lambda step: (step, 0, 0))
    return kernel_call(
        functools.partial(outer_kernel, grain),
        blocks // 2,
        [SCALAR, whole_spec((rows, inner)), pl.BlockSpec((rows, 2 * TILE), lambda step: (0, step))],
        [half, half],
        [jax.ShapeDtypeStruct((blocks, inner // 2, TILE), f32),
         jax.ShapeDtypeStruct((blocks, inner // 2, TILE), bf16)],
        [pltpu.VMEM((inner, rows), bf16), pltpu.VMEM((inner, rows), bf16)],
        2 * rows * inner * wide_values.shape[1],
    )(me, narrow_values, wide_values)


def outer_block_of(grain):
    return functools.partial(outer_block, grain=grain)


FEW_ROWS = 40


def restore_outer_kernel(narrow_ref, wide_ref, out_ref, turned):
    @pl.when(first_step())
    def _():
        turned[...] = narrow_ref[...].T

    found = product(turned[...], wide_ref[...])
    out_ref[:, 0] = found.astype(bf16).reshape(8, RESTORE_ROWS, WIDE)


def restore_outer_block(hidden, low_three):
    rows = hidden.shape[0]
    return kernel_call(
        restore_outer_kernel,
        GROUPS,
        [whole_spec((rows, B)), pl.BlockSpec((rows, WIDE), lambda step: (0, step))],
        pl.BlockSpec((8, 1, RESTORE_ROWS, WIDE), lambda step: (0, step, 0, 0)),
        jax.ShapeDtypeStruct((8, 4, RESTORE_ROWS + SPATIAL_ROWS, WIDE), bf16),
        [pltpu.VMEM((B, rows), bf16)],
        2 * rows * B * C,
    )(hidden, low_three)


def spatial_kernel(buffer_ref, hidden_ref, low_ref, out_ref, turned, padded):
    border = SIDE * 16
    halves = hidden_ref.shape[0]

    @pl.when(first_step())
    def _():
        for half in range(halves):
            padded[half, 0 : 2 * border] = jnp.zeros((2 * border, B), bf16)
            padded[half, 2 * border : 2 * border + HALF] = low_ref[half * HALF : (half + 1) * HALF]
            padded[half, 2 * border + HALF :] = jnp.zeros((2 * border, B), bf16)

    step = pl.program_id(0)

    @pl.when(step % 3 == 0)
    def _():
        for half in range(halves):
            turned[half] = hidden_ref[half].T

    top = pl.multiple_of((2 - step % 3) * border, 16)
    found = None
    for half in range(halves):
        part = product(turned[half], padded[half, pl.ds(top, HALF + 2 * border)])
        found = part if found is None else found + part
    out_ref[...] = found.astype(bf16).reshape(32, 16, B)


def spatial_block(buffer, hidden, low_two):
    halves, deep, _ = hidden.shape
    first = RESTORE_ROWS // 16
    return kernel_call(
        spatial_kernel,
        9,
        [ANY, pl.BlockSpec((halves, deep, B), lambda step: (0, 0, step // 3)),
         whole_spec(low_two.shape)],
        pl.BlockSpec((32, 16, B), lambda step: (0, first + (step % 3) * 3 + step // 3, 0)),
        jax.ShapeDtypeStruct(buffer.shape, bf16),
        [pltpu.VMEM((halves, B, deep), bf16),
         pltpu.VMEM((halves, deep + 2 * SIDE * 16, B), bf16)],
        18 * low_two.shape[0] * B * B,
        aliases={0: 0},
    )(buffer, hidden, low_two)


STEM = 64
STEM_SIDE = 16
CHANNELS = 12
SLABS = 19
STEM_LANES = STEM_SIDE * STEM
INPUT_LANES = CHANNELS * 2 * STEM_SIDE
WINDOW = 7


def frames_kernel(frames_ref, out_ref, rows):
    segments = frames_ref.shape[0]
    side = 2 * STEM_SIDE

    def segment_step(segment, carry):
        pieces = [
            frames_ref[segment, index + 1, colour].astype(f32)
            - frames_ref[segment, index, colour].astype(f32)
            for index in range(4)
            for colour in range(3)
        ]
        for group in range(3):
            rows[group, pl.ds(segment, side, stride=segments)] = jnp.concatenate(
                pieces[4 * group : 4 * group + 4], axis=1
            )
        return carry

    lax.fori_loop(0, segments, segment_step, 0)
    empty = jnp.zeros((segments, INPUT_LANES), bf16)
    for parity in range(2):
        for slab in (0, 1, SLABS - 1):
            out_ref[parity, slab] = empty
    for row in range(side):
        for group in range(3):
            out_ref[row % 2, row // 2 + 2, :, group * LANES : (group + 1) * LANES] = rows[
                group, row * segments : (row + 1) * segments
            ].astype(bf16)


def frames_block(frames):
    segments = frames.shape[0] * frames.shape[1]
    ordered = frames.transpose(0, 1, 2, 5, 3, 4).reshape(
        (segments, frames.shape[2], 3) + frames.shape[3:5]
    )
    shape = (2, SLABS, segments, INPUT_LANES)
    return kernel_call(
        frames_kernel,
        1,
        [whole_spec(ordered.shape)],
        whole_out(shape),
        jax.ShapeDtypeStruct(shape, bf16),
        [pltpu.VMEM((3, 2 * STEM_SIDE * segments, LANES), f32)],
        ordered.size * 100,
    )(ordered)


def stem_rows(input_ref, offset):
    parity = 1 - offset % 2
    top = (offset - 3) // 2 + 2 if parity == 0 else (offset - 4) // 2 + 2
    found = input_ref[parity, top : top + STEM_SIDE]
    return found.reshape(-1, INPUT_LANES)


def band_select():
    shape = (STEM_SIDE // 2, CHANNELS, 2 * STEM_SIDE, 2, LANES)
    pair, channel, place, which, entry = (
        lax.broadcasted_iota(jnp.int32, shape, axis) for axis in range(5)
    )
    met = (entry % CHANNELS == channel) & (entry < WINDOW * CHANNELS)
    met = met & (place == 2 * (2 * pair + which) + entry // CHANNELS - 3)
    return met.astype(bf16).reshape(STEM_SIDE // 2, INPUT_LANES, 2 * LANES)


def pair_weights(stem_weight):
    rows = stem_weight.reshape(WINDOW, WINDOW * CHANNELS, STEM)
    rows = jnp.pad(rows, ((0, 0), (0, LANES - WINDOW * CHANNELS), (0, 0)))
    none = jnp.zeros_like(rows)
    return jnp.concatenate(
        [jnp.concatenate([rows, none], 2), jnp.concatenate([none, rows], 2)], 1
    )


def stem_kernel(input_ref, select_ref, weights_ref, pre_ref, sums_ref, bands):
    def step_body(step, carry):
        where = lanes(step, TILE)
        for offset in range(WINDOW):
            for which in range(2):
                band = product(select_ref[2 * step + which], weights_ref[offset])
                bands[offset, :, which * LANES : (which + 1) * LANES] = band.astype(bf16)
        found = None
        for offset in range(WINDOW):
            part = product(stem_rows(input_ref, offset), bands[offset])
            found = part if found is None else found + part
        pre_ref[:, where] = found
        sums_ref[0:1, where] = jnp.sum(found, 0, keepdims=True)
        sums_ref[1:2, where] = jnp.sum(found * found, 0, keepdims=True)
        return carry

    lax.fori_loop(0, STEM_LANES // TILE, step_body, 0)


def stem_block(inputs, select, weights, after=()):
    rows = inputs.shape[2] * STEM_SIDE
    return kernel_call(
        stem_kernel,
        1,
        [whole_spec(inputs.shape), whole_spec(select.shape), whole_spec(weights.shape)],
        [whole_out((rows, STEM_LANES)), whole_out((2, STEM_LANES))],
        [jax.ShapeDtypeStruct((rows, STEM_LANES), f32),
         jax.ShapeDtypeStruct((2, STEM_LANES), f32)],
        [pltpu.VMEM((WINDOW, INPUT_LANES, TILE), bf16)],
        2 * WINDOW * rows * INPUT_LANES * STEM_LANES,
        after=after,
    )(inputs, select, weights)


def stem_norm_kernel(count, pre_ref, in_sums_ref, affine_ref, cotangent_ref,
                     out_ref, grad_ref, sums_ref):
    def step_body(step, carry):
        where = lanes(step, LANES)
        mean, inverse, gain, shift = (
            spread(row) for row in constants(in_sums_ref[:, where], affine_ref[:, where], count)
        )
        first = jnp.zeros((16, LANES), f32)
        second = jnp.zeros((16, LANES), f32)
        for chunk in range(pre_ref.shape[0] // 16):
            rows = slice(chunk * 16, chunk * 16 + 16)
            unit = (pre_ref[rows, where] - mean) * inverse
            norm = unit * gain + shift
            sigma = sigmoid(norm)
            output = norm * sigma
            out_ref[rows, where] = output.astype(bf16)
            grad = cotangent_ref[rows, where].astype(f32) * (sigma + output * (1.0 - sigma))
            grad_ref[rows, where] = grad
            first = first + grad
            second = second + grad * unit
        sums_ref[0:1, where] = jnp.sum(first, 0, keepdims=True)
        sums_ref[1:2, where] = jnp.sum(second, 0, keepdims=True)
        return carry

    lax.fori_loop(0, STEM_LANES // LANES, step_body, 0)


def stem_norm_block(pre, sums, affine, cotangent, count, after=()):
    shape = pre.shape
    return kernel_call(
        functools.partial(stem_norm_kernel, count),
        1,
        [whole_spec(shape), whole_spec(sums.shape), whole_spec(affine.shape), whole_spec(shape)],
        [whole_out(shape), whole_out(shape), whole_out((2, STEM_LANES))],
        [jax.ShapeDtypeStruct(shape, bf16), jax.ShapeDtypeStruct(shape, f32),
         jax.ShapeDtypeStruct((2, STEM_LANES), f32)],
        [],
        4000 * pre.size,
        after=after,
    )(pre, sums, affine, cotangent)


def stem_back_kernel(count, input_ref, select_ref, pre_ref, in_sums_ref, affine_ref, grad_ref,
                     grads_ref, out_ref, low, turned):
    def low_step(step, carry):
        where = lanes(step, LANES)
        mean, inverse, gain, _ = constants(in_sums_ref[:, where], affine_ref[:, where], count)
        scale = spread(gain * inverse)
        offset = spread(grads_ref[0:1, where] / count)
        along = spread(grads_ref[1:2, where] / count * inverse)
        mean = spread(mean)
        for chunk in range(pre_ref.shape[0] // 16):
            rows = slice(chunk * 16, chunk * 16 + 16)
            centred = pre_ref[rows, where] - mean
            low[rows, where] = (
                scale * (grad_ref[rows, where] - offset - centred * along)
            ).astype(bf16)
        return carry

    lax.fori_loop(0, STEM_LANES // LANES, low_step, 0)
    out_ref[...] = jnp.zeros_like(out_ref)

    for offset in range(WINDOW):
        turned[offset] = stem_rows(input_ref, offset).T

    def step_body(step, carry):
        where = lanes(step, TILE)
        for offset in range(WINDOW):
            band = product(turned[offset], low[:, where]).astype(bf16)
            found = product(select_ref[2 * step], band[:, 0:LANES]) + product(
                select_ref[2 * step + 1], band[:, LANES:TILE]
            )
            out_ref[offset] += found
        return carry

    lax.fori_loop(0, STEM_LANES // TILE, step_body, 0)


def stem_back_block(inputs, select, pre, sums, affine, grad, grads, count, after=()):
    shape = pre.shape
    out = (WINDOW, 2 * LANES, LANES)
    return kernel_call(
        functools.partial(stem_back_kernel, count),
        1,
        [whole_spec(inputs.shape), whole_spec(select.shape), whole_spec(shape),
         whole_spec(sums.shape), whole_spec(affine.shape), whole_spec(shape),
         whole_spec(grads.shape)],
        whole_out(out),
        jax.ShapeDtypeStruct(out, f32),
        [pltpu.VMEM(shape, bf16), pltpu.VMEM((WINDOW, INPUT_LANES, shape[0]), bf16)],
        2 * WINDOW * shape[0] * INPUT_LANES * STEM_LANES,
        after=after,
    )(inputs, select, pre, sums, affine, grad, grads)


SMALL_ROWS = 32
FIRST_ROWS = 64 + SMALL_ROWS


def cut_kernel(me_ref, squeeze_ref, expand_ref, reduce_ref, spatial_ref, restore_ref, class_ref,
               stem_ref, next_ref, scale_ref, outer_ref, gain_one_ref, shift_one_ref,
               gain_two_ref, shift_two_ref, stem_gain_ref, stem_shift_ref,
               first_out, pair_out, spatial_out, late_out, small):
    part = me_ref[0] & 3
    first_out[0:64] = squeeze_ref[pl.ds(pl.multiple_of(part * 64, 64), 64)]
    small[...] = jnp.zeros_like(small)
    edge = stem_ref.shape[1] - B
    small[0:8] = stem_ref[:, 0:B].astype(f32)
    small[8:16, 0:edge] = stem_ref[:, B:].astype(f32)
    small[16:25, 0 : next_ref.shape[1]] = next_ref[...].astype(f32)
    small[16:25, LANES : LANES + scale_ref.shape[1]] = scale_ref[...].astype(f32)
    small[25:26] = outer_ref[...].astype(f32)
    for place, ref in enumerate((gain_one_ref, shift_one_ref, gain_two_ref, shift_two_ref)):
        small[26:27, place * LANES : place * LANES + ref.shape[1]] = ref[...].astype(f32)
    small[27:28, 0 : stem_gain_ref.shape[1]] = stem_gain_ref[...].astype(f32)
    small[27:28, LANES : LANES + stem_shift_ref.shape[1]] = stem_shift_ref[...].astype(f32)
    first_out[64:] = small[...].astype(bf16)
    pair_out[0:PAIR_ROWS] = reduce_ref[pl.ds(pl.multiple_of(part * 64, 64), 64)]
    for half in range(2):
        pair_out[PAIR_ROWS:, half * TILE : (half + 1) * TILE] = expand_ref[
            pl.ds(pl.multiple_of(part * 128 + half * 64, 64), 64)
        ]
    for tap in range(9):
        spatial_out[tap * 16 : tap * 16 + 16] = spatial_ref[
            tap, pl.ds(pl.multiple_of(part * 16, 16), 16)
        ]
    late_out[0:RESTORE_ROWS] = restore_ref[:, pl.ds(pl.multiple_of(part * B, B), B)]
    for half in range(2):
        rows = pl.ds(pl.multiple_of(part * 64 + half * 32, 32), 32)
        late_out[RESTORE_ROWS:, half * TILE : (half + 1) * TILE] = class_ref[rows]


def cut_block(me, *weights):
    shapes = [(FIRST_ROWS, B), (2 * PAIR_ROWS, B), (SPATIAL_ROWS, B), (LATE_ROWS, B)]
    return kernel_call(
        cut_kernel,
        1,
        [SCALAR] + [whole_spec(weight.shape) for weight in weights],
        [whole_out(shape) for shape in shapes],
        [jax.ShapeDtypeStruct(shape, bf16) for shape in shapes],
        [pltpu.VMEM((SMALL_ROWS, B), f32)],
        1000000,
    )(me, *weights)


def unpack_kernel(me_ref, first_ref, weights_out, next_out, scale_out, one_out, two_out,
                  three_out, stem_out):
    wide = first_ref.shape[0]
    small = []
    for index in range(wide):
        mask = (me_ref[0] >> 2) ^ index
        entry = (mask & 1) * 4 + (mask >> 1)
        small.append(first_ref[entry, 64:].astype(f32))

    def joined(row, at, width, rows=1):
        return jnp.concatenate(
            [values[row : row + rows, at : at + width] for values in small], axis=1
        )

    own = B // wide
    next_out[...] = joined(16, 0, own, 9)
    scale_out[...] = joined(16, LANES, own, 9)
    one_out[0:1] = joined(26, 0, own)
    one_out[1:2] = joined(26, LANES, own)
    two_out[0:1] = joined(26, 2 * LANES, own)
    two_out[1:2] = joined(26, 3 * LANES, own)
    three_out[0:1] = joined(25, 0, TILE)
    three_out[1:2] = joined(25, TILE, TILE)
    for row in range(2):
        stem = joined(27, row * LANES, STEM // wide)
        stem_out[row : row + 1] = jnp.concatenate([stem] * STEM_SIDE, axis=1)
    columns = jnp.concatenate(
        [jnp.concatenate([values[0:8], values[8:16, 0:LANES]], axis=1) for values in small], axis=0
    )
    rows = columns.T
    place = lax.broadcasted_iota(jnp.int32, (LANES, STEM), 0)
    none = jnp.zeros((LANES, STEM), f32)
    for offset in range(WINDOW):
        top = offset * WINDOW * CHANNELS
        block = jnp.where(place < WINDOW * CHANNELS, rows[top : top + LANES], 0.0)
        weights_out[offset, 0:LANES] = jnp.concatenate([block, none], axis=1).astype(bf16)
        weights_out[offset, LANES:] = jnp.concatenate([none, block], axis=1).astype(bf16)


def unpack_block(me, first):
    shapes = [
        ((WINDOW, 2 * LANES, LANES), bf16), ((9, R), f32), ((9, R), f32), ((2, B), f32),
        ((2, B), f32), ((2, C), f32), ((2, STEM_LANES), f32),
    ]
    return kernel_call(
        unpack_kernel,
        1,
        [SCALAR, whole_spec(first.shape)],
        [whole_out(shape) for shape, _ in shapes],
        [jax.ShapeDtypeStruct(shape, kind) for shape, kind in shapes],
        [],
        1000000,
    )(me, first)


def shards(
    frames,
    tokens,
    stem_cotangent,
    crop_counts,
    labels,
    stem_weight,
    stem_gain,
    stem_shift,
    w_squeeze,
    next_kernel,
    scale_kernel,
    w_expand,
    w_reduce,
    gain_one,
    shift_one,
    w_spatial,
    gain_two,
    shift_two,
    w_restore,
    gain_three,
    shift_three,
    w_class,
    class_bias,
):
    view_count = frames.shape[0]
    row_count = tokens.shape[0]
    devices = lax.axis_size(AXES)
    wide = lax.axis_size("wide")
    narrow = lax.axis_size("narrow")
    count = float(row_count * devices)
    segments = view_count * SEG
    stem_rows_here = segments * STEM_SIDE
    stem_count = float(stem_rows_here * STEM_SIDE * devices)
    direct = wide == C // TILE and narrow == 4
    me = lax.axis_index(AXES)
    me_array = (me if direct else 0 * me).astype(jnp.int32).reshape(1)

    stem_width = stem_weight.shape[1]
    inner_width = gain_one.shape[0]
    outer_width = gain_three.shape[0]
    select = band_select()
    cotangent = stem_cotangent.reshape(segments, STEM_SIDE, STEM_LANES)
    cotangent = cotangent.transpose(1, 0, 2).reshape(stem_rows_here, STEM_LANES)
    if direct:
        first_own, pair_own, spatial_own, late_own = cut_block(
            me_array, w_squeeze, w_expand, w_reduce, w_spatial, w_restore,
            jnp.pad(w_class, ((0, 0), (0, TILE - CLASSES))), stem_weight.T, next_kernel,
            scale_kernel, jnp.concatenate([gain_three, shift_three])[None], gain_one[None],
            shift_one[None], gain_two[None], shift_two[None], stem_gain[None], stem_shift[None],
        )
        firsts, pairs, spatials = Gather(first_own), Gather(pair_own), Gather(spatial_own)
        (cotangent, select), came, _ = beside(
            lambda grads, band: (grads, band), [cotangent, select], firsts.depth()
        )
        firsts.take_depth(came)
        inputs, came, _ = beside(frames_block, [frames], firsts.second() + pairs.depth())
        firsts.take_second(came[:1])
        pairs.take_depth(came[1:])
        squeeze_own = firsts.eight[:, 0:64]
        (
            weights, full_next, full_scale, affine_one, affine_two, affine_three, stem_affine,
        ) = unpack_block(me_array, firsts.eight)
        (stem_pre, stem_part), came, _ = beside(
            stem_block, [inputs, select, weights],
            [(squeeze_own, 2)] + pairs.second() + spatials.depth(),
        )
        squeeze_far = came[0]
        pairs.take_second(came[1:2])
        spatials.take_depth(came[2:])
        stem_pre, came, _ = beside(
            lambda values: values, [stem_pre], [(squeeze_own, 1), (squeeze_far, 1)]
        )
        squeeze = (squeeze_own, squeeze_far) + tuple(came)
    else:
        squeeze, pair, spatial, late = gathered(
            w_squeeze, w_expand, w_reduce, w_spatial, w_restore, w_class
        )

        def whole(values):
            return lax.all_gather(values, "wide", axis=values.ndim - 1, tiled=True).astype(f32)

        weights = pair_weights(whole(stem_weight).astype(bf16))
        full_next, full_scale = whole(next_kernel), whole(scale_kernel)
        affine_one = jnp.stack([whole(gain_one), whole(shift_one)])
        affine_two = jnp.stack([whole(gain_two), whole(shift_two)])
        affine_three = jnp.stack([whole(gain_three), whole(shift_three)])
        stem_affine = jnp.tile(jnp.stack([whole(stem_gain), whole(stem_shift)]), (1, STEM_SIDE))
        inputs = frames_block(frames)
        stem_pre, stem_part = stem_block(inputs, select, weights)
    stem_part = stem_part.reshape(2, STEM_SIDE, STEM).sum(1).reshape(1, 2 * STEM)

    def stem_lanes(sums):
        return jnp.tile(sums[2, : 2 * STEM].reshape(2, STEM), (1, STEM_SIDE))

    def with_row(sums, row):
        return jnp.concatenate([sums, jnp.pad(row, ((0, 0), (0, sums.shape[1] - row.shape[1])))])

    mixing_operands = [me_array, squeeze, tokens, full_next, full_scale]
    if direct:
        (upcoming, differ, mixed_low), came, _ = beside(
            mixing_block, mixing_operands, pairs.third() + spatials.second()
        )
        pairs.take_third(came[:1])
        spatials.take_second(came[1:])
        (mixed_low, late_own), came, _ = beside(
            lambda values, mine: (values, mine), [mixed_low, late_own], pairs.core()
        )
        pairs.take_core(came)
        late = lax.all_gather(late_own, AXES)
        pair = pairs.arrays
    else:
        upcoming, differ, mixed_low = mixing_block(*mixing_operands)
    gate_operands = [me_array, pair, tokens, mixed_low]
    if direct:
        (logit, gated_low, pre_one, one_part), came, _ = beside(
            gate_block, gate_operands, spatials.third()
        )
        spatials.take_third(came)
        one_sums, came, _ = beside(swap_total, [with_row(one_part, stem_part)], spatials.core())
        spatials.take_core(came)
        spatial = spatials.arrays
    else:
        logit, gated_low, pre_one, one_part = gate_block(*gate_operands)
        one_sums = swap_total(with_row(one_part, stem_part))
    stem_sums = stem_lanes(one_sums)
    hidden_one, pre_two, two_part = second_block(
        me_array, spatial, pre_one, one_sums, affine_one, count
    )
    stem_out, stem_norm_grad, stem_part = stem_norm_block(
        stem_pre, stem_sums, stem_affine, cotangent, stem_count
    )
    stem_part = stem_part.reshape(2, STEM_SIDE, STEM).sum(1).reshape(1, 2 * STEM)
    two_sums = swap_total(two_part)
    hidden_two, pre_three, three_part = third_block(pre_two, two_sums, affine_two, late, count)
    three_sums = total(with_row(three_part, stem_part))
    stem_grads = stem_lanes(three_sums)
    activations, slope, view_sums = fourth_block(
        pre_three, gated_low, three_sums, affine_three, count
    )
    stem_features = stem_out.reshape(STEM_SIDE, segments, STEM_LANES)
    stem_features = stem_features.transpose(1, 0, 2).reshape(-1, STEM)

    def of_views(kind):
        return view_sums[:, 2 * kind : 2 * kind + 2].reshape(view_count, C)

    pooled_low = (of_views(0) / PER_VIEW).astype(bf16)

    full_class = late[:, RESTORE_ROWS:].reshape(32, CLASS_ROWS, 2, TILE)
    full_class = full_class.transpose(0, 2, 1, 3).reshape(C, TILE)[:, :CLASSES]
    view_logits = product(pooled_low, full_class) + class_bias.astype(f32)

    ends = jnp.cumsum(crop_counts)
    starts = ends - crop_counts
    positions = (me - 1) * view_count + jnp.arange(3 * view_count, dtype=jnp.int32)
    video = jnp.sum((ends[None, :] <= positions[:, None]).astype(jnp.int32), 1)
    own_video = video[view_count : 2 * view_count]
    belongs = (
        own_video[:, None] == jnp.arange(crop_counts.shape[0], dtype=jnp.int32)[None, :]
    ).astype(jnp.int32)
    own_count = jnp.sum(belongs * crop_counts[None, :], 1).astype(f32)
    own_label = jnp.sum(belongs * labels[None, :], 1)
    own_start = jnp.sum(belongs * starts[None, :], 1)
    first = (own_start == positions[view_count : 2 * view_count]).astype(f32)
    same = (own_video[:, None] == video[None, :]).astype(f32) / own_count[:, None]
    target = (own_label[:, None] == jnp.arange(CLASSES, dtype=jnp.int32)[None, :]).astype(f32)

    before = lax.ppermute(view_logits, AXES, [(i, i + 1) for i in range(devices - 1)])
    following = lax.ppermute(view_logits, AXES, [(i + 1, i) for i in range(devices - 1)])
    near = jnp.concatenate([before, view_logits, following])
    video_logits = jnp.sum(same[:, :, None] * near[None, :, :], 1)
    log_probs = jax.nn.log_softmax(video_logits, axis=-1)
    entropy_part = jnp.sum(first * -jnp.sum(target * log_probs, axis=-1))
    video_grad = loss_scale * (jnp.exp(log_probs) - target)
    bias_part = jnp.sum(first[:, None] * video_grad, 0)
    view_grad_low = (video_grad / own_count[:, None]).astype(bf16)

    factors = jnp.concatenate(
        [pooled_low, jnp.pad(view_grad_low, ((0, 0), (0, TILE - CLASSES)))], axis=1
    )
    factors = jnp.pad(factors, ((0, -view_count % 8), (0, 0)))

    pooled_grad = product_right(view_grad_low, full_class) / PER_VIEW
    part_row = jnp.concatenate([bias_part, entropy_part[None]])[None]
    three_part = jnp.stack([jnp.sum(pooled_grad * of_views(kind), 0) for kind in (1, 2)])
    three_grads = total(with_row(three_part, part_row))
    class_bias_grad = three_grads[2, :CLASSES]
    loss = three_grads[2, CLASSES] / crop_counts.shape[0]
    pooled_grad = pooled_grad.reshape(-1, 2, C)

    fifth_operands = [
        slope, pre_three, pooled_grad, three_sums, affine_three, three_grads, late,
        pre_two, two_sums, affine_two,
    ]
    run_fifth = functools.partial(fifth_block, count=count)
    run_sixth = functools.partial(sixth_block, count=count)
    run_stem_back = functools.partial(stem_back_block, count=stem_count)

    def stem_back_operands():
        return [inputs, select.swapaxes(1, 2), stem_pre, stem_sums, stem_affine, stem_norm_grad, stem_grads]
    run_low = functools.partial(low_block, count=count)
    run_outer = outer_block_of(R // 4)

    def sixth_operands():
        return [
            me_array, spatial, norm_two_grad, pre_two, two_sums, affine_two, two_grads, pre_one,
            one_sums, affine_one,
        ]

    def low_operands():
        return [norm_one_grad, pre_one, one_sums, affine_one, one_grads]

    def gate_back_operands():
        return [me_array, pair, low_one, slope, pooled_grad, tokens, logit]

    def mixing_back_operands():
        return [me_array, pair, logit_grad, upcoming, differ, full_next, full_scale]

    def few_of(stem_back, kernel_grads):
        stem_back = stem_back[:, :LANES, :STEM] + stem_back[:, LANES:, STEM:]
        stem_grad = stem_back[:, : WINDOW * CHANNELS].reshape(-1, STEM)
        stem_cut = stem_grad.T.reshape(8, 8, -1)
        stem_cut = jnp.pad(stem_cut, ((0, 0), (0, 0), (0, 3 * TILE - stem_cut.shape[2])))
        kernel_cut = kernel_grads.reshape(2, 9, 8, R // 8).transpose(2, 1, 0, 3)
        kernel_cut = jnp.pad(kernel_cut, ((0, 0), (0, 0), (0, 0), (0, LANES - R // 8)))
        few = jnp.concatenate([stem_cut.reshape(8, 24, TILE), kernel_cut.reshape(8, 9, TILE)], 1)
        return jnp.pad(few, ((0, 0), (0, FEW_ROWS - few.shape[1]), (0, 0)))

    if direct:
        views = Gather(factors)
        (low_three, norm_two_grad, two_part), came, _ = beside(
            run_fifth, fifth_operands, views.depth()
        )
        views.take_depth(came)
        (buffer, two_grads), came, _ = beside(
            lambda hidden, low, part: (restore_outer_block(hidden, low), swap_total(part)),
            [hidden_two, low_three, two_part], views.second(),
        )
        views.take_second(came)
        (low_two, norm_one_grad, one_part), came, _ = beside(
            run_sixth, sixth_operands(), views.third()
        )
        views.take_third(came)
        (buffer, one_grads), came, _ = beside(
            lambda values, hidden, low, part: (
                spatial_block(values.reshape(32, -1, WIDE), hidden, low), swap_total(part)
            ),
            [buffer, hidden_one, low_two, one_part], views.core(),
        )
        views.take_core(came)
        buffer = lax.psum_scatter(
            buffer.reshape(8, -1, WIDE), "wide", scatter_dimension=0, tiled=False
        )
        quarter = (4, 2, 2, R // 4, TILE)
        low_one = run_low(*low_operands())
        reduced_sum = Sum(run_outer(me_array, low_one, gated_low), quarter, 0)
        low_one, came, _ = beside(lambda values: values, [low_one], reduced_sum.core())
        reduced_sum.take_core(came)
        (logit_grad, tokens_part), came, _ = beside(
            gate_back_block, gate_back_operands(), reduced_sum.split("x")
        )
        reduced_sum.take(came)
        expand_half, came, _ = beside(
            run_outer, [me_array, mixed_low, logit_grad], reduced_sum.split("y")
        )
        reduced_sum.take(came)
        expand_sum = Sum(expand_half, quarter, 0)
        logit_grad, came, _ = beside(lambda values: values, [logit_grad], expand_sum.core())
        expand_sum.take_core(came)
        (low_squeezed, kernel_grads), came, _ = beside(
            mixing_back_block, mixing_back_operands(),
            expand_sum.split("x") + reduced_sum.split("z"),
        )
        expand_sum.take(came[:1])
        reduced_sum.take(came[1:])
        squeeze_half, came, _ = beside(
            run_outer, [me_array, low_squeezed, tokens],
            expand_sum.split("y") + reduced_sum.spread(),
        )
        expand_sum.take(came[:1])
        reduced_sum.take_spread(came[1:])
        squeezed = Sum(squeeze_half, quarter, 0)
        tokens_part, came, _ = beside(lambda values: values, [tokens_part], squeezed.core())
        squeezed.take_core(came)
        stem_back, came, _ = beside(
            run_stem_back, stem_back_operands(), squeezed.split("x") + expand_sum.split("z")
        )
        squeezed.take(came[:1])
        expand_sum.take(came[1:])
        few = few_of(stem_back, kernel_grads)
        (tokens_grad, few, buffer), came, _ = beside(
            lambda mine, blocks, part, low, grads, quarters: (
                tokens_block(mine, blocks, part, low),
                lax.all_to_all(grads, "wide", 0, 0, tiled=True),
                lax.all_to_all(quarters, "narrow", 0, 0, tiled=True),
            ),
            [me_array, squeeze, tokens_part, low_squeezed, few, buffer.reshape(4, -1, WIDE)],
            squeezed.split("y") + expand_sum.spread(),
        )
        buffer = jnp.sum(buffer.astype(f32), 0)
        squeezed.take(came[:1])
        expand_sum.take_spread(came[1:])
        few = jnp.sum(few, 0)
        few, came, _ = beside(
            lambda part: part + exchange(part, 1), [few], squeezed.split("z")
        )
        squeezed.take(came)
        buffers = Sum((None, None), (), 0)
        buffers.values = buffer
        few, came, _ = beside(
            lambda part: part + exchange(part, 2), [few], squeezed.spread() + buffers.spread()
        )
        squeezed.take_spread(came[:3])
        buffers.take_spread(came[3:])
        buffer = buffers.whole
        sum_stem = few[:24].reshape(8, 3 * TILE)[:, : stem_weight.shape[0]].T
        sum_next = few[24:33, :inner_width]
        sum_scale = few[24:33, LANES : LANES + inner_width]
        sum_restore = buffer[:, :RESTORE_ROWS].swapaxes(0, 1).reshape(w_restore.shape)
        sum_spatial = buffer[:, RESTORE_ROWS:].reshape(4, 9, 16, B).swapaxes(0, 1)
        sum_spatial = sum_spatial.reshape(w_spatial.shape)
        sum_reduce = reduced_sum.whole.reshape(B, TILE).T
        sum_expand = expand_sum.whole.reshape(R, TILE)
        sum_squeeze = squeezed.whole.reshape(R, TILE).T
        factors = [array.reshape(-1, C + TILE) for array in views.arrays]
    else:
        low_three, norm_two_grad, two_part = run_fifth(*fifth_operands)
        buffer = restore_outer_block(hidden_two, low_three)
        two_grads = swap_total(two_part)
        low_two, norm_one_grad, one_part = run_sixth(*sixth_operands())
        one_grads = swap_total(one_part)
        buffer = spatial_block(buffer.reshape(32, -1, WIDE), hidden_one, low_two)
        low_one = run_low(*low_operands())
        reduce_half = run_outer(me_array, low_one, gated_low)
        logit_grad, tokens_part = gate_back_block(*gate_back_operands())
        expand_half = run_outer(me_array, mixed_low, logit_grad)
        low_squeezed, kernel_grads = mixing_back_block(*mixing_back_operands())
        few = few_of(run_stem_back(*stem_back_operands()), kernel_grads)
        squeeze_half = run_outer(me_array, low_squeezed, tokens)
        tokens_grad = tokens_block(me_array, squeeze, tokens_part, low_squeezed)
        few = lax.psum(few, AXES)
        sum_stem = few[:, :24].reshape(STEM, 3 * TILE)[:, : stem_weight.shape[0]].T
        sum_next, sum_scale = (
            few[:, 24:33, at : at + R // 8].swapaxes(0, 1).reshape(9, R) for at in (0, LANES)
        )

        def own_columns(values, width):
            return lax.dynamic_slice_in_dim(values, lax.axis_index("wide") * width, width, 1)

        sum_stem = own_columns(sum_stem, stem_width)
        sum_next = own_columns(sum_next, inner_width)
        sum_scale = own_columns(sum_scale, inner_width)
        sum_restore, sum_spatial, sum_reduce, sum_expand, sum_squeeze = reduced(
            buffer, reduce_half, expand_half, squeeze_half
        )
        factors = [lax.all_gather(factors, AXES, tiled=True)]
    sum_class = sum(
        product_left(
            lax.dynamic_slice_in_dim(part, lax.axis_index("wide") * outer_width, outer_width, 1),
            part[:, C : C + CLASSES],
        )
        for part in factors
    )
    def own_slice(values, width):
        return lax.dynamic_slice_in_dim(values, lax.axis_index("wide") * width, width)

    return (
        activations,
        stem_features,
        tokens_grad,
        sum_stem,
        own_slice(stem_grads[1, :STEM], stem_width),
        own_slice(stem_grads[0, :STEM], stem_width),
        sum_squeeze,
        sum_next,
        sum_scale,
        sum_expand,
        sum_reduce,
        own_slice(one_grads[1], inner_width),
        own_slice(one_grads[0], inner_width),
        sum_spatial,
        own_slice(two_grads[1], inner_width),
        own_slice(two_grads[0], inner_width),
        sum_restore,
        own_slice(three_grads[1], outer_width),
        own_slice(three_grads[0], outer_width),
        sum_class,
        class_bias_grad,
        loss,
    )


def solution(mesh):
    in_specs = (
        P(("wide", "narrow"), None, None, None, None, None),
        P(("wide", "narrow"), None),
        P(("wide", "narrow"), None),
        P(),
        P(),
        P(None, "wide"),
        P("wide"),
        P("wide"),
        P("wide", None),
        P(None, "wide"),
        P(None, "wide"),
        P(None, "wide"),
        P("wide", None),
        P("wide"),
        P("wide"),
        P(None, "wide", None),
        P("wide"),
        P("wide"),
        P("wide", None),
        P("wide"),
        P("wide"),
        P("wide", None),
        P(),
    )
    out_specs = (
        P(("wide", "narrow"), None),
        P(("wide", "narrow"), None),
        P(("wide", "narrow"), None),
        P(None, "wide"),
        P("wide"),
        P("wide"),
        P("wide", None),
        P(None, "wide"),
        P(None, "wide"),
        P(None, "wide"),
        P("wide", None),
        P("wide"),
        P("wide"),
        P(None, "wide", None),
        P("wide"),
        P("wide"),
        P("wide", None),
        P("wide"),
        P("wide"),
        P("wide", None),
        P(),
        P(),
    )
    return jax.shard_map(shards, mesh=mesh, in_specs=in_specs, out_specs=out_specs, check_vma=False)
```

profile of v0, /device:TPU:0, one launch (start us, length us, event | category | flops | bytes accessed | tf_op | source)
XLA Modules:
  0.0 549.9 jit_solution(17001680773738286297)
XLA Ops:
  9.6 2.0 copy.116
  16.6 2.9 shard_map.390
  19.5 3.0 collective-permute-start
  22.5 2.6 collective-permute-start.1
  25.5 7.6 %collective-permute-done.1 = bf16[96,512]{1,0:T(8,128)(2,1)S(1)} collective-permute-done((bf16[96,512]{1,0:T(8,128)(2,1)}, bf16[96,512]{1,0:T(8,128)(2,1)S(1)}, u32[]{:S(2)}, u32[]{:S(2)}) %collective-permute-start.1) | collective-permute-done | bytes 98336 | tf_op jit(solution)/shard_map/ppermute | solution.py:44
  40.6 7.8 %shard_map.392.refs_0_ = bf16[2,19,32,384]{3,2,1,0:T(8,128)(2,1)} custom-call(bf16[32,5,3,32,32]{4,3,2,1,0:T(8,128)(2,1)} %bitcast.250), custom_call_target="tpu_custom_call" | custom-call | flops 98304000 | bytes 16777216 | tf_op jit(solution)/shard_map/pallas_call | solution.py:331
  50.7 2.2 shard_map.394
  53.0 1.9 slice.132.refs_1_
  55.6 1.6 copy.118.refs_1_
  59.2 2.0 collective-permute-start.9
  63.6 10.5 %shard_map.396 = (f32[512,1024]{1,0:T(8,128)}, f32[2,1024]{1,0:T(2,128)}) custom-call(bf16[2,19,32,384]{3,2,1,0:T(8,128)(2,1)} %shard_map.392.refs_0_, bf16[8,384,256]{2,1,0:T(8,128)(2,1)} %copy.118.refs_1_, bf16[7,256,128]{2,1,0:T(8,128)(2,1)} %get-tuple-element.356.refs_2_), custom_call_target="tpu_custom_call" | custom-call | flops 5637144576 | bytes 16777216 | tf_op jit(solution)/shard_map/pallas_call | solution.py:331
  79.2 15.1 %shard_map.399 = (f32[1568,512]{1,0:T(8,128)}, f32[1568,512]{1,0:T(8,128)}, bf16[1568,512]{1,0:T(8,128)(2,1)}) custom-call(s32[1]{0:T(128)} %bitcast.refs_0_, bf16[8,64,512]{2,1,0:T(8,128)(2,1)} %slice.132.refs_1_, bf16[8,64,512]{2,1,0:T(8,128)(2,1)} %copy-done.43, bf16[8,64,512]{2,1,0:T(8,128)(2,1)} %copy-done.44, bf16[8,64,512]{2,1,0:T(8,128)(2,1)} %copy-done.45, ...), custom_call_target="tpu_custom_call" | custom-call | flops 6576668672 | bytes 16777216 | tf_op jit(solution)/shard_map/pallas_call | solution.py:331
  94.3 8.0 %collective-permute-done.14.refs_2_ = bf16[8,128,512]{2,1,0:T(8,128)(2,1)S(1)} collective-permute-done((bf16[8,128,512]{2,1,0:T(8,128)(2,1)S(1)}, bf16[8,128,512]{2,1,0:T(8,128)(2,1)S(1)}, u32[]{:S(2)}, u32[]{:S(2)}) %collective-permute-start.14) | collective-permute-done | bytes 1048608 | tf_op jit(solution)/shard_map/ppermute | solution.py:44
  102.8 2.9 collective-permute-done.16.refs_3_
  107.9 19.9 %shard_map.401 = (bf16[1568,2048]{1,0:T(8,128)(2,1)}, bf16[1568,2048]{1,0:T(8,128)(2,1)}, f32[1568,512]{1,0:T(8,128)}, f32[2,512]{1,0:T(2,128)}) custom-call(s32[1]{0:T(128)} %bitcast.refs_0_, bf16[8,128,512]{2,1,0:T(8,128)(2,1)} %copy-done.1, bf16[8,128,512]{2,1,0:T(8,128)(2,1)} %copy-done.10, bf16[8,128,512]{2,1,0:T(8,128)(2,1)} %copy-done.11, ...), custom_call_target="tpu_custom_call" | custom-call | flops 13153337344 | bytes 16777216 | tf_op jit(solution)/shard_map/pallas_call | solution.py:331
  127.9 11.0 %collective-permute-done.18.refs_2_ = bf16[8,144,512]{2,1,0:T(8,128)(2,1)S(1)} collective-permute-done((bf16[8,144,512]{2,1,0:T(8,128)(2,1)S(1)}, bf16[8,144,512]{2,1,0:T(8,128)(2,1)S(1)}, u32[]{:S(2)}, u32[]{:S(2)}) %collective-permute-start.18) | collective-permute-done | bytes 1179680 | tf_op jit(solution)/shard_map/ppermute | solution.py:44
  140.9 4.2 all-to-all-start
  145.5 11.8 %all-to-all-done = f32[32,3,512]{2,1,0:T(4,128)S(1)} async-done(((f32[32,3,512]{2,1,0:T(4,128)}), f32[32,3,512]{2,1,0:T(4,128)S(1)}, u32[]{:S(2)}, u32[]{:S(2)}) %all-to-all-start) | async-done | bytes 196640 | tf_op jit(solution)/shard_map/all_to_all | solution.py:67
  158.0 15.8 %shard_map.402 = (bf16[2,1008,1536]{2,1,0:T(8,128)(2,1)}, f32[1568,512]{1,0:T(8,128)}, f32[2,512]{1,0:T(2,128)}) custom-call(s32[1]{0:T(128)} %bitcast.refs_0_, bf16[8,144,512]{2,1,0:T(8,128)(2,1)} %copy-done.2, bf16[8,144,512]{2,1,0:T(8,128)(2,1)} %copy-done.42, bf16[8,144,512]{2,1,0:T(8,128)(2,1)} %collective-permute-done.19.refs_3_, ...), custom_call_target="tpu_custom_call" | custom-call | flops 14797504512 | bytes 16777216 | tf_op jit(solution)/shard_map/pallas_call | solution.py:331
  175.1 4.1 all-to-all-start.1
  180.7 5.1 shard_map.404
  188.1 12.1 %shard_map.403 = (bf16[1568,512]{1,0:T(8,128)(2,1)}, bf16[1568,2048]{1,0:T(8,128)(2,1)}, f32[2,2048]{1,0:T(2,128)}) custom-call(f32[1568,512]{1,0:T(8,128)} %get-tuple-element.475.refs_0_.refs_7_.refs_6_, f32[2,512]{1,0:T(2,128)} %reduce_sum.177.refs_1_.refs_8_.refs_7_, f32[2,512]{1,0:T(2,128)} %get-tuple-element.477.refs_2_.refs_9_.refs_8_, ...), custom_call_target="tpu_custom_call" | custom-call | flops 6576668672 | bytes 16777216 | tf_op jit(solution)/shard_map/pallas_call | solution.py:331
  202.9 2.0 collective-permute-start.24
  209.4 3.4 collective-permute-start.27
  215.4 2.2 collective-permute-done.26
  218.2 14.2 %shard_map.405 = (bf16[1568,2048]{1,0:T(8,128)(2,1)}, bf16[1568,2048]{1,0:T(8,128)(2,1)}, f32[2,8,2048]{2,1,0:T(8,128)}) custom-call(bf16[1568,2048]{1,0:T(8,128)(2,1)} %get-tuple-element.441.refs_0_.refs_1_, bf16[1568,2048]{1,0:T(8,128)(2,1)} %get-tuple-element.429.refs_1_.refs_2_, f32[3,2048]{1,0:T(4,128)} %add_add_fusion.2.refs_2_.refs_3_, ...), custom_call_target="tpu_custom_call" | custom-call | flops 128450560 | bytes 16777216 | tf_op jit(solution)/shard_map/pallas_call | solution.py:331
  235.1 3.0 collective-permute-start.28
  242.8 3.2 collective-permute-start.33
  251.0 2.3 collective-permute-start.36
  260.0 1.9 collective-permute-start.38
  263.2 16.7 %shard_map.406 = (bf16[1568,2048]{1,0:T(8,128)(2,1)}, f32[1568,512]{1,0:T(8,128)}, f32[2,512]{1,0:T(2,128)}) custom-call(bf16[1568,2048]{1,0:T(8,128)(2,1)} %get-tuple-element.512.refs_0_.refs_6_, bf16[1568,2048]{1,0:T(8,128)(2,1)} %get-tuple-element.441.refs_0_.refs_1_, f32[2,2,2048]{2,1,0:T(2,128)} %reshape.310.refs_2_.refs_7_, ...), custom_call_target="tpu_custom_call" | custom-call | flops 6576668672 | bytes 16777216 | tf_op jit(solution)/shard_map/pallas_call | solution.py:331
  281.6 4.5 all-to-all-start.2
  286.1 1.8 collective-permute-start.40
  287.9 8.3 %shard_map.408 = bf16[8,4,208,512]{3,2,1,0:T(8,128)(2,1)} custom-call(bf16[1568,512]{1,0:T(8,128)(2,1)} %get-tuple-element.463.refs_0_, bf16[1568,2048]{1,0:T(8,128)(2,1)} %get-tuple-element.464.refs_1_), custom_call_target="tpu_custom_call" | custom-call | flops 6576668672 | bytes 16777216 | tf_op jit(solution)/shard_map/pallas_call | solution.py:331
  298.8 18.2 %shard_map.410 = (bf16[1568,512]{1,0:T(8,128)(2,1)}, f32[1568,512]{1,0:T(8,128)}, f32[2,512]{1,0:T(2,128)}) custom-call(s32[1]{0:T(128)} %bitcast.refs_0_, bf16[8,144,512]{2,1,0:T(8,128)(2,1)} %copy-done.2, bf16[8,144,512]{2,1,0:T(8,128)(2,1)} %copy-done.42, bf16[8,144,512]{2,1,0:T(8,128)(2,1)} %collective-permute-done.19.refs_3_, ...), custom_call_target="tpu_custom_call" | custom-call | flops 14797504512 | bytes 16777216 | tf_op jit(solution)/shard_map/pallas_call | solution.py:331
  318.4 3.7 all-to-all-start.3
  322.9 17.5 %shard_map.411 = bf16[32,208,512]{2,1,0:T(8,128)(2,1)} custom-call(bf16[32,208,512]{2,1,0:T(8,128)(2,1)} %bitcast.237, bf16[2,1008,1536]{2,1,0:T(8,128)(2,1)} %get-tuple-element.493.refs_1_, bf16[1568,512]{1,0:T(8,128)(2,1)} %get-tuple-element.494.refs_2_), custom_call_target="tpu_custom_call", output_to_operand_aliasing={{}: (0, {})} | custom-call | flops 14797504512 | bytes 16777216 | tf_op jit(solution)/shard_map/pallas_call | solution.py:331
  344.5 1.6 copy.137
  347.0 4.6 shard_map.412.refs_1_.refs_5_
  351.6 8.7 %shard_map.413 = (f32[8,256,256]{2,1,0:T(8,128)}, bf16[8,256,256]{2,1,0:T(8,128)(2,1)}) custom-call(s32[1]{0:T(128)} %bitcast.refs_0_, bf16[1568,512]{1,0:T(8,128)(2,1)} %shard_map.412.refs_1_.refs_5_, bf16[1568,2048]{1,0:T(8,128)(2,1)} %get-tuple-element.429.refs_1_.refs_2_), custom_call_target="tpu_custom_call" | custom-call | flops 6576668672 | bytes 16777216 | tf_op jit(solution)/shard_map/pallas_call | solution.py:331
  364.6 1.9 convert_add_fusion.2
  366.6 1.7 collective-permute-start.45
  368.3 19.2 %shard_map.414 = (bf16[1568,2048]{1,0:T(8,128)(2,1)}, bf16[1568,2048]{1,0:T(8,128)(2,1)}) custom-call(s32[1]{0:T(128)} %bitcast.refs_0_, bf16[8,128,512]{2,1,0:T(8,128)(2,1)} %copy-done.1, bf16[8,128,512]{2,1,0:T(8,128)(2,1)} %copy-done.10, bf16[8,128,512]{2,1,0:T(8,128)(2,1)} %copy-done.11, bf16[8,128,512]{2,1,0:T(8,128)(2,1)} %collective-permute-done.17.refs_4_, ...), custom_call_target="tpu_custom_call" | custom-call | flops 6576668672 | bytes 16777216 | tf_op jit(solution)/shard_map/pallas_call | solution.py:331
  391.1 8.7 %shard_map.415 = (f32[8,256,256]{2,1,0:T(8,128)}, bf16[8,256,256]{2,1,0:T(8,128)(2,1)}) custom-call(s32[1]{0:T(128)} %bitcast.refs_0_, bf16[1568,512]{1,0:T(8,128)(2,1)} %get-tuple-element.523.refs_6_.refs_1_, bf16[1568,2048]{1,0:T(8,128)(2,1)} %get-tuple-element.542.refs_2_.refs_5_), custom_call_target="tpu_custom_call" | custom-call | flops 6576668672 | bytes 16777216 | tf_op jit(solution)/shard_map/pallas_call | solution.py:331
  405.5 2.4 collective-permute-start.50
  408.7 20.3 %shard_map.416 = (bf16[1568,512]{1,0:T(8,128)(2,1)}, f32[18,512]{1,0:T(8,128)}) custom-call(s32[1]{0:T(128)} %bitcast.refs_0_, bf16[8,128,512]{2,1,0:T(8,128)(2,1)} %copy-done.1, bf16[8,128,512]{2,1,0:T(8,128)(2,1)} %copy-done.10, bf16[8,128,512]{2,1,0:T(8,128)(2,1)} %copy-done.11, bf16[8,128,512]{2,1,0:T(8,128)(2,1)} %collective-permute-done.17.refs_4_, ...), custom_call_target="tpu_custom_call" | custom-call | flops 6576668672 | bytes 16777216 | tf_op jit(solution)/shard_map/pallas_call | solution.py:331
  434.2 8.9 %shard_map.417 = (f32[8,256,256]{2,1,0:T(8,128)}, bf16[8,256,256]{2,1,0:T(8,128)(2,1)}) custom-call(s32[1]{0:T(128)} %bitcast.refs_0_, bf16[1568,512]{1,0:T(8,128)(2,1)} %get-tuple-element.599.refs_1_.refs_6_, bf16[1568,2048]{1,0:T(8,128)(2,1)} %refs_2_.2), custom_call_target="tpu_custom_call" | custom-call | flops 6576668672 | bytes 16777216 | tf_op jit(solution)/shard_map/pallas_call | solution.py:331
  451.1 3.2 collective-permute-start.59
  454.9 14.2 %shard_map.418 = f32[7,256,128]{2,1,0:T(8,128)} custom-call(bf16[2,19,32,384]{3,2,1,0:T(8,128)(2,1)} %shard_map.392.refs_0_, bf16[8,256,384]{2,1,0:T(8,128)(2,1)} %bitcast.245, f32[512,1024]{1,0:T(8,128)} %get-tuple-element.577.refs_0_.refs_2_, f32[2,1024]{1,0:T(2,128)} %tile.22.refs_1_.refs_3_, f32[2,1024]{1,0:T(2,128)} %get-tuple-element.579.refs_2_.refs_4_, ...), custom_call_target="tpu_custom_call" | custom-call | flops 5637144576 | bytes 16777216 | tf_op jit(solution)/shard_map/pallas_call | solution.py:331
  473.2 1.7 select_maximum_fusion
  475.8 5.4 all-to-all-start.4
  481.2 1.7 convolution_add_fusion
  483.0 7.8 %all-to-all-done.4 = f32[8,40,256]{2,1,0:T(8,128)S(1)} async-done(((f32[8,40,256]{2,1,0:T(8,128)}), f32[8,40,256]{2,1,0:T(8,128)S(1)}, u32[]{:S(2)}, u32[]{:S(2)}) %all-to-all-start.4) | async-done | bytes 327712 | tf_op jit(solution)/shard_map/all_to_all | solution.py:1899
  490.7 3.5 all-to-all-start.5
  497.0 1.8 collective-permute-start.63
  498.9 12.0 %shard_map.419 = bf16[1568,2048]{1,0:T(8,128)(2,1)} custom-call(s32[1]{0:T(128)} %bitcast.refs_0_, bf16[8,64,512]{2,1,0:T(8,128)(2,1)} %slice.132.refs_1_, bf16[8,64,512]{2,1,0:T(8,128)(2,1)} %copy-done.43, bf16[8,64,512]{2,1,0:T(8,128)(2,1)} %copy-done.44, bf16[8,64,512]{2,1,0:T(8,128)(2,1)} %copy-done.45, bf16[1568,2048]{1,0:T(8,128)(2,1)} %get-tuple-element.598.refs_5_, ...), custom_call_target="tpu_custom_call" | custom-call | flops 6576668672 | bytes 16777216 | tf_op jit(solution)/shard_map/pallas_call | solution.py:331
  511.4 2.0 collective-permute-start.67
  513.4 2.4 collective-permute-start.68
  516.8 3.3 collective-permute-done.67
  520.1 1.9 collective-permute-start.69
  522.3 1.6 collective-permute-start.72
  524.2 2.2 collective-permute-start.74
  527.6 5.3 collective-permute-done.74
  532.9 3.8 collective-permute-done.75
  (398 shorter events, 123.2 us)
Async XLA Ops:
  7.2 180.9 %all-gather.3.cloned.1.call-start = ((), (), s32[]{:S(2)}) async-start(), calls=%async_computation.8 | async-start | bytes 3244032 | tf_op jit(solution)/shard_map/all_gather | solution.py:1715
  19.5 6.0 %collective-permute-start = (bf16[96,512]{1,0:T(8,128)(2,1)}, bf16[96,512]{1,0:T(8,128)(2,1)S(1)}, u32[]{:S(2)}, u32[]{:S(2)}) collective-permute-start(bf16[96,512]{1,0:T(8,128)(2,1)} %get-tuple-element.337), channel_id=1, source_target_pairs={{0,8},{1,9},{2,10},{3,11},{4,12},{5,13},{6,14},{7,15},{8,0},{9,1},... | collective-permute-start | bytes 294920 | tf_op jit(solution)/shard_map/ppermute | solution.py:44
  22.5 10.6 %collective-permute-start.1 = (bf16[96,512]{1,0:T(8,128)(2,1)}, bf16[96,512]{1,0:T(8,128)(2,1)S(1)}, u32[]{:S(2)}, u32[]{:S(2)}) collective-permute-start(bf16[96,512]{1,0:T(8,128)(2,1)} %get-tuple-element.337), channel_id=1, source_target_pairs={{0,16},{1,17},{2,18},{3,19},{4,20},{5,21},{6,22},{7,23},{8,24},{9,... | collective-permute-start | bytes 294920 | tf_op jit(solution)/shard_map/ppermute | solution.py:44
  25.1 8.1 %collective-permute-start.2 = (bf16[96,512]{1,0:T(8,128)(2,1)}, bf16[96,512]{1,0:T(8,128)(2,1)S(1)}, u32[]{:S(2)}, u32[]{:S(2)}) collective-permute-start(bf16[96,512]{1,0:T(8,128)(2,1)} %get-tuple-element.337), channel_id=1, source_target_pairs={{0,24},{1,25},{2,26},{3,27},{4,28},{5,29},{6,30},{7,31},{8,16},{9,... | collective-permute-start | bytes 294920 | tf_op jit(solution)/shard_map/ppermute | solution.py:44
  34.6 14.9 %collective-permute-start.3 = (bf16[4,96,512]{2,1,0:T(8,128)(2,1)S(1)}, bf16[4,96,512]{2,1,0:T(8,128)(2,1)S(1)}, u32[]{:S(2)}, u32[]{:S(2)}) collective-permute-start(bf16[4,96,512]{2,1,0:T(8,128)(2,1)S(1)} %shard_map.391.refs_0_), channel_id=1, source_target_pairs={{0,4},{1,5},{2,6},{3,7},{4,0},{5,1},{6,2},{7,3},{8,12},{9,13},{10,... | collective-permute-start | bytes 1179656 | tf_op jit(solution)/shard_map/ppermute | solution.py:44
  36.2 12.2 %collective-permute-start.4 = (bf16[128,512]{1,0:T(8,128)(2,1)}, bf16[128,512]{1,0:T(8,128)(2,1)S(1)}, u32[]{:S(2)}, u32[]{:S(2)}) collective-permute-start(bf16[128,512]{1,0:T(8,128)(2,1)} %get-tuple-element.346), channel_id=1, source_target_pairs={{0,8},{1,9},{2,10},{3,11},{4,12},{5,13},{6,14},{7,15},{8,0},{9,1},... | collective-permute-start | bytes 393224 | tf_op jit(solution)/shard_map/ppermute | solution.py:44
  37.8 11.7 %collective-permute-start.5 = (bf16[128,512]{1,0:T(8,128)(2,1)}, bf16[128,512]{1,0:T(8,128)(2,1)S(1)}, u32[]{:S(2)}, u32[]{:S(2)}) collective-permute-start(bf16[128,512]{1,0:T(8,128)(2,1)} %get-tuple-element.346), channel_id=1, source_target_pairs={{0,16},{1,17},{2,18},{3,19},{4,20},{5,21},{6,22},{7,23},{8,24},{9,... | collective-permute-start | bytes 393224 | tf_op jit(solution)/shard_map/ppermute | solution.py:44
  39.2 10.2 %collective-permute-start.6 = (bf16[128,512]{1,0:T(8,128)(2,1)}, bf16[128,512]{1,0:T(8,128)(2,1)S(1)}, u32[]{:S(2)}, u32[]{:S(2)}) collective-permute-start(bf16[128,512]{1,0:T(8,128)(2,1)} %get-tuple-element.346), channel_id=1, source_target_pairs={{0,24},{1,25},{2,26},{3,27},{4,28},{5,29},{6,30},{7,31},{8,16},{9,... | collective-permute-start | bytes 393224 | tf_op jit(solution)/shard_map/ppermute | solution.py:44
  57.2 16.9 %collective-permute-start.7 = (bf16[8,64,512]{2,1,0:T(8,128)(2,1)}, bf16[8,64,512]{2,1,0:T(8,128)(2,1)S(1)}, u32[]{:S(2)}, u32[]{:S(2)}) collective-permute-start(bf16[8,64,512]{2,1,0:T(8,128)(2,1)} %slice.132.refs_1_), channel_id=1, source_target_pairs={{0,2},{1,3},{2,0},{3,1},{4,6},{5,7},{6,4},{7,5},{8,10},{9,11},{10,... | collective-permute-start | bytes 1572872 | tf_op jit(solution)/shard_map/ppermute | solution.py:44
  58.7 15.5 %collective-permute-start.8 = (bf16[4,128,512]{2,1,0:T(8,128)(2,1)S(1)}, bf16[4,128,512]{2,1,0:T(8,128)(2,1)S(1)}, u32[]{:S(2)}, u32[]{:S(2)}) collective-permute-start(bf16[4,128,512]{2,1,0:T(8,128)(2,1)S(1)} %shard_map.395.refs_0_), channel_id=1, source_target_pairs={{0,4},{1,5},{2,6},{3,7},{4,0},{5,1},{6,2},{7,3},{8,12},{9,13},{10,... | collective-permute-start | bytes 1572872 | tf_op jit(solution)/shard_map/ppermute | solution.py:44
  59.2 14.9 %collective-permute-start.9 = (bf16[144,512]{1,0:T(8,128)(2,1)S(1)}, bf16[144,512]{1,0:T(8,128)(2,1)S(1)}, u32[]{:S(2)}, u32[]{:S(2)}) collective-permute-start(bf16[144,512]{1,0:T(8,128)(2,1)S(1)} %copy-done.3), channel_id=1, source_target_pairs={{0,8},{1,9},{2,10},{3,11},{4,12},{5,13},{6,14},{7,15},{8,0},{9,1},... | collective-permute-start | bytes 442376 | tf_op jit(solution)/shard_map/ppermute | solution.py:44
  61.1 13.0 %collective-permute-start.10 = (bf16[144,512]{1,0:T(8,128)(2,1)S(1)}, bf16[144,512]{1,0:T(8,128)(2,1)S(1)}, u32[]{:S(2)}, u32[]{:S(2)}) collective-permute-start(bf16[144,512]{1,0:T(8,128)(2,1)S(1)} %copy-done.3), channel_id=1, source_target_pairs={{0,16},{1,17},{2,18},{3,19},{4,20},{5,21},{6,22},{7,23},{8,24},{9,... | collective-permute-start | bytes 442376 | tf_op jit(solution)/shard_map/ppermute | solution.py:44
  62.2 11.9 %collective-permute-start.11 = (bf16[144,512]{1,0:T(8,128)(2,1)S(1)}, bf16[144,512]{1,0:T(8,128)(2,1)S(1)}, u32[]{:S(2)}, u32[]{:S(2)}) collective-permute-start(bf16[144,512]{1,0:T(8,128)(2,1)S(1)} %copy-done.3), channel_id=1, source_target_pairs={{0,24},{1,25},{2,26},{3,27},{4,28},{5,29},{6,30},{7,31},{8,16},{9,... | collective-permute-start | bytes 442376 | tf_op jit(solution)/shard_map/ppermute | solution.py:44
  77.1 25.2 %collective-permute-start.14 = (bf16[8,128,512]{2,1,0:T(8,128)(2,1)S(1)}, bf16[8,128,512]{2,1,0:T(8,128)(2,1)S(1)}, u32[]{:S(2)}, u32[]{:S(2)}) collective-permute-start(bf16[8,128,512]{2,1,0:T(8,128)(2,1)S(1)} %shard_map.398.refs_1_), channel_id=1, source_target_pairs={{0,2},{1,3},{2,0},{3,1},{4,6},{5,7},{6,4},{7,5},{8,10},{9,11},{10,... | collective-permute-start | bytes 3145736 | tf_op jit(solution)/shard_map/ppermute | solution.py:44
  77.7 16.7 %collective-permute-start.15 = (bf16[4,144,512]{2,1,0:T(8,128)(2,1)S(1)}, bf16[4,144,512]{2,1,0:T(8,128)(2,1)S(1)}, u32[]{:S(2)}, u32[]{:S(2)}) collective-permute-start(bf16[4,144,512]{2,1,0:T(8,128)(2,1)S(1)} %shard_map.397.refs_0_), channel_id=1, source_target_pairs={{0,4},{1,5},{2,6},{3,7},{4,0},{5,1},{6,2},{7,3},{8,12},{9,13},{10,... | collective-permute-start | bytes 1769480 | tf_op jit(solution)/shard_map/ppermute | solution.py:44
  107.3 31.6 %collective-permute-start.18 = (bf16[8,144,512]{2,1,0:T(8,128)(2,1)S(1)}, bf16[8,144,512]{2,1,0:T(8,128)(2,1)S(1)}, u32[]{:S(2)}, u32[]{:S(2)}) collective-permute-start(bf16[8,144,512]{2,1,0:T(8,128)(2,1)S(1)} %shard_map.400.refs_1_), channel_id=1, source_target_pairs={{0,2},{1,3},{2,0},{3,1},{4,6},{5,7},{6,4},{7,5},{8,10},{9,11},{10,... | collective-permute-start | bytes 3538952 | tf_op jit(solution)/shard_map/ppermute | solution.py:44
  139.6 18.4 %collective-permute-start.19 = (bf16[8,144,512]{2,1,0:T(8,128)(2,1)S(1)}, bf16[8,144,512]{2,1,0:T(8,128)(2,1)}, u32[]{:S(2)}, u32[]{:S(2)}) collective-permute-start(bf16[8,144,512]{2,1,0:T(8,128)(2,1)S(1)} %shard_map.400.refs_1_), channel_id=1, source_target_pairs={{0,1},{1,0},{2,3},{3,2},{4,5},{5,4},{6,7},{7,6},{8,9},{9,8},{10,11... | collective-permute-start | bytes 3538952 | tf_op jit(solution)/shard_map/ppermute | solution.py:44
  139.7 18.3 %collective-permute-start.20 = (bf16[8,144,512]{2,1,0:T(8,128)(2,1)S(1)}, bf16[8,144,512]{2,1,0:T(8,128)(2,1)}, u32[]{:S(2)}, u32[]{:S(2)}) collective-permute-start(bf16[8,144,512]{2,1,0:T(8,128)(2,1)S(1)} %collective-permute-done.18.refs_2_), channel_id=1, source_target_pairs={{0,1},{1,0},{2,3},{3,2},{4,5},{5,4},{6,7},{7,6},{8,9},{9,8},{10,11... | collective-permute-start | bytes 3538952 | tf_op jit(solution)/shard_map/ppermute | solution.py:44
  140.9 16.4 %all-to-all-start = ((f32[32,3,512]{2,1,0:T(4,128)}), f32[32,3,512]{2,1,0:T(4,128)S(1)}, u32[]{:S(2)}, u32[]{:S(2)}) async-start(f32[32,3,512]{2,1,0:T(4,128)} %broadcast_in_dim.139), calls=%async_computation | async-start | bytes 524288 | tf_op jit(solution)/shard_map/all_to_all | solution.py:67
  175.1 12.3 %all-to-all-start.1 = ((f32[32,2,512]{2,1,0:T(2,128)}), f32[32,2,512]{2,1,0:T(2,128)S(1)}, u32[]{:S(2)}, u32[]{:S(2)}) async-start(f32[32,2,512]{2,1,0:T(2,128)} %broadcast_in_dim.140), calls=%async_computation.1 | async-start | bytes 262144 | tf_op jit(solution)/shard_map/all_to_all | solution.py:67
  202.9 5.0 collective-permute-start.24
  209.4 6.0 %collective-permute-start.27 = (f32[3,2048]{1,0:T(4,128)S(1)}, f32[3,2048]{1,0:T(4,128)S(1)}, u32[]{:S(2)}, u32[]{:S(2)}) collective-permute-start(f32[3,2048]{1,0:T(4,128)S(1)} %add_add_fusion.3), channel_id=1, source_target_pairs={{0,24},{1,25},{2,26},{3,27},{4,28},{5,29},{6,30},{7,31},{8,16},{9,... | collective-permute-start | bytes 73736 | tf_op jit(solution)/shard_map/ppermute | solution.py:44
  212.8 4.8 collective-permute-start.26
  242.8 5.6 %collective-permute-start.33 = (f32[3,2048]{1,0:T(4,128)S(1)}, f32[3,2048]{1,0:T(4,128)S(1)}, u32[]{:S(2)}, u32[]{:S(2)}) collective-permute-start(f32[3,2048]{1,0:T(4,128)S(1)} %fusion.52), channel_id=1, source_target_pairs={{0,6},{1,7},{2,4},{3,5},{4,2},{5,3},{6,0},{7,1},{8,14},{9,15},{10,... | collective-permute-start | bytes 73736 | tf_op jit(solution)/shard_map/ppermute | solution.py:44
  251.0 5.9 %collective-permute-start.36 = (f32[3,2048]{1,0:T(4,128)S(1)}, f32[3,2048]{1,0:T(4,128)S(1)}, u32[]{:S(2)}, u32[]{:S(2)}) collective-permute-start(f32[3,2048]{1,0:T(4,128)S(1)} %add_add_fusion.1), channel_id=1, source_target_pairs={{0,24},{1,25},{2,26},{3,27},{4,28},{5,29},{6,30},{7,31},{8,16},{9,... | collective-permute-start | bytes 73736 | tf_op jit(solution)/shard_map/ppermute | solution.py:44
  253.3 4.9 collective-permute-start.35
  258.9 21.1 %collective-permute-start.37 = (bf16[8,2304]{1,0:T(8,128)(2,1)S(1)}, bf16[8,2304]{1,0:T(8,128)(2,1)S(1)}, u32[]{:S(2)}, u32[]{:S(2)}) collective-permute-start(bf16[8,2304]{1,0:T(8,128)(2,1)S(1)} %get-tuple-element.455), channel_id=1, source_target_pairs={{0,8},{1,9},{2,10},{3,11},{4,12},{5,13},{6,14},{7,15},{8,0},{9,1},... | collective-permute-start | bytes 110600 | tf_op jit(solution)/shard_map/ppermute | solution.py:44
  260.0 20.0 %collective-permute-start.38 = (bf16[8,2304]{1,0:T(8,128)(2,1)S(1)}, bf16[8,2304]{1,0:T(8,128)(2,1)S(1)}, u32[]{:S(2)}, u32[]{:S(2)}) collective-permute-start(bf16[8,2304]{1,0:T(8,128)(2,1)S(1)} %get-tuple-element.455), channel_id=1, source_target_pairs={{0,16},{1,17},{2,18},{3,19},{4,20},{5,21},{6,22},{7,23},{8,24},{9,... | collective-permute-start | bytes 110600 | tf_op jit(solution)/shard_map/ppermute | solution.py:44
  261.9 18.0 %collective-permute-start.39 = (bf16[8,2304]{1,0:T(8,128)(2,1)S(1)}, bf16[8,2304]{1,0:T(8,128)(2,1)S(1)}, u32[]{:S(2)}, u32[]{:S(2)}) collective-permute-start(bf16[8,2304]{1,0:T(8,128)(2,1)S(1)} %get-tuple-element.455), channel_id=1, source_target_pairs={{0,24},{1,25},{2,26},{3,27},{4,28},{5,29},{6,30},{7,31},{8,16},{9,... | collective-permute-start | bytes 110600 | tf_op jit(solution)/shard_map/ppermute | solution.py:44
  281.6 14.6 %all-to-all-start.2 = ((f32[32,2,512]{2,1,0:T(2,128)}), f32[32,2,512]{2,1,0:T(2,128)S(1)}, u32[]{:S(2)}, u32[]{:S(2)}) async-start(f32[32,2,512]{2,1,0:T(2,128)} %broadcast_in_dim.147), calls=%async_computation.2 | async-start | bytes 262144 | tf_op jit(solution)/shard_map/all_to_all | solution.py:67
  286.1 10.8 %collective-permute-start.40 = (bf16[4,8,2304]{2,1,0:T(8,128)(2,1)S(1)}, bf16[4,8,2304]{2,1,0:T(8,128)(2,1)S(1)}, u32[]{:S(2)}, u32[]{:S(2)}) collective-permute-start(bf16[4,8,2304]{2,1,0:T(8,128)(2,1)S(1)} %shard_map.407.refs_0_), channel_id=1, source_target_pairs={{0,4},{1,5},{2,6},{3,7},{4,0},{5,1},{6,2},{7,3},{8,12},{9,13},{10,... | collective-permute-start | bytes 442376 | tf_op jit(solution)/shard_map/ppermute | solution.py:44
  297.3 19.7 %collective-permute-start.41 = (bf16[8,8,2304]{2,1,0:T(8,128)(2,1)S(1)}, bf16[8,8,2304]{2,1,0:T(8,128)(2,1)S(1)}, u32[]{:S(2)}, u32[]{:S(2)}) collective-permute-start(bf16[8,8,2304]{2,1,0:T(8,128)(2,1)S(1)} %shard_map.409), channel_id=1, source_target_pairs={{0,2},{1,3},{2,0},{3,1},{4,6},{5,7},{6,4},{7,5},{8,10},{9,11},{10,... | collective-permute-start | bytes 884744 | tf_op jit(solution)/shard_map/ppermute | solution.py:44
  318.4 22.1 %all-to-all-start.3 = ((f32[32,2,512]{2,1,0:T(2,128)}), f32[32,2,512]{2,1,0:T(2,128)S(1)}, u32[]{:S(2)}, u32[]{:S(2)}) async-start(f32[32,2,512]{2,1,0:T(2,128)} %broadcast_in_dim.148), calls=%async_computation.3 | async-start | bytes 262144 | tf_op jit(solution)/shard_map/all_to_all | solution.py:67
  322.1 153.7 %reduce-scatter.2.cloned.1.call-start = ((), (), s32[]{:S(2)}) async-start(), calls=%async_computation.7 | async-start | bytes 7667712 | tf_op jit(solution)/shard_map/reduce_scatter | solution.py:1856
  322.4 18.8 %collective-permute-start.42 = (bf16[8,8,2304]{2,1,0:T(8,128)(2,1)S(1)}, bf16[8,8,2304]{2,1,0:T(8,128)(2,1)S(1)}, u32[]{:S(2)}, u32[]{:S(2)}) collective-permute-start(bf16[8,8,2304]{2,1,0:T(8,128)(2,1)S(1)} %shard_map.409), channel_id=1, source_target_pairs={{0,1},{1,0},{2,3},{3,2},{4,5},{5,4},{6,7},{7,6},{8,9},{9,8},{10,11... | collective-permute-start | bytes 884744 | tf_op jit(solution)/shard_map/ppermute | solution.py:44
  322.7 18.5 %collective-permute-start.43 = (bf16[8,8,2304]{2,1,0:T(8,128)(2,1)S(1)}, bf16[8,8,2304]{2,1,0:T(8,128)(2,1)S(1)}, u32[]{:S(2)}, u32[]{:S(2)}) collective-permute-start(bf16[8,8,2304]{2,1,0:T(8,128)(2,1)S(1)} %collective-permute-done.41), channel_id=1, source_target_pairs={{0,1},{1,0},{2,3},{3,2},{4,5},{5,4},{6,7},{7,6},{8,9},{9,8},{10,11... | collective-permute-start | bytes 884744 | tf_op jit(solution)/shard_map/ppermute | solution.py:44
  366.6 20.9 %collective-permute-start.45 = (bf16[4,2,128,256]{3,2,0,1:T(8,128)(2,1)S(1)}, bf16[4,2,128,256]{3,2,0,1:T(8,128)(2,1)S(1)}, u32[]{:S(2)}, u32[]{:S(2)}) collective-permute-start(bf16[4,2,128,256]{3,2,0,1:T(8,128)(2,1)S(1)} %fusion.6), channel_id=1, source_target_pairs={{0,2},{1,3},{2,0},{3,1},{4,6},{5,7},{6,4},{7,5},{8,10},{9,11},{10,... | collective-permute-start | bytes 1572872 | tf_op jit(solution)/shard_map/ppermute | solution.py:44
  389.5 10.2 %collective-permute-start.46 = (bf16[4,128,256]{2,1,0:T(8,128)(2,1)S(1)}, bf16[4,128,256]{2,1,0:T(8,128)(2,1)S(1)}, u32[]{:S(2)}, u32[]{:S(2)}) collective-permute-start(bf16[4,128,256]{2,1,0:T(8,128)(2,1)S(1)} %fusion.8), channel_id=1, source_target_pairs={{0,4},{1,5},{2,6},{3,7},{4,0},{5,1},{6,2},{7,3},{8,12},{9,13},{10,... | collective-permute-start | bytes 786440 | tf_op jit(solution)/shard_map/ppermute | solution.py:44
  403.3 25.6 %collective-permute-start.48 = (bf16[4,2,128,256]{3,2,0,1:T(8,128)(2,1)S(1)}, bf16[4,2,128,256]{3,2,0,1:T(8,128)(2,1)S(1)}, u32[]{:S(2)}, u32[]{:S(2)}) collective-permute-start(bf16[4,2,128,256]{3,2,0,1:T(8,128)(2,1)S(1)} %fusion.7), channel_id=1, source_target_pairs={{0,2},{1,3},{2,0},{3,1},{4,6},{5,7},{6,4},{7,5},{8,10},{9,11},{10,... | collective-permute-start | bytes 1572872 | tf_op jit(solution)/shard_map/ppermute | solution.py:44
  404.3 24.7 %collective-permute-start.49 = (bf16[128,256]{1,0:T(8,128)(2,1)}, bf16[128,256]{1,0:T(8,128)(2,1)S(1)}, u32[]{:S(2)}, u32[]{:S(2)}) collective-permute-start(bf16[128,256]{1,0:T(8,128)(2,1)} %get-tuple-element.550), channel_id=1, source_target_pairs={{0,8},{1,9},{2,10},{3,11},{4,12},{5,13},{6,14},{7,15},{8,0},{9,1},... | collective-permute-start | bytes 196616 | tf_op jit(solution)/shard_map/ppermute | solution.py:44
  405.5 23.5 %collective-permute-start.50 = (bf16[128,256]{1,0:T(8,128)(2,1)S(1)}, bf16[128,256]{1,0:T(8,128)(2,1)}, u32[]{:S(2)}, u32[]{:S(2)}) collective-permute-start(bf16[128,256]{1,0:T(8,128)(2,1)S(1)} %get-tuple-element.551), channel_id=1, source_target_pairs={{0,16},{1,17},{2,18},{3,19},{4,20},{5,21},{6,22},{7,23},{8,24},{9,... | collective-permute-start | bytes 196616 | tf_op jit(solution)/shard_map/ppermute | solution.py:44
  407.9 21.1 %collective-permute-start.51 = (bf16[128,256]{1,0:T(8,128)(2,1)S(1)}, bf16[128,256]{1,0:T(8,128)(2,1)}, u32[]{:S(2)}, u32[]{:S(2)}) collective-permute-start(bf16[128,256]{1,0:T(8,128)(2,1)S(1)} %get-tuple-element.552), channel_id=1, source_target_pairs={{0,24},{1,25},{2,26},{3,27},{4,28},{5,29},{6,30},{7,31},{8,16},{9,... | collective-permute-start | bytes 196616 | tf_op jit(solution)/shard_map/ppermute | solution.py:44
  431.9 11.3 %collective-permute-start.52 = (bf16[4,128,256]{2,1,0:T(8,128)(2,1)S(1)}, bf16[4,128,256]{2,1,0:T(8,128)(2,1)S(1)}, u32[]{:S(2)}, u32[]{:S(2)}) collective-permute-start(bf16[4,128,256]{2,1,0:T(8,128)(2,1)S(1)} %fusion.9), channel_id=1, source_target_pairs={{0,4},{1,5},{2,6},{3,7},{4,0},{5,1},{6,2},{7,3},{8,12},{9,13},{10,... | collective-permute-start | bytes 786440 | tf_op jit(solution)/shard_map/ppermute | solution.py:44
  432.4 10.8 %collective-permute-start.53 = (bf16[128,256]{1,0:T(8,128)(2,1)S(1)}, bf16[128,256]{1,0:T(8,128)(2,1)S(1)}, u32[]{:S(2)}, u32[]{:S(2)}) collective-permute-start(bf16[128,256]{1,0:T(8,128)(2,1)S(1)} %fusion.19), channel_id=1, source_target_pairs={{0,1},{1,0},{2,3},{3,2},{4,5},{5,4},{6,7},{7,6},{8,9},{9,8},{10,11... | collective-permute-start | bytes 196616 | tf_op jit(solution)/shard_map/ppermute | solution.py:44
  432.4 10.8 %collective-permute-start.54 = (bf16[128,256]{1,0:T(8,128)(2,1)S(1)}, bf16[128,256]{1,0:T(8,128)(2,1)S(1)}, u32[]{:S(2)}, u32[]{:S(2)}) collective-permute-start(bf16[128,256]{1,0:T(8,128)(2,1)S(1)} %fusion.19), channel_id=1, source_target_pairs={{0,2},{1,3},{2,0},{3,1},{4,6},{5,7},{6,4},{7,5},{8,10},{9,11},{10,... | collective-permute-start | bytes 196616 | tf_op jit(solution)/shard_map/ppermute | solution.py:44
  433.8 9.4 %collective-permute-start.55 = (bf16[128,256]{1,0:T(8,128)(2,1)S(1)}, bf16[128,256]{1,0:T(8,128)(2,1)S(1)}, u32[]{:S(2)}, u32[]{:S(2)}) collective-permute-start(bf16[128,256]{1,0:T(8,128)(2,1)S(1)} %fusion.19), channel_id=1, source_target_pairs={{0,3},{1,2},{2,1},{3,0},{4,7},{5,6},{6,5},{7,4},{8,11},{9,10},{10,... | collective-permute-start | bytes 196616 | tf_op jit(solution)/shard_map/ppermute | solution.py:44
  449.1 20.1 %collective-permute-start.57 = (bf16[4,2,128,256]{3,2,1,0:T(8,128)(2,1)S(1)}, bf16[4,2,128,256]{3,2,1,0:T(8,128)(2,1)S(1)}, u32[]{:S(2)}, u32[]{:S(2)}) collective-permute-start(bf16[4,2,128,256]{3,2,1,0:T(8,128)(2,1)S(1)} %fusion.5), channel_id=1, source_target_pairs={{0,2},{1,3},{2,0},{3,1},{4,6},{5,7},{6,4},{7,5},{8,10},{9,11},{10,... | collective-permute-start | bytes 1572872 | tf_op jit(solution)/shard_map/ppermute | solution.py:44
  450.6 18.6 %collective-permute-start.58 = (bf16[128,256]{1,0:T(8,128)(2,1)S(1)}, bf16[128,256]{1,0:T(8,128)(2,1)S(1)}, u32[]{:S(2)}, u32[]{:S(2)}) collective-permute-start(bf16[128,256]{1,0:T(8,128)(2,1)S(1)} %get-tuple-element.583), channel_id=1, source_target_pairs={{0,8},{1,9},{2,10},{3,11},{4,12},{5,13},{6,14},{7,15},{8,0},{9,1},... | collective-permute-start | bytes 196616 | tf_op jit(solution)/shard_map/ppermute | solution.py:44
  451.1 18.1 %collective-permute-start.59 = (bf16[128,256]{1,0:T(8,128)(2,1)S(1)}, bf16[128,256]{1,0:T(8,128)(2,1)S(1)}, u32[]{:S(2)}, u32[]{:S(2)}) collective-permute-start(bf16[128,256]{1,0:T(8,128)(2,1)S(1)} %get-tuple-element.584), channel_id=1, source_target_pairs={{0,16},{1,17},{2,18},{3,19},{4,20},{5,21},{6,22},{7,23},{8,24},{9,... | collective-permute-start | bytes 196616 | tf_op jit(solution)/shard_map/ppermute | solution.py:44
  454.3 14.9 %collective-permute-start.60 = (bf16[128,256]{1,0:T(8,128)(2,1)S(1)}, bf16[128,256]{1,0:T(8,128)(2,1)S(1)}, u32[]{:S(2)}, u32[]{:S(2)}) collective-permute-start(bf16[128,256]{1,0:T(8,128)(2,1)S(1)} %get-tuple-element.585), channel_id=1, source_target_pairs={{0,24},{1,25},{2,26},{3,27},{4,28},{5,29},{6,30},{7,31},{8,16},{9,... | collective-permute-start | bytes 196616 | tf_op jit(solution)/shard_map/ppermute | solution.py:44
  475.8 14.9 %all-to-all-start.4 = ((f32[8,40,256]{2,1,0:T(8,128)}), f32[8,40,256]{2,1,0:T(8,128)S(1)}, u32[]{:S(2)}, u32[]{:S(2)}) async-start(f32[8,40,256]{2,1,0:T(8,128)} %select_maximum_fusion), calls=%async_computation.5 | async-start | bytes 655360 | tf_op jit(solution)/shard_map/all_to_all | solution.py:1899
  490.7 20.3 %all-to-all-start.5 = ((bf16[4,208,512]{2,1,0:T(8,128)(2,1)}), bf16[4,208,512]{2,1,0:T(8,128)(2,1)S(1)}, u32[]{:S(2)}, u32[]{:S(2)}) async-start(bf16[4,208,512]{2,1,0:T(8,128)(2,1)} %bitcast.254), calls=%async_computation.6 | async-start | bytes 1703936 | tf_op jit(solution)/shard_map/all_to_all | solution.py:1900
  495.3 15.7 %collective-permute-start.61 = (bf16[4,128,256]{2,1,0:T(8,128)(2,1)S(1)}, bf16[4,128,256]{2,1,0:T(8,128)(2,1)S(1)}, u32[]{:S(2)}, u32[]{:S(2)}) collective-permute-start(bf16[4,128,256]{2,1,0:T(8,128)(2,1)S(1)} %copy-done.16), channel_id=1, source_target_pairs={{0,4},{1,5},{2,6},{3,7},{4,0},{5,1},{6,2},{7,3},{8,12},{9,13},{10,... | collective-permute-start | bytes 786440 | tf_op jit(solution)/shard_map/ppermute | solution.py:44
  496.8 14.2 %collective-permute-start.62 = (bf16[128,256]{1,0:T(8,128)(2,1)S(1)}, bf16[128,256]{1,0:T(8,128)(2,1)S(1)}, u32[]{:S(2)}, u32[]{:S(2)}) collective-permute-start(bf16[128,256]{1,0:T(8,128)(2,1)S(1)} %fusion.16), channel_id=1, source_target_pairs={{0,1},{1,0},{2,3},{3,2},{4,5},{5,4},{6,7},{7,6},{8,9},{9,8},{10,11... | collective-permute-start | bytes 196616 | tf_op jit(solution)/shard_map/ppermute | solution.py:44
  497.0 14.0 %collective-permute-start.63 = (bf16[128,256]{1,0:T(8,128)(2,1)S(1)}, bf16[128,256]{1,0:T(8,128)(2,1)S(1)}, u32[]{:S(2)}, u32[]{:S(2)}) collective-permute-start(bf16[128,256]{1,0:T(8,128)(2,1)S(1)} %fusion.16), channel_id=1, source_target_pairs={{0,2},{1,3},{2,0},{3,1},{4,6},{5,7},{6,4},{7,5},{8,10},{9,11},{10,... | collective-permute-start | bytes 196616 | tf_op jit(solution)/shard_map/ppermute | solution.py:44
  498.8 12.2 %collective-permute-start.64 = (bf16[128,256]{1,0:T(8,128)(2,1)S(1)}, bf16[128,256]{1,0:T(8,128)(2,1)S(1)}, u32[]{:S(2)}, u32[]{:S(2)}) collective-permute-start(bf16[128,256]{1,0:T(8,128)(2,1)S(1)} %fusion.16), channel_id=1, source_target_pairs={{0,3},{1,2},{2,1},{3,0},{4,7},{5,6},{6,5},{7,4},{8,11},{9,10},{10,... | collective-permute-start | bytes 196616 | tf_op jit(solution)/shard_map/ppermute | solution.py:44
  511.2 4.8 collective-permute-start.65
  511.4 5.4 collective-permute-start.66
  511.4 8.6 %collective-permute-start.67 = (bf16[128,256]{1,0:T(8,128)(2,1)S(1)}, bf16[128,256]{1,0:T(8,128)(2,1)S(1)}, u32[]{:S(2)}, u32[]{:S(2)}) collective-permute-start(bf16[128,256]{1,0:T(8,128)(2,1)S(1)} %get-tuple-element.611), channel_id=1, source_target_pairs={{0,16},{1,17},{2,18},{3,19},{4,20},{5,21},{6,22},{7,23},{8,24},{9,... | collective-permute-start | bytes 196616 | tf_op jit(solution)/shard_map/ppermute | solution.py:44
  513.4 6.6 %collective-permute-start.68 = (bf16[128,256]{1,0:T(8,128)(2,1)S(1)}, bf16[128,256]{1,0:T(8,128)(2,1)S(1)}, u32[]{:S(2)}, u32[]{:S(2)}) collective-permute-start(bf16[128,256]{1,0:T(8,128)(2,1)S(1)} %get-tuple-element.612), channel_id=1, source_target_pairs={{0,24},{1,25},{2,26},{3,27},{4,28},{5,29},{6,30},{7,31},{8,16},{9,... | collective-permute-start | bytes 196616 | tf_op jit(solution)/shard_map/ppermute | solution.py:44
  522.0 5.3 collective-permute-start.71
  522.3 5.3 collective-permute-start.72
  524.2 8.7 %collective-permute-start.74 = (bf16[208,512]{1,0:T(8,128)(2,1)S(1)}, bf16[208,512]{1,0:T(8,128)(2,1)S(1)}, u32[]{:S(2)}, u32[]{:S(2)}) collective-permute-start(bf16[208,512]{1,0:T(8,128)(2,1)S(1)} %reduce_sum.193), channel_id=1, source_target_pairs={{0,2},{1,3},{2,0},{3,1},{4,6},{5,7},{6,4},{7,5},{8,10},{9,11},{10,... | collective-permute-start | bytes 638984 | tf_op jit(solution)/shard_map/ppermute | solution.py:44
  526.4 10.3 %collective-permute-start.75 = (bf16[208,512]{1,0:T(8,128)(2,1)S(1)}, bf16[208,512]{1,0:T(8,128)(2,1)S(1)}, u32[]{:S(2)}, u32[]{:S(2)}) collective-permute-start(bf16[208,512]{1,0:T(8,128)(2,1)S(1)} %reduce_sum.193), channel_id=1, source_target_pairs={{0,3},{1,2},{2,1},{3,0},{4,7},{5,6},{6,5},{7,4},{8,11},{9,10},{10,... | collective-permute-start | bytes 638984 | tf_op jit(solution)/shard_map/ppermute | solution.py:44
  (67 other events, 499.3 us)
Sparse Core Ops, SparseCore 0:
  107.0 60.1 all-gather.2
  341.3 132.1 reduce-scatter.1
where the time goes:
time: 561 us; the launch traced here: 550 us
  Pallas kernels  266 us (47%)
  starting transfers between devices  111 us (20%)
  waiting for transfers between devices  78.1 us (14%)
  local copies, waits for them, and re-layouts  47.5 us (8%)
  other arithmetic  24.5 us (4%)
  between operations  17.7 us (3%)
    pallas_call x30, Pallas kernels, kernel_call(): return lambda *operands: call(*operands, *after)  266 us
    ppermute x74, starting transfers between devices, exchange(): lax.ppermute(values, AXES, [(index, index ^ mask) for index in range(size)])  81.3 us
    ppermute x74, waiting for transfers between devices, exchange(): lax.ppermute(values, AXES, [(index, index ^ mask) for index in range(size)])  57 us
    all_to_all x4, starting transfers between devices, swap_total(): return jnp.sum(lax.all_to_all(copies, AXES, 0, 0, tiled=True), 0)  16.5 us
    all_to_all x4, waiting for transfers between devices, swap_total(): return jnp.sum(lax.all_to_all(copies, AXES, 0, 0, tiled=True), 0)  12.6 us
    unnamed x97, local copies, waits for them, and re-layouts  11.6 us
  transfers between devices with their start and end apart: 84, of which 27 were waited for; matrix products, arithmetic and copies ran while one was open for 8% of the time, Pallas kernels for 42%

commit v1 on v0

--- a/solution.py
+++ b/solution.py
@@ -106,6 +106,25 @@
 
     def take_core(self, came):
         self.arrays = (self.eight, self.other) + tuple(came)
+
+
+class HalvedGather(Gather):
+    def take_second(self, came):
+        self.parts = [self.four, came[0]]
+        self.far = [None, None]
+        self.arrays = [None] * 8
+
+    def third_of(self, part):
+        return [(self.parts[part], 2)]
+
+    def take_third_of(self, part, came):
+        self.far[part] = came[0]
+
+    def core_of(self, part):
+        return [(self.parts[part], 1), (self.far[part], 1)]
+
+    def take_core_of(self, part, came):
+        self.arrays[part::2] = [self.parts[part], self.far[part], came[0], came[1]]
 
 
 class Sum:
@@ -180,7 +199,8 @@
     classes = classes.reshape(32, 2, CLASS_ROWS, TILE).swapaxes(1, 2).reshape(32, CLASS_ROWS, B)
     late = jnp.concatenate([restore, classes], axis=1)
     pair = jnp.concatenate([reduce, expand], axis=1)
-    return as_blocks(squeeze), as_blocks(pair), as_blocks(spatial), late
+    spatial = [part for array in as_blocks(spatial) for part in (array[:4], array[4:])]
+    return as_blocks(squeeze), as_blocks(pair), spatial, late
 
 
 def reduced(buffer, reduce_half, expand_half, squeeze_half):
@@ -212,6 +232,7 @@
 HALF = 2 * PER_VIEW
 PADDED = SIDE + 2
 MIB = 1 << 20
+VMEM = 60
 LANES = 128
 TILE = 256
 
@@ -281,24 +302,13 @@
 GROUPS = C // WIDE
 
 
-def group_spec():
-    return pl.BlockSpec((HALF, WIDE), lambda half, group: (half, group))
-
-
-def row_spec(rows):
-    return pl.BlockSpec((rows, WIDE), lambda half, group: (0, group))
-
-
-def view_spec(rows):
-    return pl.BlockSpec((1, rows, WIDE), lambda half, group: (half, 0, group))
-
-
-def first_group():
-    return pl.program_id(1) == 0
-
-
-def last_group():
-    return pl.program_id(1) == GROUPS - 1
+def group_at(group):
+    return slice(group * WIDE, (group + 1) * WIDE)
+
+
+def chunks():
+    for chunk in range(HALF // 16):
+        yield chunk, slice(chunk * 16, chunk * 16 + 16)
 
 
 ANY = pl.BlockSpec(memory_space=pl.ANY)
@@ -306,7 +316,7 @@
 
 
 def kernel_call(kernel, steps, in_specs, out_specs, out_shapes, scratch, flops,
-                transcendentals=0, after=(), vmem=60, aliases=None):
+                transcendentals=0, after=(), vmem=VMEM, aliases=None):
     known = len(in_specs)
     grid = steps if isinstance(steps, tuple) else (steps,)
 
@@ -333,10 +343,15 @@
 
 def block_copies(me, sources, target, semaphores, rows=None, lanes_at=None, target_rows=None):
     copies = []
-    for low_mask, source in zip((0, 2, 1, 3), sources):
+    split = len(sources) // 4
+    for which, low_mask in enumerate((0, 2, 1, 3)):
         for entry in range(8):
             mask = low_mask | ((entry // 4) * 4) | ((entry % 4) << 3)
-            taken, place = source.at[entry], target.at[me ^ mask]
+            if split == 1:
+                taken = sources[which].at[entry]
+            else:
+                taken = sources[2 * which + entry // 4].at[entry % 4]
+            place = target.at[me ^ mask]
             if rows is not None:
                 taken = taken.at[rows] if lanes_at is None else taken.at[rows, lanes_at]
             if target_rows is not None:
@@ -405,10 +420,6 @@
 
 def first_step():
     return pl.program_id(0) == 0
-
-
-def very_first():
-    return (pl.program_id(0) == 0) & (pl.program_id(1) == 0)
 
 
 def add_moments(sums_ref, where, first, second):
@@ -492,67 +503,53 @@
 def gate_kernel(
     me_ref, block_a, block_b, block_c, block_d, tokens_ref, mixed_ref,
     logit_ref, gated_ref, pre_ref, sums_ref,
-    tile, found, expand_ref, reduce_ref, expand_semaphores, reduce_semaphores,
+    tile, expand_ref, reduce_ref, expand_semaphores, reduce_semaphores,
 ):
     blocks = (block_a, block_b, block_c, block_d)
     for_expand = expand_copies(me_ref[0], blocks, expand_ref, expand_semaphores)
     for_reduce = reduce_copies(me_ref[0], blocks, reduce_ref, reduce_semaphores)
-    group = pl.program_id(1)
-
-    @pl.when(very_first())
+
+    @pl.when(first_step())
     def _():
         start(for_expand)
         start(for_reduce)
         sums_ref[...] = jnp.zeros_like(sums_ref)
         wait(for_expand)
-
-    for part in range(2):
-        columns = expand_ref[pl.ds(8 * group + 4 * part, 4)].reshape(R, TILE)
-        tile[:, part * TILE : (part + 1) * TILE] = product(mixed_ref[...], columns)
-    for chunk in range(HALF // 16):
-        rows = slice(chunk * 16, chunk * 16 + 16)
-        logit = tile[rows]
-        token = tokens_ref[rows].astype(f32)
-        logit_ref[rows] = logit.astype(bf16)
-        gated_ref[rows] = (token + token * sigmoid(logit)).astype(bf16)
-
-    @pl.when(very_first())
-    def _():
         wait(for_reduce)
 
-    part = product(gated_ref[...], reduce_ref[pl.ds(8 * group, 8)].reshape(WIDE, B))
-
-    @pl.when(first_group())
-    def _():
-        found[...] = part
-
-    @pl.when(group > 0)
-    def _():
-        found[...] += part
-
-    @pl.when(last_group())
-    def _():
-        first = jnp.zeros((8, B), f32)
-        second = jnp.zeros((8, B), f32)
-        for chunk in range(HALF // 16):
-            rows = slice(chunk * 16, chunk * 16 + 16)
-            value = found[rows]
-            pre_ref[rows] = value
-            first = first + fold(value)
-            second = second + fold(value * value)
-        add_moments(sums_ref, slice(0, B), first, second)
+    for group in range(GROUPS):
+        where, found = group_at(group), tile.at[group % 2]
+        columns = [
+            expand_ref[top : top + 4].reshape(R, TILE) for top in (8 * group, 8 * group + 4)
+        ]
+        found[...] = product(mixed_ref[...], jnp.concatenate(columns, axis=1))
+        for _, rows in chunks():
+            logit = found[rows]
+            token = tokens_ref[rows, where].astype(f32)
+            logit_ref[rows, where] = logit.astype(bf16)
+            gated_ref[rows, where] = (token + token * sigmoid(logit)).astype(bf16)
+    found = tile.at[0]
+    found[...] = product(gated_ref[...], reduce_ref[...].reshape(C, B))
+    first = jnp.zeros((8, B), f32)
+    second = jnp.zeros((8, B), f32)
+    for _, rows in chunks():
+        value = found[rows]
+        pre_ref[rows] = value
+        first = first + fold(value)
+        second = second + fold(value * value)
+    add_moments(sums_ref, slice(0, B), first, second)
 
 
 def gate_block(me, pair, tokens, mixed):
     rows = tokens.shape[0]
     return kernel_call(
         gate_kernel,
-        (rows // HALF, GROUPS),
-        [SCALAR] + [ANY] * 4 + [group_spec(), half_spec(R)],
-        [group_spec(), group_spec(), half_spec(B), whole_out((2, B))],
+        rows // HALF,
+        [SCALAR] + [ANY] * 4 + [half_spec(C), half_spec(R)],
+        [half_spec(C), half_spec(C), half_spec(B), whole_out((2, B))],
         [jax.ShapeDtypeStruct((rows, C), bf16), jax.ShapeDtypeStruct((rows, C), bf16),
          jax.ShapeDtypeStruct((rows, B), f32), jax.ShapeDtypeStruct((2, B), f32)],
-        [pltpu.VMEM((HALF, WIDE), f32), pltpu.VMEM((HALF, B), f32),
+        [pltpu.VMEM((2, HALF, WIDE), f32),
          pltpu.VMEM((32, R // 4, TILE), bf16), pltpu.VMEM((32, C // 32, B), bf16),
          pltpu.SemaphoreType.DMA((2, 32)), pltpu.SemaphoreType.DMA((32,))],
         4 * rows * C * R,
@@ -570,10 +567,11 @@
     return pltpu.make_async_copy(late_ref.at[:, 0:RESTORE_ROWS], target, semaphore)
 
 
-def second_kernel(count, me_ref, block_a, block_b, block_c, block_d,
-                  pre_ref, in_sums_ref, affine_ref,
-                  hidden_ref, out_ref, sums_ref, natural, padded, tile, spatial_ref, semaphores):
-    copies = block_copies(me_ref[0], (block_a, block_b, block_c, block_d), spatial_ref, semaphores)
+def second_kernel(count, me_ref, *refs):
+    blocks, refs = refs[:8], refs[8:]
+    pre_ref, in_sums_ref, affine_ref, hidden_ref, out_ref, sums_ref, *refs = refs
+    natural, padded, tile, spatial_ref, semaphores = refs
+    copies = block_copies(me_ref[0], blocks, spatial_ref, semaphores)
 
     @pl.when(first_step())
     def _():
@@ -610,31 +608,26 @@
     def _():
         wait(copies)
 
-    def product_step(step, carry):
-        where = lanes(step, TILE)
-        found = None
-        for row in range(3):
-            taps = [
-                spatial_ref[:, tap * 16 : tap * 16 + 16, where].reshape(B, TILE)
-                for tap in range(3 * row, 3 * row + 3)
-            ]
-            part = product(
-                hidden_ref[0, row * border : row * border + HALF], jnp.concatenate(taps, axis=0)
-            )
-            found = part if found is None else found + part
-        tile[...] = found
-        first = jnp.zeros((8, TILE), f32)
-        second = jnp.zeros((8, TILE), f32)
-        for chunk in range(HALF // 16):
-            rows = slice(chunk * 16, chunk * 16 + 16)
-            value = tile[rows]
-            out_ref[rows, where] = value
-            first = first + fold(value)
-            second = second + fold(value * value)
-        add_moments(sums_ref, where, first, second)
-        return carry
-
-    lax.fori_loop(0, B // TILE, product_step, 0)
+    found = None
+    for row in range(3):
+        taps = [
+            spatial_ref[:, tap * 16 : tap * 16 + 16].reshape(B, B)
+            for tap in range(3 * row, 3 * row + 3)
+        ]
+        part = product(
+            hidden_ref[0, row * border : row * border + HALF], jnp.concatenate(taps, axis=0)
+        )
+        found = part if found is None else found + part
+    tile[...] = found
+    first = jnp.zeros((8, B), f32)
+    second = jnp.zeros((8, B), f32)
+    for chunk in range(HALF // 16):
+        rows = slice(chunk * 16, chunk * 16 + 16)
+        value = tile[rows]
+        out_ref[rows] = value
+        first = first + fold(value)
+        second = second + fold(value * value)
+    add_moments(sums_ref, slice(0, B), first, second)
 
 
 def second_block(me, spatial, pre_one, sums, affine, count):
@@ -644,13 +637,13 @@
     return kernel_call(
         functools.partial(second_kernel, count),
         steps,
-        [SCALAR, ANY, ANY, ANY, ANY, half_spec(B), whole_spec(sums.shape), whole_spec((2, B))],
+        [SCALAR] + [ANY] * 8 + [half_spec(B), whole_spec(sums.shape), whole_spec((2, B))],
         [pl.BlockSpec((1, deep, 3 * B), lambda step: (step, 0, 0)), half_spec(B),
          whole_out((2, B))],
         [jax.ShapeDtypeStruct((steps, deep, 3 * B), bf16), jax.ShapeDtypeStruct((rows, B), f32),
          jax.ShapeDtypeStruct((2, B), f32)],
         [pltpu.VMEM((HALF, LANES), f32), pltpu.VMEM((PADDED * PADDED, 16, LANES), bf16),
-         pltpu.VMEM((HALF, TILE), f32), pltpu.VMEM((32, SPATIAL_ROWS, B), bf16),
+         pltpu.VMEM((HALF, B), f32), pltpu.VMEM((32, SPATIAL_ROWS, B), bf16),
          pltpu.SemaphoreType.DMA((32,))],
         18 * rows * B * B,
         2 * rows * B,
@@ -658,59 +651,63 @@
 
 
 def third_kernel(count, pre_ref, in_sums_ref, affine_ref, late_ref,
-                 hidden_ref, out_ref, sums_ref, natural, tile, restore_ref, semaphore):
+                 hidden_ref, out_ref, centre_ref, sums_ref, natural, tile, middle, restore_ref,
+                 semaphore):
     copy = restore_copy(late_ref, restore_ref, semaphore)
-    group = pl.program_id(1)
-
-    @pl.when(very_first())
+
+    @pl.when(first_step())
     def _():
         copy.start()
         sums_ref[...] = jnp.zeros_like(sums_ref)
 
-    @pl.when(first_group())
-    def _():
-        def hidden_step(step, carry):
-            where = lanes(step, LANES)
-            mean, inverse, gain, shift = (
-                spread(row)
-                for row in constants(in_sums_ref[:, where], affine_ref[:, where], count)
-            )
-            for cell in range(CELLS):
-                rows = slice(cell * 16, cell * 16 + 16)
-                norm = (pre_ref[rows, where] - mean) * inverse * gain + shift
-                natural[pl.ds(cell, 16, stride=CELLS)] = norm * sigmoid(norm)
-            hidden_ref[:, where] = natural[...].astype(bf16)
-            return carry
-
-        lax.fori_loop(0, 4, hidden_step, 0)
-
-    @pl.when(very_first())
+    def hidden_step(step, carry):
+        where = lanes(step, LANES)
+        mean, inverse, gain, shift = (
+            spread(row) for row in constants(in_sums_ref[:, where], affine_ref[:, where], count)
+        )
+        for cell in range(CELLS):
+            rows = slice(cell * 16, cell * 16 + 16)
+            norm = (pre_ref[rows, where] - mean) * inverse * gain + shift
+            natural[pl.ds(cell, 16, stride=CELLS)] = norm * sigmoid(norm)
+        hidden_ref[:, where] = natural[...].astype(bf16)
+        middle[:, where] = spread(jnp.mean(natural[...], 0, keepdims=True)).astype(bf16)
+        return carry
+
+    lax.fori_loop(0, 4, hidden_step, 0)
+
+    @pl.when(first_step())
     def _():
         copy.wait()
 
-    columns = restore_ref.reshape(8, 4, RESTORE_ROWS, B)[:, group].reshape(B, WIDE)
-    tile[...] = product(hidden_ref[...], columns)
-    first = jnp.zeros((8, WIDE), f32)
-    second = jnp.zeros((8, WIDE), f32)
-    for chunk in range(HALF // 16):
-        rows = slice(chunk * 16, chunk * 16 + 16)
-        value = tile[rows]
-        out_ref[rows] = value.astype(bf16)
-        first = first + fold(value)
-        second = second + fold(value * value)
-    add_moments(sums_ref, lanes(group, WIDE), first, second)
+    blocks = restore_ref.reshape(8, 4, RESTORE_ROWS, B)
+    for group in range(GROUPS):
+        where, found = group_at(group), tile.at[group % 2]
+        columns = blocks[:, group].reshape(B, WIDE)
+        found[...] = product(hidden_ref[...], columns)
+        centre = product(middle[...], columns)
+        centre_ref[0, :, where] = centre[0:1]
+        first = jnp.zeros((8, WIDE), f32)
+        second = jnp.zeros((8, WIDE), f32)
+        for _, rows in chunks():
+            value = found[rows]
+            out_ref[rows, where] = (value - centre).astype(bf16)
+            first = first + fold(value)
+            second = second + fold(value * value)
+        add_moments(sums_ref, where, first, second)
 
 
 def third_block(pre_two, sums, affine, late, count):
     rows = pre_two.shape[0]
     return kernel_call(
         functools.partial(third_kernel, count),
-        (rows // HALF, GROUPS),
+        rows // HALF,
         [half_spec(B), whole_spec(sums.shape), whole_spec((2, B)), ANY],
-        [half_spec(B), group_spec(), whole_out((2, C))],
+        [half_spec(B), half_spec(C), pl.BlockSpec((1, 1, C), lambda step: (step, 0, 0)),
+         whole_out((2, C))],
         [jax.ShapeDtypeStruct((rows, B), bf16), jax.ShapeDtypeStruct((rows, C), bf16),
-         jax.ShapeDtypeStruct((2, C), f32)],
-        [pltpu.VMEM((HALF, LANES), f32), pltpu.VMEM((HALF, WIDE), f32),
+         jax.ShapeDtypeStruct((rows // HALF, 1, C), f32), jax.ShapeDtypeStruct((2, C), f32)],
+        [pltpu.VMEM((HALF, LANES), f32), pltpu.VMEM((2, HALF, WIDE), f32),
+         pltpu.VMEM((16, B), bf16),
          pltpu.VMEM((32, RESTORE_ROWS, B), bf16), pltpu.SemaphoreType.DMA(())],
         2 * rows * B * C,
         2 * rows * B,
@@ -721,13 +718,34 @@
     return (chunk * 16) // PER_VIEW, (chunk * 16 + 8) // PER_VIEW
 
 
-def fourth_kernel(count, pre_ref, gated_ref, in_sums_ref, affine_ref,
-                  out_ref, slope_ref, views_ref):
-    for part in range(WIDE // TILE):
+def class_copy(late_ref, target, semaphore):
+    return pltpu.make_async_copy(late_ref.at[:, RESTORE_ROWS:], target, semaphore)
+
+
+def order_classes(late, classes):
+    for block in range(32):
+        for half in range(2):
+            top = (2 * block + half) * CLASS_ROWS
+            classes[top : top + CLASS_ROWS] = late[block, :, half * TILE : (half + 1) * TILE]
+
+
+def fourth_kernel(count, pre_ref, centre_ref, gated_ref, in_sums_ref, affine_ref,
+                  late_ref, bias_ref, out_ref, slope_ref, views_ref, logits_ref, pooled_ref,
+                  classes, late, sums, semaphore):
+    copy = class_copy(late_ref, late, semaphore)
+    step = pl.program_id(0)
+
+    @pl.when(first_step())
+    def _():
+        copy.start()
+        sums[...] = jnp.zeros_like(sums)
+
+    for part in range(C // TILE):
         where = slice(part * TILE, (part + 1) * TILE)
         mean, inverse, gain, shift = (
             spread(row) for row in constants(in_sums_ref[:, where], affine_ref[:, where], count)
         )
+        mean = mean - spread(centre_ref[0, :, where])
         totals = [[jnp.zeros((8, TILE), f32) for _ in range(2)] for _ in range(3)]
         for chunk in range(HALF // 16):
             rows = slice(chunk * 16, chunk * 16 + 16)
@@ -748,24 +766,92 @@
         for kind in range(3):
             for view in range(2):
                 at = 2 * kind + view
-                views_ref[0, at : at + 1, where] = jnp.sum(totals[kind][view], 0, keepdims=True)
+                row = jnp.sum(totals[kind][view], 0, keepdims=True)
+                views_ref[0, at : at + 1, where] = row
+                if kind == 0:
+                    sums[pl.ds(2 * step + view, 1), where] = row
         views_ref[0, 6:8, where] = jnp.zeros((2, TILE), f32)
 
-
-def fourth_block(pre_three, gated, sums, affine, count):
+    @pl.when(step == pl.num_programs(0) - 1)
+    def _():
+        copy.wait()
+        order_classes(late, classes)
+        pooled = (sums[...] / PER_VIEW).astype(bf16)
+        pooled_ref[...] = pooled
+        logits_ref[...] = product(pooled, classes[...]) + bias_ref[...]
+
+
+def fourth_block(pre_three, centres, gated, sums, affine, late, bias, count):
     rows = pre_three.shape[0]
     steps = rows // HALF
     return kernel_call(
         functools.partial(fourth_kernel, count),
-        (steps, GROUPS),
-        [group_spec(), group_spec(), row_spec(sums.shape[0]), row_spec(2)],
-        [group_spec(), group_spec(), view_spec(8)],
+        steps,
+        [half_spec(C), pl.BlockSpec((1, 1, C), lambda step: (step, 0, 0)), half_spec(C),
+         whole_spec(sums.shape), whole_spec((2, C)), ANY, whole_spec((1, TILE))],
+        [half_spec(C), half_spec(C), pl.BlockSpec((1, 8, C), lambda step: (step, 0, 0)),
+         whole_out((16, TILE)), whole_out((16, C))],
         [jax.ShapeDtypeStruct((rows, C), bf16), jax.ShapeDtypeStruct((rows, C), bf16),
-         jax.ShapeDtypeStruct((steps, 8, C), f32)],
-        [],
+         jax.ShapeDtypeStruct((steps, 8, C), f32), jax.ShapeDtypeStruct((16, TILE), f32),
+         jax.ShapeDtypeStruct((16, C), bf16)],
+        [pltpu.VMEM((C, TILE), bf16), pltpu.VMEM((32, CLASS_ROWS, B), bf16),
+         pltpu.VMEM((16, C), f32), pltpu.SemaphoreType.DMA(())],
         20 * rows * C,
         2 * rows * C,
-    )(pre_three, gated, sums, affine)
+    )(pre_three, centres, gated, sums, affine, late, bias)
+
+
+def video_kernel(view_count, before_ref, own_ref, after_ref, marks_ref, target_ref, views_ref,
+                 late_ref, part_ref, pooled_ref, grad_ref, classes, late, semaphore):
+    copy = class_copy(late_ref, late, semaphore)
+    copy.start()
+    marks = marks_ref[...]
+    video_logits = jnp.zeros((8, TILE), f32)
+    near = (before_ref, own_ref, after_ref)
+    for index in range(3 * view_count):
+        row = near[index // view_count][index % view_count : index % view_count + 1]
+        video_logits = video_logits + marks[:, index : index + 1] * row
+    known = lax.broadcasted_iota(jnp.int32, (8, TILE), 1) < CLASSES
+    top = jnp.max(jnp.where(known, video_logits, -jnp.inf), 1, keepdims=True)
+    weights = jnp.where(known, jnp.exp(jnp.minimum(video_logits - top, 0.0)), 0.0)
+    total_weight = jnp.sum(weights, 1, keepdims=True)
+    target = target_ref[...]
+    entropy = jnp.log(total_weight) + top - jnp.sum(target * video_logits, 1, keepdims=True)
+    video_grad = loss_scale * (weights / total_weight - target)
+    first = marks[:, 3 * view_count + 1 : 3 * view_count + 2]
+    view_grad = (video_grad * marks[:, 3 * view_count : 3 * view_count + 1]).astype(bf16)
+    grad_ref[...] = view_grad
+    place = lax.broadcasted_iota(jnp.int32, (8, TILE), 1)
+    row = jnp.sum(first * jnp.where(place == CLASSES, entropy, video_grad), 0, keepdims=True)
+    copy.wait()
+    order_classes(late, classes)
+    pooled = dot_nt(view_grad, classes[...]) * (1.0 / PER_VIEW)
+    parts = [jnp.zeros((1, C), f32), jnp.zeros((1, C), f32)]
+    for view in range(view_count):
+        half, place = view // 2, view % 2
+        pooled_ref[half, place : place + 1] = pooled[view : view + 1]
+        for kind in range(2):
+            at = 2 * (kind + 1) + place
+            parts[kind] = parts[kind] + pooled[view : view + 1] * views_ref[half, at : at + 1]
+    part_ref[0:1] = parts[0]
+    part_ref[1:2] = parts[1]
+    part_ref[2:3] = jnp.zeros((1, C), f32)
+    part_ref[2:3, 0:TILE] = row
+
+
+def video_block(before, own, following, marks, target, views, late, view_count):
+    outs = [((3, C), f32), ((view_count // 2, 2, C), f32), ((8, TILE), bf16)]
+    operands = (before, own, following, marks, target, views)
+    return kernel_call(
+        functools.partial(video_kernel, view_count),
+        1,
+        [whole_spec(operand.shape) for operand in operands] + [ANY],
+        [whole_out(shape) for shape, _ in outs],
+        [jax.ShapeDtypeStruct(shape, kind) for shape, kind in outs],
+        [pltpu.VMEM((C, TILE), bf16), pltpu.VMEM((32, CLASS_ROWS, B), bf16),
+         pltpu.SemaphoreType.DMA(())],
+        1000000,
+    )(*operands, late)
 
 
 def view_scale(pooled_ref, view, where):
@@ -777,7 +863,7 @@
     return slope * jnp.concatenate([pooled[low], pooled[high]], axis=0)
 
 
-def fifth_kernel(count, slope_ref, pre_three_ref, pooled_ref, sums_three_ref, affine_three_ref,
+def fifth_kernel(count, slope_ref, pre_three_ref, centre_ref, pooled_ref, sums_three_ref, affine_three_ref,
                  grads_three_ref, late_ref, pre_two_ref, sums_two_ref, affine_two_ref,
                  low_ref, out_ref, sums_ref, natural, restore_ref, semaphore):
     copy = restore_copy(late_ref, restore_ref, semaphore)
@@ -787,42 +873,32 @@
         copy.start()
         sums_ref[...] = jnp.zeros_like(sums_ref)
 
-    def low_step(step, carry):
-        where = lanes(step, TILE)
+    for group in range(GROUPS):
+        where = group_at(group)
         mean, inverse, gain, _ = constants(
             sums_three_ref[:, where], affine_three_ref[:, where], count
         )
         scale = spread(gain * inverse)
         offset = spread(grads_three_ref[0:1, where] / count)
         along = spread(grads_three_ref[1:2, where] / count * inverse)
-        mean = spread(mean)
+        mean = spread(mean - centre_ref[0, :, where])
         pooled = [view_scale(pooled_ref, view, where) for view in range(2)]
-        for chunk in range(HALF // 16):
-            rows = slice(chunk * 16, chunk * 16 + 16)
+        for chunk, rows in chunks():
             grad = view_grad_rows(slope_ref[rows, where].astype(f32), pooled, chunk)
             centred = pre_three_ref[rows, where].astype(f32) - mean
             low_ref[rows, where] = (scale * (grad - offset - centred * along)).astype(bf16)
-        return carry
-
-    lax.fori_loop(0, C // TILE, low_step, 0)
 
     @pl.when(first_step())
     def _():
         copy.wait()
 
     blocks = restore_ref.reshape(8, 4, RESTORE_ROWS, B)
-
-    def product_step(step, carry):
-        grad = None
-        for quarter in range(4):
-            rows = blocks[pl.ds(4 * step, 4), quarter].reshape(TILE, B)
-            part = dot_nt(low_ref[:, quarter * B : (quarter + 1) * B], rows)
-            grad = part if grad is None else grad + part
-        natural[2 * step] = grad[:, 0:LANES]
-        natural[2 * step + 1] = grad[:, LANES:TILE]
-        return carry
-
-    lax.fori_loop(0, B // TILE, product_step, 0)
+    grad = None
+    for group in range(GROUPS):
+        part = dot_nt(low_ref[:, group_at(group)], blocks[:, group].reshape(B, WIDE))
+        grad = part if grad is None else grad + part
+    for step in range(4):
+        natural[step] = grad[:, step * LANES : (step + 1) * LANES]
 
     def slope_step(step, carry):
         where = lanes(step, LANES)
@@ -847,13 +923,14 @@
     lax.fori_loop(0, 4, slope_step, 0)
 
 
-def fifth_block(slope, pre_three, pooled, sums_three, affine_three, grads_three, late,
+def fifth_block(slope, pre_three, centres, pooled, sums_three, affine_three, grads_three, late,
                 pre_two, sums_two, affine_two, count, after=()):
     rows = slope.shape[0]
     return kernel_call(
         functools.partial(fifth_kernel, count),
         rows // HALF,
-        [half_spec(C), half_spec(C), pl.BlockSpec((1, 2, C), lambda step: (step, 0, 0)),
+        [half_spec(C), half_spec(C), pl.BlockSpec((1, 1, C), lambda step: (step, 0, 0)),
+         pl.BlockSpec((1, 2, C), lambda step: (step, 0, 0)),
          whole_spec(sums_three.shape), whole_spec((2, C)), whole_spec(grads_three.shape), ANY,
          half_spec(B), whole_spec(sums_two.shape), whole_spec((2, B))],
         [half_spec(C), half_spec(B), whole_out((2, B))],
@@ -864,16 +941,17 @@
         2 * rows * B * C,
         2 * rows * B,
         after=after,
-    )(slope, pre_three, pooled, sums_three, affine_three, grads_three, late,
+    )(slope, pre_three, centres, pooled, sums_three, affine_three, grads_three, late,
       pre_two, sums_two, affine_two)
 
 
-def sixth_kernel(count, me_ref, block_a, block_b, block_c, block_d, grad_ref, pre_two_ref, sums_two_ref, affine_two_ref, grads_two_ref,
-                 pre_one_ref, sums_one_ref, affine_one_ref,
-                 low_ref, out_ref, sums_ref, padded, shifted, tile, natural, spatial_ref,
-                 semaphores):
+def sixth_kernel(count, me_ref, *refs):
+    blocks, refs = refs[:8], refs[8:]
+    grad_ref, pre_two_ref, sums_two_ref, affine_two_ref, grads_two_ref, *refs = refs
+    pre_one_ref, sums_one_ref, affine_one_ref, low_ref, out_ref, sums_ref, *refs = refs
+    padded, shifted, tile, natural, spatial_ref, semaphores = refs
     border = SIDE * 16
-    copies = block_copies(me_ref[0], (block_a, block_b, block_c, block_d), spatial_ref, semaphores)
+    copies = block_copies(me_ref[0], blocks, spatial_ref, semaphores)
 
     @pl.when(first_step())
     def _():
@@ -910,24 +988,22 @@
     def _():
         wait(copies)
 
-    def product_step(step, carry):
-        grad = None
-        for tap in range(9):
-            top = (tap // 3) * border
-            at = (tap % 3) * B
-            back = (8 - tap) * 16
-            rows = spatial_ref[pl.ds(16 * step, 16), back : back + 16].reshape(TILE, B)
-            part = dot_nt(shifted[top : top + HALF, at : at + B], rows)
-            grad = part if grad is None else grad + part
-        tile[...] = grad
-        for half in range(2):
-            for cell in range(CELLS):
-                natural[2 * step + half, pl.ds(cell, 16, stride=CELLS)] = tile[
-                    cell * 16 : cell * 16 + 16, half * LANES : (half + 1) * LANES
-                ]
-        return carry
-
-    lax.fori_loop(0, B // TILE, product_step, 0)
+    grad = None
+    for tap in range(9):
+        top = (tap // 3) * border
+        at = (tap % 3) * B
+        back = (8 - tap) * 16
+        part = dot_nt(
+            shifted[top : top + HALF, at : at + B],
+            spatial_ref[:, back : back + 16].reshape(B, B),
+        )
+        grad = part if grad is None else grad + part
+    tile[...] = grad
+    for group in range(4):
+        for cell in range(CELLS):
+            natural[group, pl.ds(cell, 16, stride=CELLS)] = tile[
+                cell * 16 : cell * 16 + 16, group * LANES : (group + 1) * LANES
+            ]
 
     def slope_step(step, carry):
         where = lanes(step, LANES)
@@ -958,14 +1034,14 @@
     return kernel_call(
         functools.partial(sixth_kernel, count),
         rows // HALF,
-        [SCALAR, ANY, ANY, ANY, ANY, half_spec(B), half_spec(B), whole_spec(sums_two.shape),
+        [SCALAR] + [ANY] * 8 + [half_spec(B), half_spec(B), whole_spec(sums_two.shape),
          whole_spec((2, B)), whole_spec(grads_two.shape), half_spec(B), whole_spec(sums_one.shape),
          whole_spec((2, B))],
         [half_spec(B), half_spec(B), whole_out((2, B))],
         [jax.ShapeDtypeStruct((rows, B), bf16), jax.ShapeDtypeStruct((rows, B), f32),
          jax.ShapeDtypeStruct((2, B), f32)],
         [pltpu.VMEM((PADDED * PADDED, 16, LANES), bf16), pltpu.VMEM((deep, 3 * B), bf16),
-         pltpu.VMEM((HALF, TILE), f32), pltpu.VMEM((4, HALF, LANES), f32),
+         pltpu.VMEM((HALF, B), f32), pltpu.VMEM((4, HALF, LANES), f32),
          pltpu.VMEM((32, SPATIAL_ROWS, B), bf16), pltpu.SemaphoreType.DMA((32,))],
         18 * rows * B * B,
         2 * rows * B,
@@ -992,52 +1068,75 @@
     lax.fori_loop(0, 4, low_step, 0)
 
 
-def low_block(grad, pre, sums, affine, grads, count):
-    return kernel_call(
-        functools.partial(low_kernel, count),
-        grad.shape[0] // HALF,
-        [half_spec(B), half_spec(B), whole_spec(sums.shape), whole_spec((2, B)),
-         whole_spec(grads.shape)],
-        half_spec(B),
-        jax.ShapeDtypeStruct(grad.shape, bf16),
-        [],
-        100 * grad.size,
-    )(grad, pre, sums, affine, grads)
+def low_outer_kernel(count, grain, me_ref, grad_ref, pre_ref, sums_ref, affine_ref, grads_ref,
+                     wide_ref, low_ref, keep_ref, send_ref, plain, turned):
+    @pl.when(first_step())
+    def _():
+        for half in range(low_ref.shape[0] // HALF):
+            rows = pl.ds(half * HALF, HALF)
+            low_kernel(
+                count, grad_ref.at[rows], pre_ref.at[rows], sums_ref, affine_ref, grads_ref,
+                low_ref.at[rows],
+            )
+        turn(me_ref[0], low_ref[...], grain, plain, turned)
+
+    store_tiles(product(turned[...], wide_ref[...]), keep_ref, send_ref)
+
+
+def low_outer_block(me, grad, pre, sums, affine, grads, wide_values, count):
+    rows, inner = grad.shape
+    blocks = wide_values.shape[1] // TILE
+    half = pl.BlockSpec((2, inner // 2, TILE), lambda step: (step, 0, 0))
+    low, keep, send = kernel_call(
+        functools.partial(low_outer_kernel, count, inner // 4),
+        blocks // 2,
+        [SCALAR, whole_spec(grad.shape), whole_spec(grad.shape), whole_spec(sums.shape),
+         whole_spec((2, B)), whole_spec(grads.shape),
+         pl.BlockSpec((rows, 2 * TILE), lambda step: (0, step))],
+        [whole_out(grad.shape), half, half],
+        [jax.ShapeDtypeStruct(grad.shape, bf16),
+         jax.ShapeDtypeStruct((blocks, inner // 2, TILE), f32),
+         jax.ShapeDtypeStruct((blocks, inner // 2, TILE), bf16)],
+        [pltpu.VMEM((inner, rows), bf16), pltpu.VMEM((inner, rows), bf16)],
+        2 * rows * inner * wide_values.shape[1],
+    )(me, grad, pre, sums, affine, grads, wide_values)
+    return low, (keep, send)
 
 
 def gate_back_kernel(me_ref, block_a, block_b, block_c, block_d, low_ref,
                      slope_ref, pooled_ref, tokens_ref, logit_ref,
                      logit_grad_ref, part_ref, tile, reduce_ref, semaphores):
     copies = reduce_copies(me_ref[0], (block_a, block_b, block_c, block_d), reduce_ref, semaphores)
-    group = pl.program_id(1)
-
-    @pl.when(very_first())
+
+    @pl.when(first_step())
     def _():
         start(copies)
         wait(copies)
 
-    tile[...] = dot_nt(low_ref[...], reduce_ref[pl.ds(8 * group, 8)].reshape(WIDE, B))
-    pooled = [view_scale(pooled_ref, view, slice(0, WIDE)) for view in range(2)]
-    for chunk in range(HALF // 16):
-        rows = slice(chunk * 16, chunk * 16 + 16)
-        grad = tile[rows] + view_grad_rows(slope_ref[rows].astype(f32), pooled, chunk)
-        gate = sigmoid(logit_ref[rows].astype(f32))
-        token = tokens_ref[rows].astype(f32)
-        part = grad * gate
-        part_ref[rows] = (grad + part).astype(bf16)
-        logit_grad_ref[rows] = (part * (1.0 - gate) * token).astype(bf16)
+    for group in range(GROUPS):
+        where, found = group_at(group), tile.at[group % 2]
+        found[...] = dot_nt(low_ref[...], reduce_ref[8 * group : 8 * group + 8].reshape(WIDE, B))
+        pooled = [view_scale(pooled_ref, view, where) for view in range(2)]
+        for chunk, rows in chunks():
+            slope = slope_ref[rows, where].astype(f32)
+            grad = found[rows] + view_grad_rows(slope, pooled, chunk)
+            gate = sigmoid(logit_ref[rows, where].astype(f32))
+            part = grad * gate
+            part_ref[rows, where] = (grad + part).astype(bf16)
+            token = tokens_ref[rows, where].astype(f32)
+            logit_grad_ref[rows, where] = (part * (1.0 - gate) * token).astype(bf16)
 
 
 def gate_back_block(me, pair, low_one, slope, pooled, tokens, logit):
     rows = low_one.shape[0]
     return kernel_call(
         gate_back_kernel,
-        (rows // HALF, GROUPS),
-        [SCALAR, ANY, ANY, ANY, ANY, half_spec(B), group_spec(), view_spec(2),
-         group_spec(), group_spec()],
-        [group_spec(), group_spec()],
+        rows // HALF,
+        [SCALAR, ANY, ANY, ANY, ANY, half_spec(B), half_spec(C),
+         pl.BlockSpec((1, 2, C), lambda step: (step, 0, 0)), half_spec(C), half_spec(C)],
+        [half_spec(C), half_spec(C)],
         [jax.ShapeDtypeStruct((rows, C), bf16), jax.ShapeDtypeStruct((rows, C), bf16)],
-        [pltpu.VMEM((HALF, WIDE), f32), pltpu.VMEM((32, C // 32, B), bf16),
+        [pltpu.VMEM((2, HALF, WIDE), f32), pltpu.VMEM((32, C // 32, B), bf16),
          pltpu.SemaphoreType.DMA((32,))],
         2 * rows * C * R,
         2 * rows * C,
@@ -1059,20 +1158,15 @@
         later[0:CELLS] = jnp.zeros((CELLS, LANES), f32)
         wait(copies)
 
-    quarters = expand_ref.reshape(8, 4, R // 4, TILE)
-
-    def mixed_step(step, carry):
-        grad = None
-        for block in range(C // TILE):
-            at = slice(block * TILE, (block + 1) * TILE)
-            rows = quarters[block, pl.ds(2 * step, 2)].reshape(TILE, TILE)
-            part = dot_nt(logit_grad_ref[:, at], rows)
-            grad = part if grad is None else grad + part
-        natural[2 * step] = grad[:, 0:LANES]
-        natural[2 * step + 1] = grad[:, LANES:TILE]
-        return carry
-
-    lax.fori_loop(0, R // TILE, mixed_step, 0)
+    grad = None
+    for group in range(GROUPS):
+        columns = [
+            expand_ref[top : top + 4].reshape(R, TILE) for top in (8 * group, 8 * group + 4)
+        ]
+        part = dot_nt(logit_grad_ref[:, group_at(group)], jnp.concatenate(columns, axis=1))
+        grad = part if grad is None else grad + part
+    for step in range(4):
+        natural[step] = grad[:, step * LANES : (step + 1) * LANES]
     segment = lax.broadcasted_iota(jnp.int32, (16, LANES), 0) % SEG
     not_last = (segment != SEG - 1).astype(f32)
 
@@ -1142,8 +1236,8 @@
 
 
 def tokens_kernel(me_ref, block_a, block_b, block_c, block_d, part_ref, squeezed_ref, out_ref,
-                  tile, squeeze_ref, semaphores):
-    @pl.when(very_first())
+                  squeeze_ref, semaphores):
+    @pl.when(first_step())
     def _():
         copies = block_copies(
             me_ref[0], (block_a, block_b, block_c, block_d), squeeze_ref, semaphores, slice(0, 64)
@@ -1151,24 +1245,19 @@
         start(copies)
         wait(copies)
 
-    tile[...] = dot_nt(
-        squeezed_ref[...], squeeze_ref[pl.ds(8 * pl.program_id(1), 8)].reshape(WIDE, R)
-    )
-    for chunk in range(HALF // 16):
-        rows = slice(chunk * 16, chunk * 16 + 16)
-        out_ref[rows] = (tile[rows] + part_ref[rows].astype(f32)).astype(bf16)
+    found = dot_nt(squeezed_ref[...], squeeze_ref[...].reshape(C, R))
+    out_ref[...] = (found + part_ref[...].astype(f32)).astype(bf16)
 
 
 def tokens_block(me, squeeze, part, squeezed_grad):
     rows = part.shape[0]
     return kernel_call(
         tokens_kernel,
-        (rows // HALF, GROUPS),
-        [SCALAR, ANY, ANY, ANY, ANY, group_spec(), half_spec(R)],
-        group_spec(),
+        rows // HALF,
+        [SCALAR, ANY, ANY, ANY, ANY, half_spec(C), half_spec(R)],
+        half_spec(C),
         jax.ShapeDtypeStruct((rows, C), bf16),
-        [pltpu.VMEM((HALF, WIDE), f32), pltpu.VMEM((32, C // 32, R), bf16),
-         pltpu.SemaphoreType.DMA((32,))],
+        [pltpu.VMEM((32, C // 32, R), bf16), pltpu.SemaphoreType.DMA((32,))],
         2 * rows * C * R,
     )(me, *squeeze, part, squeezed_grad)
 
@@ -1350,14 +1439,18 @@
     return found.reshape(-1, INPUT_LANES)
 
 
-def band_select():
-    shape = (STEM_SIDE // 2, CHANNELS, 2 * STEM_SIDE, 2, LANES)
+def band_select(turned=False):
+    shape = [STEM_SIDE // 2, CHANNELS, 2 * STEM_SIDE, 2, LANES]
+    axes = [0, 1, 2, 3, 4]
+    if turned:
+        shape, axes = [shape[axis] for axis in (0, 3, 4, 1, 2)], [0, 3, 4, 1, 2]
     pair, channel, place, which, entry = (
-        lax.broadcasted_iota(jnp.int32, shape, axis) for axis in range(5)
+        lax.broadcasted_iota(jnp.int32, shape, axis) for axis in axes
     )
     met = (entry % CHANNELS == channel) & (entry < WINDOW * CHANNELS)
     met = met & (place == 2 * (2 * pair + which) + entry // CHANNELS - 3)
-    return met.astype(bf16).reshape(STEM_SIDE // 2, INPUT_LANES, 2 * LANES)
+    ends = (2 * LANES, INPUT_LANES) if turned else (INPUT_LANES, 2 * LANES)
+    return met.astype(bf16).reshape((STEM_SIDE // 2,) + ends)
 
 
 def pair_weights(stem_weight):
@@ -1369,23 +1462,25 @@
     )
 
 
+PAIRS = STEM_SIDE // 2
+
+
 def stem_kernel(input_ref, select_ref, weights_ref, pre_ref, sums_ref, bands):
-    def step_body(step, carry):
-        where = lanes(step, TILE)
-        for offset in range(WINDOW):
-            for which in range(2):
-                band = product(select_ref[2 * step + which], weights_ref[offset])
-                bands[offset, :, which * LANES : (which + 1) * LANES] = band.astype(bf16)
-        found = None
-        for offset in range(WINDOW):
-            part = product(stem_rows(input_ref, offset), bands[offset])
-            found = part if found is None else found + part
+    selects = select_ref[...].reshape(PAIRS * INPUT_LANES, 2 * LANES)
+    for offset in range(WINDOW):
+        band = product(selects, weights_ref[offset]).astype(bf16)
+        top = offset * INPUT_LANES
+        for pair in range(PAIRS):
+            bands[top : top + INPUT_LANES, pair * LANES : (pair + 1) * LANES] = band[
+                pair * INPUT_LANES : (pair + 1) * INPUT_LANES
+            ]
+    rows = jnp.concatenate([stem_rows(input_ref, offset) for offset in range(WINDOW)], axis=1)
+    for half in range(2):
+        where = slice(half * WIDE, (half + 1) * WIDE)
+        found = product(rows, bands[:, where])
         pre_ref[:, where] = found
         sums_ref[0:1, where] = jnp.sum(found, 0, keepdims=True)
         sums_ref[1:2, where] = jnp.sum(found * found, 0, keepdims=True)
-        return carry
-
-    lax.fori_loop(0, STEM_LANES // TILE, step_body, 0)
 
 
 def stem_block(inputs, select, weights, after=()):
@@ -1397,7 +1492,7 @@
         [whole_out((rows, STEM_LANES)), whole_out((2, STEM_LANES))],
         [jax.ShapeDtypeStruct((rows, STEM_LANES), f32),
          jax.ShapeDtypeStruct((2, STEM_LANES), f32)],
-        [pltpu.VMEM((WINDOW, INPUT_LANES, TILE), bf16)],
+        [pltpu.VMEM((WINDOW * INPUT_LANES, STEM_LANES), bf16)],
         2 * WINDOW * rows * INPUT_LANES * STEM_LANES,
         after=after,
     )(inputs, select, weights)
@@ -1446,7 +1541,7 @@
 
 
 def stem_back_kernel(count, input_ref, select_ref, pre_ref, in_sums_ref, affine_ref, grad_ref,
-                     grads_ref, out_ref, low, turned):
+                     grads_ref, out_ref, low):
     def low_step(step, carry):
         where = lanes(step, LANES)
         mean, inverse, gain, _ = constants(in_sums_ref[:, where], affine_ref[:, where], count)
@@ -1463,22 +1558,11 @@
         return carry
 
     lax.fori_loop(0, STEM_LANES // LANES, low_step, 0)
-    out_ref[...] = jnp.zeros_like(out_ref)
-
+    selects = jnp.concatenate([select_ref[pair] for pair in range(PAIRS)], axis=1)
     for offset in range(WINDOW):
-        turned[offset] = stem_rows(input_ref, offset).T
-
-    def step_body(step, carry):
-        where = lanes(step, TILE)
-        for offset in range(WINDOW):
-            band = product(turned[offset], low[:, where]).astype(bf16)
-            found = product(select_ref[2 * step], band[:, 0:LANES]) + product(
-                select_ref[2 * step + 1], band[:, LANES:TILE]
-            )
-            out_ref[offset] += found
-        return carry
-
-    lax.fori_loop(0, STEM_LANES // TILE, step_body, 0)
+        band = product(stem_rows(input_ref, offset).T, low[...]).astype(bf16)
+        lined = [band[:, pair * LANES : (pair + 1) * LANES] for pair in range(PAIRS)]
+        out_ref[offset] = product(selects, jnp.concatenate(lined, axis=0))
 
 
 def stem_back_block(inputs, select, pre, sums, affine, grad, grads, count, after=()):
@@ -1492,7 +1576,7 @@
          whole_spec(grads.shape)],
         whole_out(out),
         jax.ShapeDtypeStruct(out, f32),
-        [pltpu.VMEM(shape, bf16), pltpu.VMEM((WINDOW, INPUT_LANES, shape[0]), bf16)],
+        [pltpu.VMEM(shape, bf16)],
         2 * WINDOW * shape[0] * INPUT_LANES * STEM_LANES,
         after=after,
     )(inputs, select, pre, sums, affine, grad, grads)
@@ -1548,8 +1632,9 @@
     )(me, *weights)
 
 
-def unpack_kernel(me_ref, first_ref, weights_out, next_out, scale_out, one_out, two_out,
-                  three_out, stem_out):
+def unpack_kernel(me_ref, first_ref, squeeze_out, weights_out, next_out, scale_out,
+                  one_out, two_out, three_out, stem_out):
+    squeeze_out[...] = first_ref[:, 0:64]
     wide = first_ref.shape[0]
     small = []
     for index in range(wide):
@@ -1589,7 +1674,7 @@
 
 def unpack_block(me, first):
     shapes = [
-        ((WINDOW, 2 * LANES, LANES), bf16), ((9, R), f32), ((9, R), f32), ((2, B), f32),
+        ((first.shape[0], 64, B), bf16), ((WINDOW, 2 * LANES, LANES), bf16), ((9, R), f32), ((9, R), f32), ((2, B), f32),
         ((2, B), f32), ((2, C), f32), ((2, STEM_LANES), f32),
     ]
     return kernel_call(
@@ -1644,9 +1729,11 @@
     stem_width = stem_weight.shape[1]
     inner_width = gain_one.shape[0]
     outer_width = gain_three.shape[0]
-    select = band_select()
-    cotangent = stem_cotangent.reshape(segments, STEM_SIDE, STEM_LANES)
-    cotangent = cotangent.transpose(1, 0, 2).reshape(stem_rows_here, STEM_LANES)
+
+    def by_output_row(values):
+        values = values.reshape(segments, STEM_SIDE, STEM_LANES)
+        return values.transpose(1, 0, 2).reshape(stem_rows_here, STEM_LANES)
+
     if direct:
         first_own, pair_own, spatial_own, late_own = cut_block(
             me_array, w_squeeze, w_expand, w_reduce, w_spatial, w_restore,
@@ -1654,17 +1741,16 @@
             scale_kernel, jnp.concatenate([gain_three, shift_three])[None], gain_one[None],
             shift_one[None], gain_two[None], shift_two[None], stem_gain[None], stem_shift[None],
         )
-        firsts, pairs, spatials = Gather(first_own), Gather(pair_own), Gather(spatial_own)
+        firsts, pairs, spatials = Gather(first_own), Gather(pair_own), HalvedGather(spatial_own)
         (cotangent, select), came, _ = beside(
-            lambda grads, band: (grads, band), [cotangent, select], firsts.depth()
+            lambda grads: (by_output_row(grads), band_select()), [stem_cotangent], firsts.depth()
         )
         firsts.take_depth(came)
         inputs, came, _ = beside(frames_block, [frames], firsts.second() + pairs.depth())
         firsts.take_second(came[:1])
         pairs.take_depth(came[1:])
-        squeeze_own = firsts.eight[:, 0:64]
         (
-            weights, full_next, full_scale, affine_one, affine_two, affine_three, stem_affine,
+            squeeze_own, weights, full_next, full_scale, affine_one, affine_two, affine_three, stem_affine,
         ) = unpack_block(me_array, firsts.eight)
         (stem_pre, stem_part), came, _ = beside(
             stem_block, [inputs, select, weights],
@@ -1691,7 +1777,7 @@
         affine_two = jnp.stack([whole(gain_two), whole(shift_two)])
         affine_three = jnp.stack([whole(gain_three), whole(shift_three)])
         stem_affine = jnp.tile(jnp.stack([whole(stem_gain), whole(stem_shift)]), (1, STEM_SIDE))
-        inputs = frames_block(frames)
+        inputs, select, cotangent = frames_block(frames), band_select(), by_output_row(stem_cotangent)
         stem_pre, stem_part = stem_block(inputs, select, weights)
     stem_part = stem_part.reshape(2, STEM_SIDE, STEM).sum(1).reshape(1, 2 * STEM)
 
@@ -1719,11 +1805,17 @@
     gate_operands = [me_array, pair, tokens, mixed_low]
     if direct:
         (logit, gated_low, pre_one, one_part), came, _ = beside(
-            gate_block, gate_operands, spatials.third()
-        )
-        spatials.take_third(came)
-        one_sums, came, _ = beside(swap_total, [with_row(one_part, stem_part)], spatials.core())
-        spatials.take_core(came)
+            gate_block, gate_operands, spatials.third_of(0)
+        )
+        spatials.take_third_of(0, came)
+        one_sums, came, _ = beside(
+            swap_total, [with_row(one_part, stem_part)],
+            spatials.third_of(1) + spatials.core_of(0),
+        )
+        spatials.take_third_of(1, came[:1])
+        spatials.take_core_of(0, came[1:])
+        one_sums, came, _ = beside(lambda values: values, [one_sums], spatials.core_of(1))
+        spatials.take_core_of(1, came)
         spatial = spatials.arrays
     else:
         logit, gated_low, pre_one, one_part = gate_block(*gate_operands)
@@ -1737,23 +1829,14 @@
     )
     stem_part = stem_part.reshape(2, STEM_SIDE, STEM).sum(1).reshape(1, 2 * STEM)
     two_sums = swap_total(two_part)
-    hidden_two, pre_three, three_part = third_block(pre_two, two_sums, affine_two, late, count)
+    hidden_two, pre_three, centres, three_part = third_block(pre_two, two_sums, affine_two, late, count)
     three_sums = total(with_row(three_part, stem_part))
     stem_grads = stem_lanes(three_sums)
-    activations, slope, view_sums = fourth_block(
-        pre_three, gated_low, three_sums, affine_three, count
+    bias = jnp.pad(class_bias.astype(f32), (0, TILE - CLASSES))[None]
+    activations, slope, view_sums, view_logits, pooled_low = fourth_block(
+        pre_three, centres, gated_low, three_sums, affine_three, late, bias, count
     )
-    stem_features = stem_out.reshape(STEM_SIDE, segments, STEM_LANES)
-    stem_features = stem_features.transpose(1, 0, 2).reshape(-1, STEM)
-
-    def of_views(kind):
-        return view_sums[:, 2 * kind : 2 * kind + 2].reshape(view_count, C)
-
-    pooled_low = (of_views(0) / PER_VIEW).astype(bf16)
-
-    full_class = late[:, RESTORE_ROWS:].reshape(32, CLASS_ROWS, 2, TILE)
-    full_class = full_class.transpose(0, 2, 1, 3).reshape(C, TILE)[:, :CLASSES]
-    view_logits = product(pooled_low, full_class) + class_bias.astype(f32)
+    pooled_low = pooled_low[:view_count]
 
     ends = jnp.cumsum(crop_counts)
     starts = ends - crop_counts
@@ -1768,33 +1851,35 @@
     own_start = jnp.sum(belongs * starts[None, :], 1)
     first = (own_start == positions[view_count : 2 * view_count]).astype(f32)
     same = (own_video[:, None] == video[None, :]).astype(f32) / own_count[:, None]
-    target = (own_label[:, None] == jnp.arange(CLASSES, dtype=jnp.int32)[None, :]).astype(f32)
+    target = (own_label[:, None] == jnp.arange(TILE, dtype=jnp.int32)[None, :]).astype(f32)
+    marks = jnp.concatenate([same, 1.0 / own_count[:, None], first[:, None]], axis=1)
+    marks = jnp.pad(marks, ((0, 8 - view_count), (0, LANES - marks.shape[1])))
+    target = jnp.pad(target, ((0, 8 - view_count), (0, 0)))
 
     before = lax.ppermute(view_logits, AXES, [(i, i + 1) for i in range(devices - 1)])
     following = lax.ppermute(view_logits, AXES, [(i + 1, i) for i in range(devices - 1)])
-    near = jnp.concatenate([before, view_logits, following])
-    video_logits = jnp.sum(same[:, :, None] * near[None, :, :], 1)
-    log_probs = jax.nn.log_softmax(video_logits, axis=-1)
-    entropy_part = jnp.sum(first * -jnp.sum(target * log_probs, axis=-1))
-    video_grad = loss_scale * (jnp.exp(log_probs) - target)
-    bias_part = jnp.sum(first[:, None] * video_grad, 0)
-    view_grad_low = (video_grad / own_count[:, None]).astype(bf16)
-
-    factors = jnp.concatenate(
-        [pooled_low, jnp.pad(view_grad_low, ((0, 0), (0, TILE - CLASSES)))], axis=1
+    three_part, pooled_grad, view_grad_low = video_block(
+        before, view_logits, following, marks, target, view_sums, late, view_count
     )
-    factors = jnp.pad(factors, ((0, -view_count % 8), (0, 0)))
-
-    pooled_grad = product_right(view_grad_low, full_class) / PER_VIEW
-    part_row = jnp.concatenate([bias_part, entropy_part[None]])[None]
-    three_part = jnp.stack([jnp.sum(pooled_grad * of_views(kind), 0) for kind in (1, 2)])
-    three_grads = total(with_row(three_part, part_row))
+    view_grad_low = view_grad_low[:view_count]
+
+    own_parts = pooled_low.reshape(view_count, wide, outer_width).swapaxes(0, 1)
+    grad_parts = jnp.broadcast_to(
+        view_grad_low, (wide, view_count, TILE)
+    )
+    factors = jnp.concatenate([own_parts, grad_parts], axis=2)
+    factors = jnp.broadcast_to(factors[:, None], (wide, narrow) + factors.shape[1:])
+    factors = factors.reshape((devices,) + factors.shape[2:])
+
+    def send_factors(parts):
+        return lax.all_to_all(parts, AXES, 0, 0, tiled=True)
+
+    three_grads = total(three_part)
     class_bias_grad = three_grads[2, :CLASSES]
     loss = three_grads[2, CLASSES] / crop_counts.shape[0]
-    pooled_grad = pooled_grad.reshape(-1, 2, C)
 
     fifth_operands = [
-        slope, pre_three, pooled_grad, three_sums, affine_three, three_grads, late,
+        slope, pre_three, centres, pooled_grad, three_sums, affine_three, three_grads, late,
         pre_two, two_sums, affine_two,
     ]
     run_fifth = functools.partial(fifth_block, count=count)
@@ -1802,8 +1887,7 @@
     run_stem_back = functools.partial(stem_back_block, count=stem_count)
 
     def stem_back_operands():
-        return [inputs, select.swapaxes(1, 2), stem_pre, stem_sums, stem_affine, stem_norm_grad, stem_grads]
-    run_low = functools.partial(low_block, count=count)
+        return [inputs, band_select(True), stem_pre, stem_sums, stem_affine, stem_norm_grad, stem_grads]
     run_outer = outer_block_of(R // 4)
 
     def sixth_operands():
@@ -1813,7 +1897,7 @@
         ]
 
     def low_operands():
-        return [norm_one_grad, pre_one, one_sums, affine_one, one_grads]
+        return [me_array, norm_one_grad, pre_one, one_sums, affine_one, one_grads, gated_low]
 
     def gate_back_operands():
         return [me_array, pair, low_one, slope, pooled_grad, tokens, logit]
@@ -1832,33 +1916,27 @@
         return jnp.pad(few, ((0, 0), (0, FEW_ROWS - few.shape[1]), (0, 0)))
 
     if direct:
-        views = Gather(factors)
-        (low_three, norm_two_grad, two_part), came, _ = beside(
-            run_fifth, fifth_operands, views.depth()
-        )
-        views.take_depth(came)
-        (buffer, two_grads), came, _ = beside(
+        low_three, norm_two_grad, two_part = run_fifth(*fifth_operands)
+        (buffer, two_grads), _, _ = beside(
             lambda hidden, low, part: (restore_outer_block(hidden, low), swap_total(part)),
-            [hidden_two, low_three, two_part], views.second(),
-        )
-        views.take_second(came)
-        (low_two, norm_one_grad, one_part), came, _ = beside(
-            run_sixth, sixth_operands(), views.third()
-        )
-        views.take_third(came)
-        (buffer, one_grads), came, _ = beside(
+            [hidden_two, low_three, two_part], [],
+        )
+        (low_two, norm_one_grad, one_part, factors), _, _ = beside(
+            lambda parts, *operands: (*run_sixth(*operands), send_factors(parts)),
+            [factors] + sixth_operands(), [],
+        )
+        (buffer, one_grads), _, _ = beside(
             lambda values, hidden, low, part: (
                 spatial_block(values.reshape(32, -1, WIDE), hidden, low), swap_total(part)
             ),
-            [buffer, hidden_one, low_two, one_part], views.core(),
-        )
-        views.take_core(came)
+            [buffer, hidden_one, low_two, one_part], [],
+        )
         buffer = lax.psum_scatter(
             buffer.reshape(8, -1, WIDE), "wide", scatter_dimension=0, tiled=False
         )
         quarter = (4, 2, 2, R // 4, TILE)
-        low_one = run_low(*low_operands())
-        reduced_sum = Sum(run_outer(me_array, low_one, gated_low), quarter, 0)
+        low_one, reduce_half = low_outer_block(*low_operands(), count)
+        reduced_sum = Sum(reduce_half, quarter, 0)
         low_one, came, _ = beside(lambda values: values, [low_one], reduced_sum.core())
         reduced_sum.take_core(came)
         (logit_grad, tokens_part), came, _ = beside(
@@ -1892,29 +1970,35 @@
         )
         squeezed.take(came[:1])
         expand_sum.take(came[1:])
-        few = few_of(stem_back, kernel_grads)
-        (tokens_grad, few, buffer), came, _ = beside(
-            lambda mine, blocks, part, low, grads, quarters: (
-                tokens_block(mine, blocks, part, low),
-                lax.all_to_all(grads, "wide", 0, 0, tiled=True),
-                lax.all_to_all(quarters, "narrow", 0, 0, tiled=True),
+        (tokens_grad, few), came, _ = beside(
+            lambda grads, *operands: (
+                tokens_block(*operands), lax.all_to_all(grads, "wide", 0, 0, tiled=True)
             ),
-            [me_array, squeeze, tokens_part, low_squeezed, few, buffer.reshape(4, -1, WIDE)],
+            [few_of(stem_back, kernel_grads), me_array, squeeze, tokens_part, low_squeezed],
             squeezed.split("y") + expand_sum.spread(),
         )
-        buffer = jnp.sum(buffer.astype(f32), 0)
         squeezed.take(came[:1])
         expand_sum.take_spread(came[1:])
         few = jnp.sum(few, 0)
-        few, came, _ = beside(
-            lambda part: part + exchange(part, 1), [few], squeezed.split("z")
-        )
-        squeezed.take(came)
+        buffer = buffer.reshape(4, -1, WIDE)
+        near_place = lax.axis_index("narrow")
+        (few, stem_out, own), came, _ = beside(
+            lambda part, *kept: (
+                part + exchange(part, 1) + exchange(part, 2) + exchange(part, 3), *kept
+            ),
+            [few, stem_out, lax.dynamic_index_in_dim(buffer, near_place, 0, keepdims=False)],
+            squeezed.split("z") + [
+                (lax.dynamic_index_in_dim(buffer, near_place ^ mask, 0, keepdims=False), mask)
+                for mask in (1, 2, 3)
+            ],
+        )
+        squeezed.take(came[:3])
+        own = own.astype(f32)
+        for part in came[3:]:
+            own = own + part.astype(f32)
         buffers = Sum((None, None), (), 0)
-        buffers.values = buffer
-        few, came, _ = beside(
-            lambda part: part + exchange(part, 2), [few], squeezed.spread() + buffers.spread()
-        )
+        buffers.values = own
+        _, came, _ = beside(lambda: None, [], squeezed.spread() + buffers.spread())
         squeezed.take_spread(came[:3])
         buffers.take_spread(came[3:])
         buffer = buffers.whole
@@ -1927,16 +2011,15 @@
         sum_reduce = reduced_sum.whole.reshape(B, TILE).T
         sum_expand = expand_sum.whole.reshape(R, TILE)
         sum_squeeze = squeezed.whole.reshape(R, TILE).T
-        factors = [array.reshape(-1, C + TILE) for array in views.arrays]
     else:
         low_three, norm_two_grad, two_part = run_fifth(*fifth_operands)
         buffer = restore_outer_block(hidden_two, low_three)
         two_grads = swap_total(two_part)
         low_two, norm_one_grad, one_part = run_sixth(*sixth_operands())
+        factors = send_factors(factors)
         one_grads = swap_total(one_part)
         buffer = spatial_block(buffer.reshape(32, -1, WIDE), hidden_one, low_two)
-        low_one = run_low(*low_operands())
-        reduce_half = run_outer(me_array, low_one, gated_low)
+        low_one, reduce_half = low_outer_block(*low_operands(), count)
         logit_grad, tokens_part = gate_back_block(*gate_back_operands())
         expand_half = run_outer(me_array, mixed_low, logit_grad)
         low_squeezed, kernel_grads = mixing_back_block(*mixing_back_operands())
@@ -1958,14 +2041,14 @@
         sum_restore, sum_spatial, sum_reduce, sum_expand, sum_squeeze = reduced(
             buffer, reduce_half, expand_half, squeeze_half
         )
-        factors = [lax.all_gather(factors, AXES, tiled=True)]
-    sum_class = sum(
-        product_left(
-            lax.dynamic_slice_in_dim(part, lax.axis_index("wide") * outer_width, outer_width, 1),
-            part[:, C : C + CLASSES],
-        )
-        for part in factors
+    factors = factors.reshape(devices * view_count, outer_width + TILE)
+    sum_class = product_left(
+        factors[:, :outer_width], factors[:, outer_width : outer_width + CLASSES]
     )
+
+    stem_features = stem_out.reshape(STEM_SIDE, segments, STEM_LANES)
+    stem_features = stem_features.transpose(1, 0, 2).reshape(-1, STEM)
+
     def own_slice(values, width):
         return lax.dynamic_slice_in_dim(values, lax.axis_index("wide") * width, width)
 

time: 561 us -> 525 us (0.936)
  waiting for transfers between devices: 78.1 us -> 62.6 us
  Pallas kernels: 266 us -> 252 us
    pallas_call x30 -> x27, Pallas kernels: 266 us -> 252 us  [kernel_call(): return lambda *operands: call(*operands, *after)]
    ppermute x74, waiting for transfers between devices: 57 us -> 43.2 us  [exchange(): lax.ppermute(values, AXES, [(index, index ^ mask) for index in range(size)])]
    all_to_all x1, waiting for transfers between devices: 7.76 us -> 0.91 us  [shards(): lax.all_to_all(grads, 'wide', 0, 0, tiled=True)]
    unnamed x97 -> x75, local copies, waits for them, and re-layouts: 11.6 us -> 8.59 us
  transfers between devices with their start and end apart: 84 -> 84, of which waited for: 27 -> 28; matrix products, arithmetic and copies ran while one was open for 8% -> 10% of each run, Pallas kernels for 42% -> 39%
where the time goes in v1:
time: 525 us; the launch traced here: 515 us
  Pallas kernels  252 us (48%)
  starting transfers between devices  109 us (21%)
  waiting for transfers between devices  62.6 us (12%)
  local copies, waits for them, and re-layouts  43.9 us (8%)
  other arithmetic  28.5 us (5%)
  between operations  17.6 us (3%)
    pallas_call x27, Pallas kernels, kernel_call(): return lambda *operands: call(*operands, *after)  252 us
    ppermute x74, starting transfers between devices, exchange(): lax.ppermute(values, AXES, [(index, index ^ mask) for index in range(size)])  76.6 us
    ppermute x74, waiting for transfers between devices, exchange(): lax.ppermute(values, AXES, [(index, index ^ mask) for index in range(size)])  43.2 us
    all_to_all x4, starting transfers between devices, swap_total(): return jnp.sum(lax.all_to_all(copies, AXES, 0, 0, tiled=True), 0)  17.7 us
    all_to_all x4, waiting for transfers between devices, swap_total(): return jnp.sum(lax.all_to_all(copies, AXES, 0, 0, tiled=True), 0)  16.3 us
  transfers between devices with their start and end apart: 84, of which 28 were waited for; matrix products, arithmetic and copies ran while one was open for 10% of the time, Pallas kernels for 39%

profile of v1, /device:TPU:0, one launch (start us, length us, event | category | flops | bytes accessed | tf_op | source)
XLA Modules:
  0.0 515.1 jit_solution(3166059592327896340)
XLA Ops:
  10.2 2.3 shard_map.390
  12.5 3.0 collective-permute-start
  15.5 2.6 collective-permute-start.1
  18.4 1.8 fusion.3.refs_1_
  20.2 2.0 copy.121
  22.3 2.3 reshape.253
  24.5 2.8 copy.122
  27.9 1.8 collective-permute-start.3
  30.4 3.5 collective-permute-start.5
  34.1 7.8 %shard_map.392.refs_0_ = bf16[2,19,32,384]{3,2,1,0:T(8,128)(2,1)} custom-call(bf16[32,5,3,32,32]{4,3,2,1,0:T(8,128)(2,1)} %bitcast.244), custom_call_target="tpu_custom_call" | custom-call | flops 98304000 | bytes 16777216 | tf_op jit(solution)/shard_map/pallas_call | solution.py:341
  44.3 2.3 shard_map.394
  49.4 2.9 collective-permute-start.10
  53.7 9.2 %shard_map.396 = (f32[512,1024]{1,0:T(8,128)}, f32[2,1024]{1,0:T(2,128)}) custom-call(bf16[2,19,32,384]{3,2,1,0:T(8,128)(2,1)} %shard_map.392.refs_0_, bf16[8,384,256]{2,1,0:T(8,128)(2,1)} %fusion.3.refs_1_, bf16[7,256,128]{2,1,0:T(8,128)(2,1)} %get-tuple-element.356.refs_2_), custom_call_target="tpu_custom_call" | custom-call | flops 5637144576 | bytes 16777216 | tf_op jit(solution)/shard_map/pallas_call | solution.py:341
  68.2 15.1 %shard_map.399 = (f32[1568,512]{1,0:T(8,128)}, f32[1568,512]{1,0:T(8,128)}, bf16[1568,512]{1,0:T(8,128)(2,1)}) custom-call(s32[1]{0:T(128)} %bitcast.refs_0_, bf16[8,64,512]{2,1,0:T(8,128)(2,1)} %get-tuple-element.587.refs_1_, bf16[8,64,512]{2,1,0:T(8,128)(2,1)} %collective-permute-done.7.refs_2_, bf16[8,64,512]{2,1,0:T(8,128)(2,1)} %copy-done.33, ...), custom_call_target="tpu_custom_call" | custom-call | flops 6576668672 | bytes 16777216 | tf_op jit(solution)/shard_map/pallas_call | solution.py:341
  83.3 7.8 %collective-permute-done.14.refs_2_ = bf16[8,128,512]{2,1,0:T(8,128)(2,1)S(1)} collective-permute-done((bf16[8,128,512]{2,1,0:T(8,128)(2,1)S(1)}, bf16[8,128,512]{2,1,0:T(8,128)(2,1)S(1)}, u32[]{:S(2)}, u32[]{:S(2)}) %collective-permute-start.14) | collective-permute-done | bytes 1048608 | tf_op jit(solution)/shard_map/ppermute | solution.py:44
  91.6 2.9 collective-permute-done.16.refs_3_
  96.4 15.8 %shard_map.400 = (bf16[1568,2048]{1,0:T(8,128)(2,1)}, bf16[1568,2048]{1,0:T(8,128)(2,1)}, f32[1568,512]{1,0:T(8,128)}, f32[2,512]{1,0:T(2,128)}) custom-call(s32[1]{0:T(128)} %bitcast.refs_0_, bf16[8,128,512]{2,1,0:T(8,128)(2,1)} %copy-done, bf16[8,128,512]{2,1,0:T(8,128)(2,1)} %copy-done.7, bf16[8,128,512]{2,1,0:T(8,128)(2,1)} %copy-done.8, ...), custom_call_target="tpu_custom_call" | custom-call | flops 13153337344 | bytes 16777216 | tf_op jit(solution)/shard_map/pallas_call | solution.py:341
  115.7 4.3 all-to-all-start
  120.8 14.0 %all-to-all-done = f32[32,3,512]{2,1,0:T(4,128)S(1)} async-done(((f32[32,3,512]{2,1,0:T(4,128)}), f32[32,3,512]{2,1,0:T(4,128)S(1)}, u32[]{:S(2)}, u32[]{:S(2)}) %all-to-all-start) | async-done | bytes 196640 | tf_op jit(solution)/shard_map/all_to_all | solution.py:67
  139.4 14.4 %shard_map.401 = (bf16[2,1008,1536]{2,1,0:T(8,128)(2,1)}, f32[1568,512]{1,0:T(8,128)}, f32[2,512]{1,0:T(2,128)}) custom-call(s32[1]{0:T(128)} %bitcast.refs_0_, bf16[4,144,512]{2,1,0:T(8,128)(2,1)} %copy-done.2, bf16[4,144,512]{2,1,0:T(8,128)(2,1)} %collective-permute-done.15.refs_2_, bf16[4,144,512]{2,1,0:T(8,128)(2,1)} %copy-done.28, ...), custom_call_target="tpu_custom_call" | custom-call | flops 14797504512 | bytes 16777216 | tf_op jit(solution)/shard_map/pallas_call | solution.py:341
  155.3 4.6 all-to-all-start.1
  159.9 5.1 shard_map.403
  165.8 2.3 all-to-all-done.1
  168.8 11.1 %shard_map.402 = (bf16[1568,512]{1,0:T(8,128)(2,1)}, bf16[1568,2048]{1,0:T(8,128)(2,1)}, f32[2,1,2048]{2,1,0:T(1,128)}, f32[2,2048]{1,0:T(2,128)}) custom-call(f32[1568,512]{1,0:T(8,128)} %get-tuple-element.472.refs_0_.refs_8_.refs_10_, f32[2,512]{1,0:T(2,128)} %reduce_sum.101.refs_1_.refs_9_.refs_11_, ...), custom_call_target="tpu_custom_call" | custom-call | flops 6576668672 | bytes 16777216 | tf_op jit(solution)/shard_map/pallas_call | solution.py:341
  184.1 2.1 collective-permute-start.27
  187.0 1.9 collective-permute-done.27
  190.1 2.5 collective-permute-start.29
  194.9 3.4 collective-permute-done.30
  198.9 14.5 %shard_map.404 = (bf16[1568,2048]{1,0:T(8,128)(2,1)}, bf16[1568,2048]{1,0:T(8,128)(2,1)}, f32[2,8,2048]{2,1,0:T(8,128)}, f32[16,256]{1,0:T(8,128)}, bf16[16,2048]{1,0:T(8,128)(2,1)}) custom-call(bf16[1568,2048]{1,0:T(8,128)(2,1)} %get-tuple-element.436.refs_0_.refs_1_, f32[2,1,2048]{2,1,0:T(1,128)} %get-tuple-element.437.refs_1_.refs_2_, ...), custom_call_target="tpu_custom_call" | custom-call | flops 128450560 | bytes 16777216 | tf_op jit(solution)/shard_map/pallas_call | solution.py:341
  216.7 2.1 collective-permute-done.32.refs_2_
  219.4 3.2 shard_map.405
  222.7 2.5 collective-permute-start.33
  227.1 2.4 collective-permute-start.34
  235.9 1.8 collective-permute-start.38
  237.6 1.7 collective-permute-start.39
  239.3 1.7 collective-permute-done.38
  241.0 2.3 collective-permute-done.39
  244.0 16.7 %shard_map.406 = (bf16[1568,2048]{1,0:T(8,128)(2,1)}, f32[1568,512]{1,0:T(8,128)}, f32[2,512]{1,0:T(2,128)}) custom-call(bf16[1568,2048]{1,0:T(8,128)(2,1)} %get-tuple-element.507.refs_0_.refs_6_, bf16[1568,2048]{1,0:T(8,128)(2,1)} %get-tuple-element.436.refs_0_.refs_1_, f32[2,1,2048]{2,1,0:T(1,128)} %get-tuple-element.437.refs_1_.refs_2_, ...), custom_call_target="tpu_custom_call" | custom-call | flops 6576668672 | bytes 16777216 | tf_op jit(solution)/shard_map/pallas_call | solution.py:341
  262.0 3.0 all-to-all-start.2
  265.0 8.3 %shard_map.407 = bf16[8,4,208,512]{3,2,1,0:T(8,128)(2,1)} custom-call(bf16[1568,512]{1,0:T(8,128)(2,1)} %get-tuple-element.458.refs_0_, bf16[1568,2048]{1,0:T(8,128)(2,1)} %get-tuple-element.459.refs_1_), custom_call_target="tpu_custom_call" | custom-call | flops 6576668672 | bytes 16777216 | tf_op jit(solution)/shard_map/pallas_call | solution.py:341
  274.7 5.8 %all-to-all-start.3 = ((bf16[32,4,512]{2,1,0:T(4,128)(2,1)}), bf16[32,4,512]{2,1,0:T(4,128)(2,1)S(1)}, u32[]{:S(2)}, u32[]{:S(2)}) async-start(bf16[32,4,512]{2,1,0:T(4,128)(2,1)} %bitcast.38), calls=%async_computation.3 | async-start | bytes 262144 | tf_op jit(solution)/shard_map/all_to_all | solution.py:1875
  280.5 17.8 %shard_map.408 = (bf16[1568,512]{1,0:T(8,128)(2,1)}, f32[1568,512]{1,0:T(8,128)}, f32[2,512]{1,0:T(2,128)}) custom-call(s32[1]{0:T(128)} %bitcast.refs_0_, bf16[4,144,512]{2,1,0:T(8,128)(2,1)} %copy-done.2, bf16[4,144,512]{2,1,0:T(8,128)(2,1)} %collective-permute-done.15.refs_2_, bf16[4,144,512]{2,1,0:T(8,128)(2,1)} %copy-done.28, ...), custom_call_target="tpu_custom_call" | custom-call | flops 14797504512 | bytes 16777216 | tf_op jit(solution)/shard_map/pallas_call | solution.py:341
  299.7 5.8 %all-to-all-start.4 = ((f32[32,2,512]{2,1,0:T(2,128)}), f32[32,2,512]{2,1,0:T(2,128)S(1)}, u32[]{:S(2)}, u32[]{:S(2)}) async-start(f32[32,2,512]{2,1,0:T(2,128)} %broadcast_in_dim.142), calls=%async_computation.4 | async-start | bytes 262144 | tf_op jit(solution)/shard_map/all_to_all | solution.py:67
  305.5 17.8 %shard_map.409 = bf16[32,208,512]{2,1,0:T(8,128)(2,1)} custom-call(bf16[32,208,512]{2,1,0:T(8,128)(2,1)} %bitcast.233, bf16[2,1008,1536]{2,1,0:T(8,128)(2,1)} %get-tuple-element.489.refs_1_, bf16[1568,512]{1,0:T(8,128)(2,1)} %get-tuple-element.490.refs_2_), custom_call_target="tpu_custom_call", output_to_operand_aliasing={{}: (0, {})} | custom-call | flops 14797504512 | bytes 16777216 | tf_op jit(solution)/shard_map/pallas_call | solution.py:341
  324.0 2.0 fusion.2.refs_1_
  327.6 11.4 %shard_map.410 = (bf16[1568,512]{1,0:T(8,128)(2,1)}, f32[8,256,256]{2,1,0:T(8,128)}, bf16[8,256,256]{2,1,0:T(8,128)(2,1)}) custom-call(s32[1]{0:T(128)} %bitcast.refs_0_, f32[1568,512]{1,0:T(8,128)} %get-tuple-element.483.refs_1_, f32[1568,512]{1,0:T(8,128)} %get-tuple-element.476.refs_9_.refs_14_.refs_2_, f32[3,512]{1,0:T(4,128)} %copy-done.24, ...), custom_call_target="tpu_custom_call" | custom-call | flops 6576668672 | bytes 16777216 | tf_op jit(solution)/shard_map/pallas_call | solution.py:341
  343.4 1.9 convert_add_fusion.2
  345.4 1.7 collective-permute-start.41
  347.1 18.7 %shard_map.411 = (bf16[1568,2048]{1,0:T(8,128)(2,1)}, bf16[1568,2048]{1,0:T(8,128)(2,1)}) custom-call(s32[1]{0:T(128)} %bitcast.refs_0_, bf16[8,128,512]{2,1,0:T(8,128)(2,1)} %copy-done, bf16[8,128,512]{2,1,0:T(8,128)(2,1)} %copy-done.7, bf16[8,128,512]{2,1,0:T(8,128)(2,1)} %copy-done.8, bf16[8,128,512]{2,1,0:T(8,128)(2,1)} %collective-permute-done.17.refs_4_, ...), custom_call_target="tpu_custom_call" | custom-call | flops 6576668672 | bytes 16777216 | tf_op jit(solution)/shard_map/pallas_call | solution.py:341
  369.4 8.7 %shard_map.412 = (f32[8,256,256]{2,1,0:T(8,128)}, bf16[8,256,256]{2,1,0:T(8,128)(2,1)}) custom-call(s32[1]{0:T(128)} %bitcast.refs_0_, bf16[1568,512]{1,0:T(8,128)(2,1)} %get-tuple-element.517.refs_6_.refs_1_, bf16[1568,2048]{1,0:T(8,128)(2,1)} %get-tuple-element.536.refs_2_.refs_5_), custom_call_target="tpu_custom_call" | custom-call | flops 6576668672 | bytes 16777216 | tf_op jit(solution)/shard_map/pallas_call | solution.py:341
  381.1 2.1 convert_add_fusion.1
  385.4 2.4 collective-permute-start.46
  388.3 20.3 %shard_map.413 = (bf16[1568,512]{1,0:T(8,128)(2,1)}, f32[18,512]{1,0:T(8,128)}) custom-call(s32[1]{0:T(128)} %bitcast.refs_0_, bf16[8,128,512]{2,1,0:T(8,128)(2,1)} %copy-done, bf16[8,128,512]{2,1,0:T(8,128)(2,1)} %copy-done.7, bf16[8,128,512]{2,1,0:T(8,128)(2,1)} %copy-done.8, bf16[8,128,512]{2,1,0:T(8,128)(2,1)} %collective-permute-done.17.refs_4_, ...), custom_call_target="tpu_custom_call" | custom-call | flops 6576668672 | bytes 16777216 | tf_op jit(solution)/shard_map/pallas_call | solution.py:341
  411.0 1.7 collective-permute-start.50
  412.9 8.7 %shard_map.414 = (f32[8,256,256]{2,1,0:T(8,128)}, bf16[8,256,256]{2,1,0:T(8,128)(2,1)}) custom-call(s32[1]{0:T(128)} %bitcast.refs_0_, bf16[1568,512]{1,0:T(8,128)(2,1)} %get-tuple-element.592.refs_1_.refs_6_, bf16[1568,2048]{1,0:T(8,128)(2,1)} %refs_2_.2), custom_call_target="tpu_custom_call" | custom-call | flops 6576668672 | bytes 16777216 | tf_op jit(solution)/shard_map/pallas_call | solution.py:341
  424.6 1.8 convert_add_fusion
  426.5 1.7 collective-permute-start.53
  428.8 3.3 collective-permute-start.55
  432.7 10.9 %shard_map.415 = f32[7,256,128]{2,1,0:T(8,128)} custom-call(bf16[2,19,32,384]{3,2,1,0:T(8,128)(2,1)} %shard_map.392.refs_0_, bf16[8,256,384]{2,1,0:T(8,128)(2,1)} %fusion.2.refs_1_, f32[512,1024]{1,0:T(8,128)} %get-tuple-element.570.refs_0_.refs_2_, f32[2,1024]{1,0:T(2,128)} %tile.22.refs_1_.refs_3_, f32[2,1024]{1,0:T(2,128)} %get-tuple-element.572.refs_2_.refs_4_, ...), custom_call_target="tpu_custom_call" | custom-call | flops 5637144576 | bytes 16777216 | tf_op jit(solution)/shard_map/pallas_call | solution.py:341
  451.9 6.5 %all-to-all-start.5 = ((f32[8,40,256]{2,1,0:T(8,128)}), f32[8,40,256]{2,1,0:T(8,128)S(1)}, u32[]{:S(2)}, u32[]{:S(2)}) async-start(f32[8,40,256]{2,1,0:T(8,128)} %select_maximum_fusion), calls=%async_computation.5 | async-start | bytes 655360 | tf_op jit(solution)/shard_map/all_to_all | solution.py:1975
  458.5 9.7 %shard_map.416 = bf16[1568,2048]{1,0:T(8,128)(2,1)} custom-call(s32[1]{0:T(128)} %bitcast.refs_0_, bf16[8,64,512]{2,1,0:T(8,128)(2,1)} %get-tuple-element.587.refs_1_, bf16[8,64,512]{2,1,0:T(8,128)(2,1)} %collective-permute-done.7.refs_2_, bf16[8,64,512]{2,1,0:T(8,128)(2,1)} %copy-done.33, bf16[8,64,512]{2,1,0:T(8,128)(2,1)} %copy-done.34, ...), custom_call_target="tpu_custom_call" | custom-call | flops 6576668672 | bytes 16777216 | tf_op jit(solution)/shard_map/pallas_call | solution.py:341
  476.6 2.4 collective-permute-start.65
  480.0 4.3 collective-permute-done.65
  495.3 5.8 %collective-permute-done.71 = bf16[128,256]{1,0:T(8,128)(2,1)S(1)} collective-permute-done((bf16[128,256]{1,0:T(8,128)(2,1)S(1)}, bf16[128,256]{1,0:T(8,128)(2,1)S(1)}, u32[]{:S(2)}, u32[]{:S(2)}) %collective-permute-start.71) | collective-permute-done | bytes 65568 | tf_op jit(solution)/shard_map/ppermute | solution.py:44
  (362 shorter events, 112.5 us)
Async XLA Ops:
  7.2 161.6 %all-gather.3.cloned.1.call-start = ((), (), s32[]{:S(2)}) async-start(), calls=%async_computation.8 | async-start | bytes 3244032 | tf_op jit(solution)/shard_map/all_gather | solution.py:1801
  12.5 14.9 %collective-permute-start = (bf16[96,512]{1,0:T(8,128)(2,1)}, bf16[96,512]{1,0:T(8,128)(2,1)S(1)}, u32[]{:S(2)}, u32[]{:S(2)}) collective-permute-start(bf16[96,512]{1,0:T(8,128)(2,1)} %get-tuple-element.336), channel_id=1, source_target_pairs={{0,8},{1,9},{2,10},{3,11},{4,12},{5,13},{6,14},{7,15},{8,0},{9,1},... | collective-permute-start | bytes 294920 | tf_op jit(solution)/shard_map/ppermute | solution.py:44
  15.5 11.8 %collective-permute-start.1 = (bf16[96,512]{1,0:T(8,128)(2,1)}, bf16[96,512]{1,0:T(8,128)(2,1)S(1)}, u32[]{:S(2)}, u32[]{:S(2)}) collective-permute-start(bf16[96,512]{1,0:T(8,128)(2,1)} %get-tuple-element.336), channel_id=1, source_target_pairs={{0,16},{1,17},{2,18},{3,19},{4,20},{5,21},{6,22},{7,23},{8,24},{9,... | collective-permute-start | bytes 294920 | tf_op jit(solution)/shard_map/ppermute | solution.py:44
  18.1 9.2 %collective-permute-start.2 = (bf16[96,512]{1,0:T(8,128)(2,1)}, bf16[96,512]{1,0:T(8,128)(2,1)S(1)}, u32[]{:S(2)}, u32[]{:S(2)}) collective-permute-start(bf16[96,512]{1,0:T(8,128)(2,1)} %get-tuple-element.336), channel_id=1, source_target_pairs={{0,24},{1,25},{2,26},{3,27},{4,28},{5,29},{6,30},{7,31},{8,16},{9,... | collective-permute-start | bytes 294920 | tf_op jit(solution)/shard_map/ppermute | solution.py:44
  27.9 15.1 %collective-permute-start.3 = (bf16[4,96,512]{2,1,0:T(8,128)(2,1)S(1)}, bf16[4,96,512]{2,1,0:T(8,128)(2,1)S(1)}, u32[]{:S(2)}, u32[]{:S(2)}) collective-permute-start(bf16[4,96,512]{2,1,0:T(8,128)(2,1)S(1)} %shard_map.391.refs_0_), channel_id=1, source_target_pairs={{0,4},{1,5},{2,6},{3,7},{4,0},{5,1},{6,2},{7,3},{8,12},{9,13},{10,... | collective-permute-start | bytes 1179656 | tf_op jit(solution)/shard_map/ppermute | solution.py:44
  29.7 12.2 %collective-permute-start.4 = (bf16[128,512]{1,0:T(8,128)(2,1)S(1)}, bf16[128,512]{1,0:T(8,128)(2,1)S(1)}, u32[]{:S(2)}, u32[]{:S(2)}) collective-permute-start(bf16[128,512]{1,0:T(8,128)(2,1)S(1)} %copy-done.4), channel_id=1, source_target_pairs={{0,8},{1,9},{2,10},{3,11},{4,12},{5,13},{6,14},{7,15},{8,0},{9,1},... | collective-permute-start | bytes 393224 | tf_op jit(solution)/shard_map/ppermute | solution.py:44
  30.4 12.6 %collective-permute-start.5 = (bf16[128,512]{1,0:T(8,128)(2,1)S(1)}, bf16[128,512]{1,0:T(8,128)(2,1)S(1)}, u32[]{:S(2)}, u32[]{:S(2)}) collective-permute-start(bf16[128,512]{1,0:T(8,128)(2,1)S(1)} %copy-done.4), channel_id=1, source_target_pairs={{0,16},{1,17},{2,18},{3,19},{4,20},{5,21},{6,22},{7,23},{8,24},{9,... | collective-permute-start | bytes 393224 | tf_op jit(solution)/shard_map/ppermute | solution.py:44
  33.9 9.1 %collective-permute-start.6 = (bf16[128,512]{1,0:T(8,128)(2,1)S(1)}, bf16[128,512]{1,0:T(8,128)(2,1)S(1)}, u32[]{:S(2)}, u32[]{:S(2)}) collective-permute-start(bf16[128,512]{1,0:T(8,128)(2,1)S(1)} %copy-done.4), channel_id=1, source_target_pairs={{0,24},{1,25},{2,26},{3,27},{4,28},{5,29},{6,30},{7,31},{8,16},{9,... | collective-permute-start | bytes 393224 | tf_op jit(solution)/shard_map/ppermute | solution.py:44
  47.3 15.6 %collective-permute-start.7 = (bf16[8,64,512]{2,1,0:T(8,128)(2,1)}, bf16[8,64,512]{2,1,0:T(8,128)(2,1)}, u32[]{:S(2)}, u32[]{:S(2)}) collective-permute-start(bf16[8,64,512]{2,1,0:T(8,128)(2,1)} %get-tuple-element.587.refs_1_), channel_id=1, source_target_pairs={{0,2},{1,3},{2,0},{3,1},{4,6},{5,7},{6,4},{7,5},{8,10},{9,11},{10,... | collective-permute-start | bytes 1572872 | tf_op jit(solution)/shard_map/ppermute | solution.py:44
  48.9 14.1 %collective-permute-start.8 = (bf16[4,128,512]{2,1,0:T(8,128)(2,1)S(1)}, bf16[4,128,512]{2,1,0:T(8,128)(2,1)S(1)}, u32[]{:S(2)}, u32[]{:S(2)}) collective-permute-start(bf16[4,128,512]{2,1,0:T(8,128)(2,1)S(1)} %shard_map.395.refs_0_), channel_id=1, source_target_pairs={{0,4},{1,5},{2,6},{3,7},{4,0},{5,1},{6,2},{7,3},{8,12},{9,13},{10,... | collective-permute-start | bytes 1572872 | tf_op jit(solution)/shard_map/ppermute | solution.py:44
  49.4 13.5 %collective-permute-start.10 = (bf16[144,512]{1,0:T(8,128)(2,1)S(1)}, bf16[144,512]{1,0:T(8,128)(2,1)S(1)}, u32[]{:S(2)}, u32[]{:S(2)}) collective-permute-start(bf16[144,512]{1,0:T(8,128)(2,1)S(1)} %copy-done.3), channel_id=1, source_target_pairs={{0,16},{1,17},{2,18},{3,19},{4,20},{5,21},{6,22},{7,23},{8,24},{9,... | collective-permute-start | bytes 442376 | tf_op jit(solution)/shard_map/ppermute | solution.py:44
  52.3 10.6 %collective-permute-start.11 = (bf16[144,512]{1,0:T(8,128)(2,1)S(1)}, bf16[144,512]{1,0:T(8,128)(2,1)S(1)}, u32[]{:S(2)}, u32[]{:S(2)}) collective-permute-start(bf16[144,512]{1,0:T(8,128)(2,1)S(1)} %copy-done.3), channel_id=1, source_target_pairs={{0,24},{1,25},{2,26},{3,27},{4,28},{5,29},{6,30},{7,31},{8,16},{9,... | collective-permute-start | bytes 442376 | tf_op jit(solution)/shard_map/ppermute | solution.py:44
  53.7 9.2 %collective-permute-start.9 = (bf16[144,512]{1,0:T(8,128)(2,1)S(1)}, bf16[144,512]{1,0:T(8,128)(2,1)S(1)}, u32[]{:S(2)}, u32[]{:S(2)}) collective-permute-start(bf16[144,512]{1,0:T(8,128)(2,1)S(1)} %copy-done.3), channel_id=1, source_target_pairs={{0,8},{1,9},{2,10},{3,11},{4,12},{5,13},{6,14},{7,15},{8,0},{9,1},... | collective-permute-start | bytes 442376 | tf_op jit(solution)/shard_map/ppermute | solution.py:44
  65.9 25.2 %collective-permute-start.14 = (bf16[8,128,512]{2,1,0:T(8,128)(2,1)S(1)}, bf16[8,128,512]{2,1,0:T(8,128)(2,1)S(1)}, u32[]{:S(2)}, u32[]{:S(2)}) collective-permute-start(bf16[8,128,512]{2,1,0:T(8,128)(2,1)S(1)} %shard_map.398.refs_1_), channel_id=1, source_target_pairs={{0,2},{1,3},{2,0},{3,1},{4,6},{5,7},{6,4},{7,5},{8,10},{9,11},{10,... | collective-permute-start | bytes 3145736 | tf_op jit(solution)/shard_map/ppermute | solution.py:44
  66.7 16.6 %collective-permute-start.15 = (bf16[4,144,512]{2,1,0:T(8,128)(2,1)S(1)}, bf16[4,144,512]{2,1,0:T(8,128)(2,1)}, u32[]{:S(2)}, u32[]{:S(2)}) collective-permute-start(bf16[4,144,512]{2,1,0:T(8,128)(2,1)S(1)} %shard_map.397.refs_1_), channel_id=1, source_target_pairs={{0,4},{1,5},{2,6},{3,7},{4,0},{5,1},{6,2},{7,3},{8,12},{9,13},{10,... | collective-permute-start | bytes 1769480 | tf_op jit(solution)/shard_map/ppermute | solution.py:44
  95.8 16.4 %collective-permute-start.18 = (bf16[4,144,512]{2,1,0:T(8,128)(2,1)S(1)}, bf16[4,144,512]{2,1,0:T(8,128)(2,1)S(1)}, u32[]{:S(2)}, u32[]{:S(2)}) collective-permute-start(bf16[4,144,512]{2,1,0:T(8,128)(2,1)S(1)} %shard_map.397.refs_1_), channel_id=1, source_target_pairs={{0,2},{1,3},{2,0},{3,1},{4,6},{5,7},{6,4},{7,5},{8,10},{9,11},{10,... | collective-permute-start | bytes 1769480 | tf_op jit(solution)/shard_map/ppermute | solution.py:44
  113.0 21.9 %collective-permute-start.19 = (bf16[4,144,512]{2,1,0:T(8,128)(2,1)}, bf16[4,144,512]{2,1,0:T(8,128)(2,1)S(1)}, u32[]{:S(2)}, u32[]{:S(2)}) collective-permute-start(bf16[4,144,512]{2,1,0:T(8,128)(2,1)} %collective-permute-done.15.refs_2_), channel_id=1, source_target_pairs={{0,2},{1,3},{2,0},{3,1},{4,6},{5,7},{6,4},{7,5},{8,10},{9,11},{10,... | collective-permute-start | bytes 1769480 | tf_op jit(solution)/shard_map/ppermute | solution.py:44
  114.4 20.5 %collective-permute-start.20 = (bf16[4,144,512]{2,1,0:T(8,128)(2,1)S(1)}, bf16[4,144,512]{2,1,0:T(8,128)(2,1)}, u32[]{:S(2)}, u32[]{:S(2)}) collective-permute-start(bf16[4,144,512]{2,1,0:T(8,128)(2,1)S(1)} %shard_map.397.refs_1_), channel_id=1, source_target_pairs={{0,1},{1,0},{2,3},{3,2},{4,5},{5,4},{6,7},{7,6},{8,9},{9,8},{10,11... | collective-permute-start | bytes 1769480 | tf_op jit(solution)/shard_map/ppermute | solution.py:44
  114.4 20.5 %collective-permute-start.21 = (bf16[4,144,512]{2,1,0:T(8,128)(2,1)S(1)}, bf16[4,144,512]{2,1,0:T(8,128)(2,1)}, u32[]{:S(2)}, u32[]{:S(2)}) collective-permute-start(bf16[4,144,512]{2,1,0:T(8,128)(2,1)S(1)} %collective-permute-done.18.refs_3_), channel_id=1, source_target_pairs={{0,1},{1,0},{2,3},{3,2},{4,5},{5,4},{6,7},{7,6},{8,9},{9,8},{10,11... | collective-permute-start | bytes 1769480 | tf_op jit(solution)/shard_map/ppermute | solution.py:44
  115.7 19.1 %all-to-all-start = ((f32[32,3,512]{2,1,0:T(4,128)}), f32[32,3,512]{2,1,0:T(4,128)S(1)}, u32[]{:S(2)}, u32[]{:S(2)}) async-start(f32[32,3,512]{2,1,0:T(4,128)} %broadcast_in_dim.133), calls=%async_computation | async-start | bytes 524288 | tf_op jit(solution)/shard_map/all_to_all | solution.py:67
  155.3 12.8 %all-to-all-start.1 = ((f32[32,2,512]{2,1,0:T(2,128)}), f32[32,2,512]{2,1,0:T(2,128)S(1)}, u32[]{:S(2)}, u32[]{:S(2)}) async-start(f32[32,2,512]{2,1,0:T(2,128)} %broadcast_in_dim.134), calls=%async_computation.1 | async-start | bytes 262144 | tf_op jit(solution)/shard_map/all_to_all | solution.py:67
  184.1 4.8 collective-permute-start.27
  188.9 5.2 %collective-permute-start.28 = (f32[3,2048]{1,0:T(4,128)S(1)}, f32[3,2048]{1,0:T(4,128)S(1)}, u32[]{:S(2)}, u32[]{:S(2)}) collective-permute-start(f32[3,2048]{1,0:T(4,128)S(1)} %add_add_fusion.4), channel_id=1, source_target_pairs={{0,8},{1,9},{2,10},{3,11},{4,12},{5,13},{6,14},{7,15},{8,0},{9,1},... | collective-permute-start | bytes 73736 | tf_op jit(solution)/shard_map/ppermute | solution.py:44
  190.1 4.8 collective-permute-start.29
  192.6 5.7 %collective-permute-start.30 = (f32[3,2048]{1,0:T(4,128)S(1)}, f32[3,2048]{1,0:T(4,128)S(1)}, u32[]{:S(2)}, u32[]{:S(2)}) collective-permute-start(f32[3,2048]{1,0:T(4,128)S(1)} %add_add_fusion.4), channel_id=1, source_target_pairs={{0,24},{1,25},{2,26},{3,27},{4,28},{5,29},{6,30},{7,31},{8,16},{9,... | collective-permute-start | bytes 73736 | tf_op jit(solution)/shard_map/ppermute | solution.py:44
  227.1 5.4 %collective-permute-start.34 = (f32[3,2048]{1,0:T(4,128)S(1)}, f32[3,2048]{1,0:T(4,128)S(1)}, u32[]{:S(2)}, u32[]{:S(2)}) collective-permute-start(f32[3,2048]{1,0:T(4,128)S(1)} %add.289), channel_id=1, source_target_pairs={{0,2},{1,3},{2,0},{3,1},{4,6},{5,7},{6,4},{7,5},{8,10},{9,11},{10,... | collective-permute-start | bytes 73736 | tf_op jit(solution)/shard_map/ppermute | solution.py:44
  230.0 4.8 collective-permute-start.36
  235.9 5.2 %collective-permute-start.38 = (f32[3,2048]{1,0:T(4,128)S(1)}, f32[3,2048]{1,0:T(4,128)S(1)}, u32[]{:S(2)}, u32[]{:S(2)}) collective-permute-start(f32[3,2048]{1,0:T(4,128)S(1)} %add_add_fusion.2), channel_id=1, source_target_pairs={{0,16},{1,17},{2,18},{3,19},{4,20},{5,21},{6,22},{7,23},{8,24},{9,... | collective-permute-start | bytes 73736 | tf_op jit(solution)/shard_map/ppermute | solution.py:44
  237.6 5.7 %collective-permute-start.39 = (f32[3,2048]{1,0:T(4,128)S(1)}, f32[3,2048]{1,0:T(4,128)S(1)}, u32[]{:S(2)}, u32[]{:S(2)}) collective-permute-start(f32[3,2048]{1,0:T(4,128)S(1)} %add_add_fusion.2), channel_id=1, source_target_pairs={{0,24},{1,25},{2,26},{3,27},{4,28},{5,29},{6,30},{7,31},{8,16},{9,... | collective-permute-start | bytes 73736 | tf_op jit(solution)/shard_map/ppermute | solution.py:44
  262.0 11.3 %all-to-all-start.2 = ((f32[32,2,512]{2,1,0:T(2,128)}), f32[32,2,512]{2,1,0:T(2,128)S(1)}, u32[]{:S(2)}, u32[]{:S(2)}) async-start(f32[32,2,512]{2,1,0:T(2,128)} %broadcast_in_dim.141), calls=%async_computation.2 | async-start | bytes 262144 | tf_op jit(solution)/shard_map/all_to_all | solution.py:67
  274.7 23.6 %all-to-all-start.3 = ((bf16[32,4,512]{2,1,0:T(4,128)(2,1)}), bf16[32,4,512]{2,1,0:T(4,128)(2,1)S(1)}, u32[]{:S(2)}, u32[]{:S(2)}) async-start(bf16[32,4,512]{2,1,0:T(4,128)(2,1)} %bitcast.38), calls=%async_computation.3 | async-start | bytes 262144 | tf_op jit(solution)/shard_map/all_to_all | solution.py:1875
  299.7 23.7 %all-to-all-start.4 = ((f32[32,2,512]{2,1,0:T(2,128)}), f32[32,2,512]{2,1,0:T(2,128)S(1)}, u32[]{:S(2)}, u32[]{:S(2)}) async-start(f32[32,2,512]{2,1,0:T(2,128)} %broadcast_in_dim.142), calls=%async_computation.4 | async-start | bytes 262144 | tf_op jit(solution)/shard_map/all_to_all | solution.py:67
  305.5 163.9 %reduce-scatter.2.cloned.1.call-start = ((), (), s32[]{:S(2)}) async-start(), calls=%async_computation.7 | async-start | bytes 7667712 | tf_op jit(solution)/shard_map/reduce_scatter | solution.py:1934
  345.4 20.5 %collective-permute-start.41 = (bf16[4,2,128,256]{3,2,0,1:T(8,128)(2,1)S(1)}, bf16[4,2,128,256]{3,2,0,1:T(8,128)(2,1)S(1)}, u32[]{:S(2)}, u32[]{:S(2)}) collective-permute-start(bf16[4,2,128,256]{3,2,0,1:T(8,128)(2,1)S(1)} %fusion.7), channel_id=1, source_target_pairs={{0,2},{1,3},{2,0},{3,1},{4,6},{5,7},{6,4},{7,5},{8,10},{9,11},{10,... | collective-permute-start | bytes 1572872 | tf_op jit(solution)/shard_map/ppermute | solution.py:44
  367.9 10.2 %collective-permute-start.42 = (bf16[4,128,256]{2,1,0:T(8,128)(2,1)S(1)}, bf16[4,128,256]{2,1,0:T(8,128)(2,1)S(1)}, u32[]{:S(2)}, u32[]{:S(2)}) collective-permute-start(bf16[4,128,256]{2,1,0:T(8,128)(2,1)S(1)} %fusion.9), channel_id=1, source_target_pairs={{0,4},{1,5},{2,6},{3,7},{4,0},{5,1},{6,2},{7,3},{8,12},{9,13},{10,... | collective-permute-start | bytes 786440 | tf_op jit(solution)/shard_map/ppermute | solution.py:44
  383.3 25.4 %collective-permute-start.44 = (bf16[4,2,128,256]{3,2,0,1:T(8,128)(2,1)S(1)}, bf16[4,2,128,256]{3,2,0,1:T(8,128)(2,1)S(1)}, u32[]{:S(2)}, u32[]{:S(2)}) collective-permute-start(bf16[4,2,128,256]{3,2,0,1:T(8,128)(2,1)S(1)} %fusion.8), channel_id=1, source_target_pairs={{0,2},{1,3},{2,0},{3,1},{4,6},{5,7},{6,4},{7,5},{8,10},{9,11},{10,... | collective-permute-start | bytes 1572872 | tf_op jit(solution)/shard_map/ppermute | solution.py:44
  384.0 24.7 %collective-permute-start.45 = (bf16[128,256]{1,0:T(8,128)(2,1)S(1)}, bf16[128,256]{1,0:T(8,128)(2,1)S(1)}, u32[]{:S(2)}, u32[]{:S(2)}) collective-permute-start(bf16[128,256]{1,0:T(8,128)(2,1)S(1)} %get-tuple-element.544), channel_id=1, source_target_pairs={{0,8},{1,9},{2,10},{3,11},{4,12},{5,13},{6,14},{7,15},{8,0},{9,1},... | collective-permute-start | bytes 196616 | tf_op jit(solution)/shard_map/ppermute | solution.py:44
  385.4 23.2 %collective-permute-start.46 = (bf16[128,256]{1,0:T(8,128)(2,1)S(1)}, bf16[128,256]{1,0:T(8,128)(2,1)S(1)}, u32[]{:S(2)}, u32[]{:S(2)}) collective-permute-start(bf16[128,256]{1,0:T(8,128)(2,1)S(1)} %get-tuple-element.545), channel_id=1, source_target_pairs={{0,16},{1,17},{2,18},{3,19},{4,20},{5,21},{6,22},{7,23},{8,24},{9,... | collective-permute-start | bytes 196616 | tf_op jit(solution)/shard_map/ppermute | solution.py:44
  387.8 20.8 %collective-permute-start.47 = (bf16[128,256]{1,0:T(8,128)(2,1)S(1)}, bf16[128,256]{1,0:T(8,128)(2,1)S(1)}, u32[]{:S(2)}, u32[]{:S(2)}) collective-permute-start(bf16[128,256]{1,0:T(8,128)(2,1)S(1)} %get-tuple-element.546), channel_id=1, source_target_pairs={{0,24},{1,25},{2,26},{3,27},{4,28},{5,29},{6,30},{7,31},{8,16},{9,... | collective-permute-start | bytes 196616 | tf_op jit(solution)/shard_map/ppermute | solution.py:44
  410.7 10.9 %collective-permute-start.48 = (bf16[4,128,256]{2,1,0:T(8,128)(2,1)S(1)}, bf16[4,128,256]{2,1,0:T(8,128)(2,1)S(1)}, u32[]{:S(2)}, u32[]{:S(2)}) collective-permute-start(bf16[4,128,256]{2,1,0:T(8,128)(2,1)S(1)} %fusion.10), channel_id=1, source_target_pairs={{0,4},{1,5},{2,6},{3,7},{4,0},{5,1},{6,2},{7,3},{8,12},{9,13},{10,... | collective-permute-start | bytes 786440 | tf_op jit(solution)/shard_map/ppermute | solution.py:44
  411.0 10.6 %collective-permute-start.49 = (bf16[128,256]{1,0:T(8,128)(2,1)S(1)}, bf16[128,256]{1,0:T(8,128)(2,1)S(1)}, u32[]{:S(2)}, u32[]{:S(2)}) collective-permute-start(bf16[128,256]{1,0:T(8,128)(2,1)S(1)} %fusion.20), channel_id=1, source_target_pairs={{0,1},{1,0},{2,3},{3,2},{4,5},{5,4},{6,7},{7,6},{8,9},{9,8},{10,11... | collective-permute-start | bytes 196616 | tf_op jit(solution)/shard_map/ppermute | solution.py:44
  411.0 10.6 %collective-permute-start.50 = (bf16[128,256]{1,0:T(8,128)(2,1)S(1)}, bf16[128,256]{1,0:T(8,128)(2,1)S(1)}, u32[]{:S(2)}, u32[]{:S(2)}) collective-permute-start(bf16[128,256]{1,0:T(8,128)(2,1)S(1)} %fusion.20), channel_id=1, source_target_pairs={{0,2},{1,3},{2,0},{3,1},{4,6},{5,7},{6,4},{7,5},{8,10},{9,11},{10,... | collective-permute-start | bytes 196616 | tf_op jit(solution)/shard_map/ppermute | solution.py:44
  412.7 9.0 %collective-permute-start.51 = (bf16[128,256]{1,0:T(8,128)(2,1)S(1)}, bf16[128,256]{1,0:T(8,128)(2,1)S(1)}, u32[]{:S(2)}, u32[]{:S(2)}) collective-permute-start(bf16[128,256]{1,0:T(8,128)(2,1)S(1)} %fusion.20), channel_id=1, source_target_pairs={{0,3},{1,2},{2,1},{3,0},{4,7},{5,6},{6,5},{7,4},{8,11},{9,10},{10,... | collective-permute-start | bytes 196616 | tf_op jit(solution)/shard_map/ppermute | solution.py:44
  426.5 17.1 %collective-permute-start.53 = (bf16[4,2,128,256]{3,2,1,0:T(8,128)(2,1)S(1)}, bf16[4,2,128,256]{3,2,1,0:T(8,128)(2,1)S(1)}, u32[]{:S(2)}, u32[]{:S(2)}) collective-permute-start(bf16[4,2,128,256]{3,2,1,0:T(8,128)(2,1)S(1)} %fusion.6), channel_id=1, source_target_pairs={{0,2},{1,3},{2,0},{3,1},{4,6},{5,7},{6,4},{7,5},{8,10},{9,11},{10,... | collective-permute-start | bytes 1572872 | tf_op jit(solution)/shard_map/ppermute | solution.py:44
  428.3 15.3 %collective-permute-start.54 = (bf16[128,256]{1,0:T(8,128)(2,1)S(1)}, bf16[128,256]{1,0:T(8,128)(2,1)S(1)}, u32[]{:S(2)}, u32[]{:S(2)}) collective-permute-start(bf16[128,256]{1,0:T(8,128)(2,1)S(1)} %get-tuple-element.576), channel_id=1, source_target_pairs={{0,8},{1,9},{2,10},{3,11},{4,12},{5,13},{6,14},{7,15},{8,0},{9,1},... | collective-permute-start | bytes 196616 | tf_op jit(solution)/shard_map/ppermute | solution.py:44
  428.8 14.7 %collective-permute-start.55 = (bf16[128,256]{1,0:T(8,128)(2,1)S(1)}, bf16[128,256]{1,0:T(8,128)(2,1)S(1)}, u32[]{:S(2)}, u32[]{:S(2)}) collective-permute-start(bf16[128,256]{1,0:T(8,128)(2,1)S(1)} %get-tuple-element.577), channel_id=1, source_target_pairs={{0,16},{1,17},{2,18},{3,19},{4,20},{5,21},{6,22},{7,23},{8,24},{9,... | collective-permute-start | bytes 196616 | tf_op jit(solution)/shard_map/ppermute | solution.py:44
  432.1 11.5 %collective-permute-start.56 = (bf16[128,256]{1,0:T(8,128)(2,1)S(1)}, bf16[128,256]{1,0:T(8,128)(2,1)S(1)}, u32[]{:S(2)}, u32[]{:S(2)}) collective-permute-start(bf16[128,256]{1,0:T(8,128)(2,1)S(1)} %get-tuple-element.578), channel_id=1, source_target_pairs={{0,24},{1,25},{2,26},{3,27},{4,28},{5,29},{6,30},{7,31},{8,16},{9,... | collective-permute-start | bytes 196616 | tf_op jit(solution)/shard_map/ppermute | solution.py:44
  448.5 19.8 %collective-permute-start.57 = (bf16[4,128,256]{2,1,0:T(8,128)(2,1)S(1)}, bf16[4,128,256]{2,1,0:T(8,128)(2,1)S(1)}, u32[]{:S(2)}, u32[]{:S(2)}) collective-permute-start(bf16[4,128,256]{2,1,0:T(8,128)(2,1)S(1)} %fusion.11), channel_id=1, source_target_pairs={{0,4},{1,5},{2,6},{3,7},{4,0},{5,1},{6,2},{7,3},{8,12},{9,13},{10,... | collective-permute-start | bytes 786440 | tf_op jit(solution)/shard_map/ppermute | solution.py:44
  450.1 18.1 %collective-permute-start.58 = (bf16[128,256]{1,0:T(8,128)(2,1)S(1)}, bf16[128,256]{1,0:T(8,128)(2,1)S(1)}, u32[]{:S(2)}, u32[]{:S(2)}) collective-permute-start(bf16[128,256]{1,0:T(8,128)(2,1)S(1)} %fusion.17), channel_id=1, source_target_pairs={{0,1},{1,0},{2,3},{3,2},{4,5},{5,4},{6,7},{7,6},{8,9},{9,8},{10,11... | collective-permute-start | bytes 196616 | tf_op jit(solution)/shard_map/ppermute | solution.py:44
  450.1 18.1 %collective-permute-start.59 = (bf16[128,256]{1,0:T(8,128)(2,1)S(1)}, bf16[128,256]{1,0:T(8,128)(2,1)S(1)}, u32[]{:S(2)}, u32[]{:S(2)}) collective-permute-start(bf16[128,256]{1,0:T(8,128)(2,1)S(1)} %fusion.17), channel_id=1, source_target_pairs={{0,2},{1,3},{2,0},{3,1},{4,6},{5,7},{6,4},{7,5},{8,10},{9,11},{10,... | collective-permute-start | bytes 196616 | tf_op jit(solution)/shard_map/ppermute | solution.py:44
  450.7 17.5 %collective-permute-start.60 = (bf16[128,256]{1,0:T(8,128)(2,1)S(1)}, bf16[128,256]{1,0:T(8,128)(2,1)S(1)}, u32[]{:S(2)}, u32[]{:S(2)}) collective-permute-start(bf16[128,256]{1,0:T(8,128)(2,1)S(1)} %fusion.17), channel_id=1, source_target_pairs={{0,3},{1,2},{2,1},{3,0},{4,7},{5,6},{6,5},{7,4},{8,11},{9,10},{10,... | collective-permute-start | bytes 196616 | tf_op jit(solution)/shard_map/ppermute | solution.py:44
  451.9 17.2 %all-to-all-start.5 = ((f32[8,40,256]{2,1,0:T(8,128)}), f32[8,40,256]{2,1,0:T(8,128)S(1)}, u32[]{:S(2)}, u32[]{:S(2)}) async-start(f32[8,40,256]{2,1,0:T(8,128)} %select_maximum_fusion), calls=%async_computation.5 | async-start | bytes 655360 | tf_op jit(solution)/shard_map/all_to_all | solution.py:1975
  470.9 4.8 collective-permute-start.62
  472.7 6.2 %collective-permute-start.64 = (bf16[128,256]{1,0:T(8,128)(2,1)S(1)}, bf16[128,256]{1,0:T(8,128)(2,1)S(1)}, u32[]{:S(2)}, u32[]{:S(2)}) collective-permute-start(bf16[128,256]{1,0:T(8,128)(2,1)S(1)} %get-tuple-element.605), channel_id=1, source_target_pairs={{0,8},{1,9},{2,10},{3,11},{4,12},{5,13},{6,14},{7,15},{8,0},{9,1},... | collective-permute-start | bytes 196616 | tf_op jit(solution)/shard_map/ppermute | solution.py:44
  474.7 10.4 %collective-permute-start.67 = (bf16[208,512]{1,0:T(8,128)(2,1)S(1)}, bf16[208,512]{1,0:T(8,128)(2,1)S(1)}, u32[]{:S(2)}, u32[]{:S(2)}) collective-permute-start(bf16[208,512]{1,0:T(8,128)(2,1)S(1)} %get-tuple-element.608), channel_id=1, source_target_pairs={{0,1},{1,0},{2,3},{3,2},{4,5},{5,4},{6,7},{7,6},{8,9},{9,8},{10,11... | collective-permute-start | bytes 638984 | tf_op jit(solution)/shard_map/ppermute | solution.py:44
  474.8 10.3 %collective-permute-start.68 = (bf16[208,512]{1,0:T(8,128)(2,1)S(1)}, bf16[208,512]{1,0:T(8,128)(2,1)S(1)}, u32[]{:S(2)}, u32[]{:S(2)}) collective-permute-start(bf16[208,512]{1,0:T(8,128)(2,1)S(1)} %get-tuple-element.609), channel_id=1, source_target_pairs={{0,2},{1,3},{2,0},{3,1},{4,6},{5,7},{6,4},{7,5},{8,10},{9,11},{10,... | collective-permute-start | bytes 638984 | tf_op jit(solution)/shard_map/ppermute | solution.py:44
  475.7 10.8 %collective-permute-start.69 = (bf16[208,512]{1,0:T(8,128)(2,1)S(1)}, bf16[208,512]{1,0:T(8,128)(2,1)S(1)}, u32[]{:S(2)}, u32[]{:S(2)}) collective-permute-start(bf16[208,512]{1,0:T(8,128)(2,1)S(1)} %get-tuple-element.610), channel_id=1, source_target_pairs={{0,3},{1,2},{2,1},{3,0},{4,7},{5,6},{6,5},{7,4},{8,11},{9,10},{10,... | collective-permute-start | bytes 638984 | tf_op jit(solution)/shard_map/ppermute | solution.py:44
  476.6 7.7 %collective-permute-start.65 = (bf16[128,256]{1,0:T(8,128)(2,1)S(1)}, bf16[128,256]{1,0:T(8,128)(2,1)S(1)}, u32[]{:S(2)}, u32[]{:S(2)}) collective-permute-start(bf16[128,256]{1,0:T(8,128)(2,1)S(1)} %get-tuple-element.606), channel_id=1, source_target_pairs={{0,16},{1,17},{2,18},{3,19},{4,20},{5,21},{6,22},{7,23},{8,24},{9,... | collective-permute-start | bytes 196616 | tf_op jit(solution)/shard_map/ppermute | solution.py:44
  478.9 6.1 %collective-permute-start.66 = (bf16[128,256]{1,0:T(8,128)(2,1)S(1)}, bf16[128,256]{1,0:T(8,128)(2,1)S(1)}, u32[]{:S(2)}, u32[]{:S(2)}) collective-permute-start(bf16[128,256]{1,0:T(8,128)(2,1)S(1)} %get-tuple-element.607), channel_id=1, source_target_pairs={{0,24},{1,25},{2,26},{3,27},{4,28},{5,29},{6,30},{7,31},{8,16},{9,... | collective-permute-start | bytes 196616 | tf_op jit(solution)/shard_map/ppermute | solution.py:44
  486.6 14.5 %collective-permute-start.73 = (bf16[208,512]{1,0:T(8,128)(2,1)S(1)}, bf16[208,512]{1,0:T(8,128)(2,1)}, u32[]{:S(2)}, u32[]{:S(2)}) collective-permute-start(bf16[208,512]{1,0:T(8,128)(2,1)S(1)} %add_convert_fusion), channel_id=1, source_target_pairs={{0,1},{1,0},{2,3},{3,2},{4,5},{5,4},{6,7},{7,6},{8,9},{9,8},{10,11... | collective-permute-start | bytes 638984 | tf_op jit(solution)/shard_map/ppermute | solution.py:44
  487.0 14.2 %collective-permute-start.74 = (bf16[208,512]{1,0:T(8,128)(2,1)S(1)}, bf16[208,512]{1,0:T(8,128)(2,1)}, u32[]{:S(2)}, u32[]{:S(2)}) collective-permute-start(bf16[208,512]{1,0:T(8,128)(2,1)S(1)} %add_convert_fusion), channel_id=1, source_target_pairs={{0,2},{1,3},{2,0},{3,1},{4,6},{5,7},{6,4},{7,5},{8,10},{9,11},{10,... | collective-permute-start | bytes 638984 | tf_op jit(solution)/shard_map/ppermute | solution.py:44
  487.9 13.3 %collective-permute-start.75 = (bf16[208,512]{1,0:T(8,128)(2,1)S(1)}, bf16[208,512]{1,0:T(8,128)(2,1)}, u32[]{:S(2)}, u32[]{:S(2)}) collective-permute-start(bf16[208,512]{1,0:T(8,128)(2,1)S(1)} %add_convert_fusion), channel_id=1, source_target_pairs={{0,3},{1,2},{2,1},{3,0},{4,7},{5,6},{6,5},{7,4},{8,11},{9,10},{10,... | collective-permute-start | bytes 638984 | tf_op jit(solution)/shard_map/ppermute | solution.py:44
  489.1 11.9 %collective-permute-start.71 = (bf16[128,256]{1,0:T(8,128)(2,1)S(1)}, bf16[128,256]{1,0:T(8,128)(2,1)S(1)}, u32[]{:S(2)}, u32[]{:S(2)}) collective-permute-start(bf16[128,256]{1,0:T(8,128)(2,1)S(1)} %fusion.14), channel_id=1, source_target_pairs={{0,2},{1,3},{2,0},{3,1},{4,6},{5,7},{6,4},{7,5},{8,10},{9,11},{10,... | collective-permute-start | bytes 196616 | tf_op jit(solution)/shard_map/ppermute | solution.py:44
  490.6 10.5 %collective-permute-start.72 = (bf16[128,256]{1,0:T(8,128)(2,1)S(1)}, bf16[128,256]{1,0:T(8,128)(2,1)}, u32[]{:S(2)}, u32[]{:S(2)}) collective-permute-start(bf16[128,256]{1,0:T(8,128)(2,1)S(1)} %fusion.14), channel_id=1, source_target_pairs={{0,3},{1,2},{2,1},{3,0},{4,7},{5,6},{6,5},{7,4},{8,11},{9,10},{10,... | collective-permute-start | bytes 196616 | tf_op jit(solution)/shard_map/ppermute | solution.py:44
  (56 other events, 438.6 us)
Sparse Core Ops, SparseCore 0:
  95.7 62.3 all-gather.2
  324.1 133.8 reduce-scatter.1

commit v2 on v1

--- a/solution.py
+++ b/solution.py
@@ -61,10 +61,26 @@
     return values
 
 
-def swap_total(values):
-    size = lax.axis_size(AXES)
-    copies = jnp.broadcast_to(values[None], (size,) + values.shape)
+def total_beside(values, run, inputs):
+    bits = lax.axis_size(AXES).bit_length() - 1
+    values = values + exchange(values, 1)
+    for bit in range(1, bits, 2):
+        masks = [1 << bit] + ([2 << bit, 3 << bit] if bit + 1 < bits else [])
+        if bit == 3:
+            out, parts, _ = beside(run, inputs, [(values, mask) for mask in masks])
+        else:
+            parts = [exchange(values, mask) for mask in masks]
+        for part in parts:
+            values = values + part
+    return values, out
+
+
+def swap_total(copies):
     return jnp.sum(lax.all_to_all(copies, AXES, 0, 0, tiled=True), 0)
+
+
+def to_all(values):
+    return jnp.broadcast_to(values[None], (lax.axis_size(AXES),) + values.shape)
 
 
 def beside(run, inputs, sends, more=()):
@@ -136,7 +152,7 @@
         return [(self.send, 1)]
 
     def take_core(self, came):
-        self.values = (self.keep + came[0].astype(f32)).reshape(self.shape)
+        self.values = (self.keep.astype(f32) + came[0].astype(f32)).reshape(self.shape)
 
     def split(self, letter):
         place = self.lead + self.axes.index(letter)
@@ -203,7 +219,7 @@
     return as_blocks(squeeze), as_blocks(pair), spatial, late
 
 
-def reduced(buffer, reduce_half, expand_half, squeeze_half):
+def reduced(buffers, reduce_half, expand_half, squeeze_half):
     def whole(half, grain):
         keep, send = (part.astype(bf16) for part in half)
         shape = keep.shape[:1] + (-1, grain) + keep.shape[2:]
@@ -217,8 +233,10 @@
     def columns(tiles):
         return tiles.swapaxes(0, 1).reshape(tiles.shape[1], -1)
 
-    restore = buffer[:, :RESTORE_ROWS].reshape(8, 4, RESTORE_ROWS, WIDE).swapaxes(1, 2).reshape(B, C)
-    spatial = buffer[:, RESTORE_ROWS:].reshape(32, 9, 16, B).swapaxes(0, 1).reshape(9, B, B)
+    shared = jnp.stack([part.reshape(16, SHARED, 16, WIDE) for part in buffers], axis=1)
+    shared = shared.transpose(2, 0, 1, 3, 4).reshape(SHARED, B, WIDE)
+    restore = shared[:GROUPS].swapaxes(0, 1).reshape(B, C)
+    spatial = shared[GROUPS:]
     return (
         scattered(restore, 0),
         scattered(spatial, 1),
@@ -420,6 +438,14 @@
 
 def first_step():
     return pl.program_id(0) == 0
+
+
+def store_copies(copies_ref, sums):
+    @pl.when(pl.program_id(0) == pl.num_programs(0) - 1)
+    def _():
+        values = sums[...]
+        for index in range(copies_ref.shape[0]):
+            copies_ref[index] = values
 
 
 def add_moments(sums_ref, where, first, second):
@@ -569,8 +595,8 @@
 
 def second_kernel(count, me_ref, *refs):
     blocks, refs = refs[:8], refs[8:]
-    pre_ref, in_sums_ref, affine_ref, hidden_ref, out_ref, sums_ref, *refs = refs
-    natural, padded, tile, spatial_ref, semaphores = refs
+    pre_ref, in_sums_ref, affine_ref, hidden_ref, out_ref, copies_ref, *refs = refs
+    natural, padded, tile, spatial_ref, sums_ref, semaphores = refs
     copies = block_copies(me_ref[0], blocks, spatial_ref, semaphores)
 
     @pl.when(first_step())
@@ -628,10 +654,12 @@
         first = first + fold(value)
         second = second + fold(value * value)
     add_moments(sums_ref, slice(0, B), first, second)
+    store_copies(copies_ref, sums_ref)
 
 
 def second_block(me, spatial, pre_one, sums, affine, count):
     rows = pre_one.shape[0]
+    devices = lax.axis_size(AXES)
     steps = rows // HALF
     deep = HALF + 2 * SIDE * 16
     return kernel_call(
@@ -639,11 +667,12 @@
         steps,
         [SCALAR] + [ANY] * 8 + [half_spec(B), whole_spec(sums.shape), whole_spec((2, B))],
         [pl.BlockSpec((1, deep, 3 * B), lambda step: (step, 0, 0)), half_spec(B),
-         whole_out((2, B))],
+         whole_out((devices, 2, B))],
         [jax.ShapeDtypeStruct((steps, deep, 3 * B), bf16), jax.ShapeDtypeStruct((rows, B), f32),
-         jax.ShapeDtypeStruct((2, B), f32)],
+         jax.ShapeDtypeStruct((devices, 2, B), f32)],
         [pltpu.VMEM((HALF, LANES), f32), pltpu.VMEM((PADDED * PADDED, 16, LANES), bf16),
          pltpu.VMEM((HALF, B), f32), pltpu.VMEM((32, SPATIAL_ROWS, B), bf16),
+         pltpu.VMEM((2, B), f32),
          pltpu.SemaphoreType.DMA((32,))],
         18 * rows * B * B,
         2 * rows * B,
@@ -865,7 +894,7 @@
 
 def fifth_kernel(count, slope_ref, pre_three_ref, centre_ref, pooled_ref, sums_three_ref, affine_three_ref,
                  grads_three_ref, late_ref, pre_two_ref, sums_two_ref, affine_two_ref,
-                 low_ref, out_ref, sums_ref, natural, restore_ref, semaphore):
+                 low_ref, out_ref, copies_ref, natural, restore_ref, sums_ref, semaphore):
     copy = restore_copy(late_ref, restore_ref, semaphore)
 
     @pl.when(first_step())
@@ -921,11 +950,13 @@
         return carry
 
     lax.fori_loop(0, 4, slope_step, 0)
+    store_copies(copies_ref, sums_ref)
 
 
 def fifth_block(slope, pre_three, centres, pooled, sums_three, affine_three, grads_three, late,
                 pre_two, sums_two, affine_two, count, after=()):
     rows = slope.shape[0]
+    devices = lax.axis_size(AXES)
     return kernel_call(
         functools.partial(fifth_kernel, count),
         rows // HALF,
@@ -933,10 +964,11 @@
          pl.BlockSpec((1, 2, C), lambda step: (step, 0, 0)),
          whole_spec(sums_three.shape), whole_spec((2, C)), whole_spec(grads_three.shape), ANY,
          half_spec(B), whole_spec(sums_two.shape), whole_spec((2, B))],
-        [half_spec(C), half_spec(B), whole_out((2, B))],
+        [half_spec(C), half_spec(B), whole_out((devices, 2, B))],
         [jax.ShapeDtypeStruct((rows, C), bf16), jax.ShapeDtypeStruct((rows, B), f32),
-         jax.ShapeDtypeStruct((2, B), f32)],
+         jax.ShapeDtypeStruct((devices, 2, B), f32)],
         [pltpu.VMEM((4, HALF, LANES), f32), pltpu.VMEM((32, RESTORE_ROWS, B), bf16),
+         pltpu.VMEM((2, B), f32),
          pltpu.SemaphoreType.DMA(())],
         2 * rows * B * C,
         2 * rows * B,
@@ -948,8 +980,8 @@
 def sixth_kernel(count, me_ref, *refs):
     blocks, refs = refs[:8], refs[8:]
     grad_ref, pre_two_ref, sums_two_ref, affine_two_ref, grads_two_ref, *refs = refs
-    pre_one_ref, sums_one_ref, affine_one_ref, low_ref, out_ref, sums_ref, *refs = refs
-    padded, shifted, tile, natural, spatial_ref, semaphores = refs
+    pre_one_ref, sums_one_ref, affine_one_ref, low_ref, out_ref, copies_ref, *refs = refs
+    padded, shifted, tile, natural, spatial_ref, sums_ref, semaphores = refs
     border = SIDE * 16
     copies = block_copies(me_ref[0], blocks, spatial_ref, semaphores)
 
@@ -1025,11 +1057,13 @@
         return carry
 
     lax.fori_loop(0, 4, slope_step, 0)
+    store_copies(copies_ref, sums_ref)
 
 
 def sixth_block(me, spatial, grad, pre_two, sums_two, affine_two, grads_two, pre_one, sums_one,
                 affine_one, count):
     rows = grad.shape[0]
+    devices = lax.axis_size(AXES)
     deep = HALF + 2 * SIDE * 16
     return kernel_call(
         functools.partial(sixth_kernel, count),
@@ -1037,12 +1071,13 @@
         [SCALAR] + [ANY] * 8 + [half_spec(B), half_spec(B), whole_spec(sums_two.shape),
          whole_spec((2, B)), whole_spec(grads_two.shape), half_spec(B), whole_spec(sums_one.shape),
          whole_spec((2, B))],
-        [half_spec(B), half_spec(B), whole_out((2, B))],
+        [half_spec(B), half_spec(B), whole_out((devices, 2, B))],
         [jax.ShapeDtypeStruct((rows, B), bf16), jax.ShapeDtypeStruct((rows, B), f32),
-         jax.ShapeDtypeStruct((2, B), f32)],
+         jax.ShapeDtypeStruct((devices, 2, B), f32)],
         [pltpu.VMEM((PADDED * PADDED, 16, LANES), bf16), pltpu.VMEM((deep, 3 * B), bf16),
          pltpu.VMEM((HALF, B), f32), pltpu.VMEM((4, HALF, LANES), f32),
-         pltpu.VMEM((32, SPATIAL_ROWS, B), bf16), pltpu.SemaphoreType.DMA((32,))],
+         pltpu.VMEM((32, SPATIAL_ROWS, B), bf16),
+         pltpu.VMEM((2, B), f32), pltpu.SemaphoreType.DMA((32,))],
         18 * rows * B * B,
         2 * rows * B,
     )(me, *spatial, grad, pre_two, sums_two, affine_two, grads_two, pre_one, sums_one,
@@ -1095,7 +1130,7 @@
          pl.BlockSpec((rows, 2 * TILE), lambda step: (0, step))],
         [whole_out(grad.shape), half, half],
         [jax.ShapeDtypeStruct(grad.shape, bf16),
-         jax.ShapeDtypeStruct((blocks, inner // 2, TILE), f32),
+         jax.ShapeDtypeStruct((blocks, inner // 2, TILE), bf16),
          jax.ShapeDtypeStruct((blocks, inner // 2, TILE), bf16)],
         [pltpu.VMEM((inner, rows), bf16), pltpu.VMEM((inner, rows), bf16)],
         2 * rows * inner * wide_values.shape[1],
@@ -1277,7 +1312,7 @@
     half = found.shape[0] // 2
     for tile in range(2):
         at = slice(tile * TILE, (tile + 1) * TILE)
-        keep_ref[tile, 0:half] = found[0:half, at]
+        keep_ref[tile, 0:half] = found[0:half, at].astype(bf16)
         send_ref[tile, 0:half] = found[half:, at].astype(bf16)
 
 
@@ -1298,8 +1333,7 @@
         blocks // 2,
         [SCALAR, whole_spec((rows, inner)), pl.BlockSpec((rows, 2 * TILE), lambda step: (0, step))],
         [half, half],
-        [jax.ShapeDtypeStruct((blocks, inner // 2, TILE), f32),
-         jax.ShapeDtypeStruct((blocks, inner // 2, TILE), bf16)],
+        [jax.ShapeDtypeStruct((blocks, inner // 2, TILE), bf16)] * 2,
         [pltpu.VMEM((inner, rows), bf16), pltpu.VMEM((inner, rows), bf16)],
         2 * rows * inner * wide_values.shape[1],
     )(me, narrow_values, wide_values)
@@ -1312,29 +1346,39 @@
 FEW_ROWS = 40
 
 
-def restore_outer_kernel(narrow_ref, wide_ref, out_ref, turned):
+SHARED = GROUPS + 9
+
+
+def store_shared(found, keep_ref, send_ref):
+    half = found.shape[0] // 2
+    keep_ref[...] = found[:half].astype(bf16).reshape(16, 16, WIDE)
+    send_ref[...] = found[half:].astype(bf16).reshape(16, 16, WIDE)
+
+
+def restore_outer_kernel(me_ref, narrow_ref, wide_ref, keep_ref, send_ref, plain, turned):
     @pl.when(first_step())
     def _():
-        turned[...] = narrow_ref[...].T
-
-    found = product(turned[...], wide_ref[...])
-    out_ref[:, 0] = found.astype(bf16).reshape(8, RESTORE_ROWS, WIDE)
-
-
-def restore_outer_block(hidden, low_three):
+        turn(me_ref[0], narrow_ref[...], 16, plain, turned)
+
+    store_shared(product(turned[...], wide_ref[...]), keep_ref, send_ref)
+
+
+def restore_outer_block(me, hidden, low_three):
     rows = hidden.shape[0]
+    out = pl.BlockSpec((16, 16, WIDE), lambda step: (0, step, 0))
     return kernel_call(
         restore_outer_kernel,
         GROUPS,
-        [whole_spec((rows, B)), pl.BlockSpec((rows, WIDE), lambda step: (0, step))],
-        pl.BlockSpec((8, 1, RESTORE_ROWS, WIDE), lambda step: (0, step, 0, 0)),
-        jax.ShapeDtypeStruct((8, 4, RESTORE_ROWS + SPATIAL_ROWS, WIDE), bf16),
-        [pltpu.VMEM((B, rows), bf16)],
+        [SCALAR, whole_spec((rows, B)), pl.BlockSpec((rows, WIDE), lambda step: (0, step))],
+        [out, out],
+        [jax.ShapeDtypeStruct((16, 16 * SHARED, WIDE), bf16)] * 2,
+        [pltpu.VMEM((B, rows), bf16), pltpu.VMEM((B, rows), bf16)],
         2 * rows * B * C,
-    )(hidden, low_three)
-
-
-def spatial_kernel(buffer_ref, hidden_ref, low_ref, out_ref, turned, padded):
+    )(me, hidden, low_three)
+
+
+def spatial_kernel(me_ref, kept_ref, sent_ref, hidden_ref, low_ref, keep_ref, send_ref, plain,
+                   turned, padded):
     border = SIDE * 16
     halves = hidden_ref.shape[0]
 
@@ -1350,31 +1394,31 @@
     @pl.when(step % 3 == 0)
     def _():
         for half in range(halves):
-            turned[half] = hidden_ref[half].T
+            turn(me_ref[0], hidden_ref[half], 16, plain, turned.at[half])
 
     top = pl.multiple_of((2 - step % 3) * border, 16)
     found = None
     for half in range(halves):
         part = product(turned[half], padded[half, pl.ds(top, HALF + 2 * border)])
         found = part if found is None else found + part
-    out_ref[...] = found.astype(bf16).reshape(32, 16, B)
-
-
-def spatial_block(buffer, hidden, low_two):
+    store_shared(found, keep_ref, send_ref)
+
+
+def spatial_block(me, buffers, hidden, low_two):
     halves, deep, _ = hidden.shape
-    first = RESTORE_ROWS // 16
+    out = pl.BlockSpec((16, 16, B), lambda step: (0, GROUPS + (step % 3) * 3 + step // 3, 0))
     return kernel_call(
         spatial_kernel,
         9,
-        [ANY, pl.BlockSpec((halves, deep, B), lambda step: (0, 0, step // 3)),
+        [SCALAR, ANY, ANY, pl.BlockSpec((halves, deep, B), lambda step: (0, 0, step // 3)),
          whole_spec(low_two.shape)],
-        pl.BlockSpec((32, 16, B), lambda step: (0, first + (step % 3) * 3 + step // 3, 0)),
-        jax.ShapeDtypeStruct(buffer.shape, bf16),
-        [pltpu.VMEM((halves, B, deep), bf16),
+        [out, out],
+        [jax.ShapeDtypeStruct(buffers[0].shape, bf16)] * 2,
+        [pltpu.VMEM((B, deep), bf16), pltpu.VMEM((halves, B, deep), bf16),
          pltpu.VMEM((halves, deep + 2 * SIDE * 16, B), bf16)],
         18 * low_two.shape[0] * B * B,
-        aliases={0: 0},
-    )(buffer, hidden, low_two)
+        aliases={1: 0, 2: 1},
+    )(me, *buffers, hidden, low_two)
 
 
 STEM = 64
@@ -1541,7 +1585,7 @@
 
 
 def stem_back_kernel(count, input_ref, select_ref, pre_ref, in_sums_ref, affine_ref, grad_ref,
-                     grads_ref, out_ref, low):
+                     grads_ref, kernels_ref, out_ref, low):
     def low_step(step, carry):
         where = lanes(step, LANES)
         mean, inverse, gain, _ = constants(in_sums_ref[:, where], affine_ref[:, where], count)
@@ -1559,37 +1603,52 @@
 
     lax.fori_loop(0, STEM_LANES // LANES, low_step, 0)
     selects = jnp.concatenate([select_ref[pair] for pair in range(PAIRS)], axis=1)
+    pieces = []
     for offset in range(WINDOW):
         band = product(stem_rows(input_ref, offset).T, low[...]).astype(bf16)
         lined = [band[:, pair * LANES : (pair + 1) * LANES] for pair in range(PAIRS)]
-        out_ref[offset] = product(selects, jnp.concatenate(lined, axis=0))
-
-
-def stem_back_block(inputs, select, pre, sums, affine, grad, grads, count, after=()):
+        found = product(selects, jnp.concatenate(lined, axis=0))
+        found = found[:LANES, :STEM] + found[LANES:, STEM:]
+        pieces.append(found[: WINDOW * CHANNELS])
+    pieces.append(jnp.zeros((3 * TILE - WINDOW * WINDOW * CHANNELS, STEM), f32))
+    turned = jnp.concatenate(pieces, axis=0).T
+    out_ref[...] = jnp.zeros_like(out_ref)
+    own = R // 8
+    for index in range(8):
+        for piece in range(3):
+            out_ref[index, piece * 8 : piece * 8 + 8] = turned[
+                index * 8 : index * 8 + 8, piece * TILE : (piece + 1) * TILE
+            ]
+        for kind in range(2):
+            out_ref[index, 24:33, kind * LANES : kind * LANES + own] = kernels_ref[
+                9 * kind : 9 * kind + 9, index * own : (index + 1) * own
+            ]
+
+
+def stem_back_block(inputs, select, pre, sums, affine, grad, grads, kernel_grads, count):
     shape = pre.shape
-    out = (WINDOW, 2 * LANES, LANES)
+    out = (8, FEW_ROWS, TILE)
     return kernel_call(
         functools.partial(stem_back_kernel, count),
         1,
         [whole_spec(inputs.shape), whole_spec(select.shape), whole_spec(shape),
          whole_spec(sums.shape), whole_spec(affine.shape), whole_spec(shape),
-         whole_spec(grads.shape)],
+         whole_spec(grads.shape), whole_spec(kernel_grads.shape)],
         whole_out(out),
         jax.ShapeDtypeStruct(out, f32),
         [pltpu.VMEM(shape, bf16)],
         2 * WINDOW * shape[0] * INPUT_LANES * STEM_LANES,
-        after=after,
-    )(inputs, select, pre, sums, affine, grad, grads)
+    )(inputs, select, pre, sums, affine, grad, grads, kernel_grads)
 
 
 SMALL_ROWS = 32
 FIRST_ROWS = 64 + SMALL_ROWS
 
 
-def cut_kernel(me_ref, squeeze_ref, expand_ref, reduce_ref, spatial_ref, restore_ref, class_ref,
+def cut_kernel(me_ref, squeeze_ref, expand_ref, reduce_ref, spatial_ref,
                stem_ref, next_ref, scale_ref, outer_ref, gain_one_ref, shift_one_ref,
                gain_two_ref, shift_two_ref, stem_gain_ref, stem_shift_ref,
-               first_out, pair_out, spatial_out, late_out, small):
+               first_out, pair_out, spatial_out, small):
     part = me_ref[0] & 3
     first_out[0:64] = squeeze_ref[pl.ds(pl.multiple_of(part * 64, 64), 64)]
     small[...] = jnp.zeros_like(small)
@@ -1613,14 +1672,30 @@
         spatial_out[tap * 16 : tap * 16 + 16] = spatial_ref[
             tap, pl.ds(pl.multiple_of(part * 16, 16), 16)
         ]
+
+
+def late_cut_kernel(me_ref, restore_ref, class_ref, late_out):
+    part = me_ref[0] & 3
     late_out[0:RESTORE_ROWS] = restore_ref[:, pl.ds(pl.multiple_of(part * B, B), B)]
     for half in range(2):
         rows = pl.ds(pl.multiple_of(part * 64 + half * 32, 32), 32)
         late_out[RESTORE_ROWS:, half * TILE : (half + 1) * TILE] = class_ref[rows]
 
 
+def late_cut_block(me, restore, classes):
+    return kernel_call(
+        late_cut_kernel,
+        1,
+        [SCALAR, whole_spec(restore.shape), whole_spec(classes.shape)],
+        whole_out((LATE_ROWS, B)),
+        jax.ShapeDtypeStruct((LATE_ROWS, B), bf16),
+        [],
+        1000000,
+    )(me, restore, classes)
+
+
 def cut_block(me, *weights):
-    shapes = [(FIRST_ROWS, B), (2 * PAIR_ROWS, B), (SPATIAL_ROWS, B), (LATE_ROWS, B)]
+    shapes = [(FIRST_ROWS, B), (2 * PAIR_ROWS, B), (SPATIAL_ROWS, B)]
     return kernel_call(
         cut_kernel,
         1,
@@ -1730,14 +1805,17 @@
     inner_width = gain_one.shape[0]
     outer_width = gain_three.shape[0]
 
+    def by_segment(values):
+        values = values.reshape(STEM_SIDE, segments, STEM_LANES)
+        return values.transpose(1, 0, 2).reshape(-1, STEM)
+
     def by_output_row(values):
         values = values.reshape(segments, STEM_SIDE, STEM_LANES)
         return values.transpose(1, 0, 2).reshape(stem_rows_here, STEM_LANES)
 
     if direct:
-        first_own, pair_own, spatial_own, late_own = cut_block(
-            me_array, w_squeeze, w_expand, w_reduce, w_spatial, w_restore,
-            jnp.pad(w_class, ((0, 0), (0, TILE - CLASSES))), stem_weight.T, next_kernel,
+        first_own, pair_own, spatial_own = cut_block(
+            me_array, w_squeeze, w_expand, w_reduce, w_spatial, stem_weight.T, next_kernel,
             scale_kernel, jnp.concatenate([gain_three, shift_three])[None], gain_one[None],
             shift_one[None], gain_two[None], shift_two[None], stem_gain[None], stem_shift[None],
         )
@@ -1746,7 +1824,15 @@
             lambda grads: (by_output_row(grads), band_select()), [stem_cotangent], firsts.depth()
         )
         firsts.take_depth(came)
-        inputs, came, _ = beside(frames_block, [frames], firsts.second() + pairs.depth())
+        (inputs, late_own), came, _ = beside(
+            lambda images, mine, restore, classes: (
+                frames_block(images),
+                late_cut_block(
+                    mine, restore, jnp.pad(classes, ((0, 0), (0, TILE - CLASSES)))
+                ),
+            ),
+            [frames, me_array, w_restore, w_class], firsts.second() + pairs.depth(),
+        )
         firsts.take_second(came[:1])
         pairs.take_depth(came[1:])
         (
@@ -1809,7 +1895,7 @@
         )
         spatials.take_third_of(0, came)
         one_sums, came, _ = beside(
-            swap_total, [with_row(one_part, stem_part)],
+            swap_total, [to_all(with_row(one_part, stem_part))],
             spatials.third_of(1) + spatials.core_of(0),
         )
         spatials.take_third_of(1, came[:1])
@@ -1819,7 +1905,7 @@
         spatial = spatials.arrays
     else:
         logit, gated_low, pre_one, one_part = gate_block(*gate_operands)
-        one_sums = swap_total(with_row(one_part, stem_part))
+        one_sums = swap_total(to_all(with_row(one_part, stem_part)))
     stem_sums = stem_lanes(one_sums)
     hidden_one, pre_two, two_part = second_block(
         me_array, spatial, pre_one, one_sums, affine_one, count
@@ -1830,7 +1916,9 @@
     stem_part = stem_part.reshape(2, STEM_SIDE, STEM).sum(1).reshape(1, 2 * STEM)
     two_sums = swap_total(two_part)
     hidden_two, pre_three, centres, three_part = third_block(pre_two, two_sums, affine_two, late, count)
-    three_sums = total(with_row(three_part, stem_part))
+    three_sums, stem_features = total_beside(
+        with_row(three_part, stem_part), by_segment, [stem_out]
+    )
     stem_grads = stem_lanes(three_sums)
     bias = jnp.pad(class_bias.astype(f32), (0, TILE - CLASSES))[None]
     activations, slope, view_sums, view_logits, pooled_low = fourth_block(
@@ -1887,7 +1975,10 @@
     run_stem_back = functools.partial(stem_back_block, count=stem_count)
 
     def stem_back_operands():
-        return [inputs, band_select(True), stem_pre, stem_sums, stem_affine, stem_norm_grad, stem_grads]
+        return [
+            inputs, band_select(True), stem_pre, stem_sums, stem_affine, stem_norm_grad, stem_grads,
+            kernel_grads,
+        ]
     run_outer = outer_block_of(R // 4)
 
     def sixth_operands():
@@ -1905,39 +1996,36 @@
     def mixing_back_operands():
         return [me_array, pair, logit_grad, upcoming, differ, full_next, full_scale]
 
-    def few_of(stem_back, kernel_grads):
-        stem_back = stem_back[:, :LANES, :STEM] + stem_back[:, LANES:, STEM:]
-        stem_grad = stem_back[:, : WINDOW * CHANNELS].reshape(-1, STEM)
-        stem_cut = stem_grad.T.reshape(8, 8, -1)
-        stem_cut = jnp.pad(stem_cut, ((0, 0), (0, 0), (0, 3 * TILE - stem_cut.shape[2])))
-        kernel_cut = kernel_grads.reshape(2, 9, 8, R // 8).transpose(2, 1, 0, 3)
-        kernel_cut = jnp.pad(kernel_cut, ((0, 0), (0, 0), (0, 0), (0, LANES - R // 8)))
-        few = jnp.concatenate([stem_cut.reshape(8, 24, TILE), kernel_cut.reshape(8, 9, TILE)], 1)
-        return jnp.pad(few, ((0, 0), (0, FEW_ROWS - few.shape[1]), (0, 0)))
-
     if direct:
         low_three, norm_two_grad, two_part = run_fifth(*fifth_operands)
-        (buffer, two_grads), _, _ = beside(
-            lambda hidden, low, part: (restore_outer_block(hidden, low), swap_total(part)),
-            [hidden_two, low_three, two_part], [],
+        (buffers, two_grads), _, _ = beside(
+            lambda mine, hidden, low, part: (
+                restore_outer_block(mine, hidden, low), swap_total(part)
+            ),
+            [me_array, hidden_two, low_three, two_part], [],
         )
         (low_two, norm_one_grad, one_part, factors), _, _ = beside(
             lambda parts, *operands: (*run_sixth(*operands), send_factors(parts)),
             [factors] + sixth_operands(), [],
         )
-        (buffer, one_grads), _, _ = beside(
-            lambda values, hidden, low, part: (
-                spatial_block(values.reshape(32, -1, WIDE), hidden, low), swap_total(part)
+        ((keep, send), one_grads), _, _ = beside(
+            lambda mine, shared, hidden, low, part: (
+                spatial_block(mine, shared, hidden, low), swap_total(part)
             ),
-            [buffer, hidden_one, low_two, one_part], [],
+            [me_array, buffers, hidden_one, low_two, one_part], [],
+        )
+        quarter = (4, 2, 2, R // 4, TILE)
+        (low_one, reduce_half), came, _ = beside(
+            functools.partial(low_outer_block, count=count), low_operands(), [(send, 1)]
+        )
+        buffer = (keep.astype(f32) + came[0].astype(f32)).astype(bf16)
+        reduced_sum = Sum(reduce_half, quarter, 0)
+        (low_one, buffer), came, _ = beside(
+            lambda *values: values, [low_one, buffer], reduced_sum.core()
         )
         buffer = lax.psum_scatter(
             buffer.reshape(8, -1, WIDE), "wide", scatter_dimension=0, tiled=False
         )
-        quarter = (4, 2, 2, R // 4, TILE)
-        low_one, reduce_half = low_outer_block(*low_operands(), count)
-        reduced_sum = Sum(reduce_half, quarter, 0)
-        low_one, came, _ = beside(lambda values: values, [low_one], reduced_sum.core())
         reduced_sum.take_core(came)
         (logit_grad, tokens_part), came, _ = beside(
             gate_back_block, gate_back_operands(), reduced_sum.split("x")
@@ -1952,82 +2040,80 @@
         expand_sum.take_core(came)
         (low_squeezed, kernel_grads), came, _ = beside(
             mixing_back_block, mixing_back_operands(),
-            expand_sum.split("x") + reduced_sum.split("z"),
-        )
-        expand_sum.take(came[:1])
-        reduced_sum.take(came[1:])
+            expand_sum.split("x"),
+        )
+        expand_sum.take(came)
         squeeze_half, came, _ = beside(
             run_outer, [me_array, low_squeezed, tokens],
-            expand_sum.split("y") + reduced_sum.spread(),
-        )
-        expand_sum.take(came[:1])
-        reduced_sum.take_spread(came[1:])
+            expand_sum.split("y"),
+        )
+        expand_sum.take(came)
+        both_sum = Sum((None, None), (), 1)
+        both_sum.axes = "z"
+        both_sum.values = jnp.stack([reduced_sum.values, expand_sum.values])
+        shared = Sum((None, None), (), 0)
+        shared.axes = "x"
+        shared.values = buffer.reshape(2, -1, WIDE)
         squeezed = Sum(squeeze_half, quarter, 0)
         tokens_part, came, _ = beside(lambda values: values, [tokens_part], squeezed.core())
         squeezed.take_core(came)
         stem_back, came, _ = beside(
-            run_stem_back, stem_back_operands(), squeezed.split("x") + expand_sum.split("z")
+            run_stem_back, stem_back_operands(),
+            squeezed.split("x") + both_sum.split("z") + shared.split("x"),
         )
         squeezed.take(came[:1])
-        expand_sum.take(came[1:])
-        (tokens_grad, few), came, _ = beside(
-            lambda grads, *operands: (
-                tokens_block(*operands), lax.all_to_all(grads, "wide", 0, 0, tiled=True)
-            ),
-            [few_of(stem_back, kernel_grads), me_array, squeeze, tokens_part, low_squeezed],
-            squeezed.split("y") + expand_sum.spread(),
+        both_sum.take(came[1:4])
+        shared.take(came[4:])
+        few = Sum((None, None), (), 0)
+        few.axes = "zy"
+        few.values = stem_back.reshape(4, 2, FEW_ROWS, TILE)
+        tokens_grad, came, _ = beside(
+            tokens_block, [me_array, squeeze, tokens_part, low_squeezed],
+            squeezed.split("y") + few.split("y") + both_sum.spread(),
         )
         squeezed.take(came[:1])
-        expand_sum.take_spread(came[1:])
-        few = jnp.sum(few, 0)
-        buffer = buffer.reshape(4, -1, WIDE)
-        near_place = lax.axis_index("narrow")
-        (few, stem_out, own), came, _ = beside(
-            lambda part, *kept: (
-                part + exchange(part, 1) + exchange(part, 2) + exchange(part, 3), *kept
-            ),
-            [few, stem_out, lax.dynamic_index_in_dim(buffer, near_place, 0, keepdims=False)],
-            squeezed.split("z") + [
-                (lax.dynamic_index_in_dim(buffer, near_place ^ mask, 0, keepdims=False), mask)
-                for mask in (1, 2, 3)
-            ],
-        )
+        few.take(came[1:2])
+        both_sum.take_spread(came[2:])
+        squeezed.values = jnp.concatenate([squeezed.values, few.values], axis=1)
+        _, came, _ = beside(lambda: None, [], squeezed.split("z") + shared.spread())
         squeezed.take(came[:3])
-        own = own.astype(f32)
-        for part in came[3:]:
-            own = own + part.astype(f32)
-        buffers = Sum((None, None), (), 0)
-        buffers.values = own
-        _, came, _ = beside(lambda: None, [], squeezed.spread() + buffers.spread())
-        squeezed.take_spread(came[:3])
-        buffers.take_spread(came[3:])
-        buffer = buffers.whole
-        sum_stem = few[:24].reshape(8, 3 * TILE)[:, : stem_weight.shape[0]].T
+        shared.take_spread(came[3:])
+        last = Sum((None, None), (), 0)
+        last.values = squeezed.values.astype(bf16)
+        _, came, _ = beside(lambda: None, [], last.spread())
+        last.take_spread(came)
+        squeezed.whole = last.whole[:, : R // 4]
+        few = jnp.sum(last.whole[:, R // 4 :], 0)
+        buffer = shared.whole
+        sum_stem = few[:24].reshape(3, 8, TILE).swapaxes(0, 1).reshape(8, 3 * TILE)
+        sum_stem = sum_stem[:, : stem_weight.shape[0]].T
         sum_next = few[24:33, :inner_width]
         sum_scale = few[24:33, LANES : LANES + inner_width]
-        sum_restore = buffer[:, :RESTORE_ROWS].swapaxes(0, 1).reshape(w_restore.shape)
-        sum_spatial = buffer[:, RESTORE_ROWS:].reshape(4, 9, 16, B).swapaxes(0, 1)
+        buffer = buffer.reshape(4, SHARED, 16, WIDE)
+        sum_restore = buffer[:, :GROUPS].swapaxes(1, 2).reshape(w_restore.shape)
+        sum_spatial = buffer[:, GROUPS:].swapaxes(0, 1)
         sum_spatial = sum_spatial.reshape(w_spatial.shape)
-        sum_reduce = reduced_sum.whole.reshape(B, TILE).T
-        sum_expand = expand_sum.whole.reshape(R, TILE)
+        sum_reduce = both_sum.whole[:, 0].reshape(B, TILE).T
+        sum_expand = both_sum.whole[:, 1].reshape(R, TILE)
         sum_squeeze = squeezed.whole.reshape(R, TILE).T
     else:
         low_three, norm_two_grad, two_part = run_fifth(*fifth_operands)
-        buffer = restore_outer_block(hidden_two, low_three)
+        buffers = restore_outer_block(me_array, hidden_two, low_three)
         two_grads = swap_total(two_part)
         low_two, norm_one_grad, one_part = run_sixth(*sixth_operands())
         factors = send_factors(factors)
         one_grads = swap_total(one_part)
-        buffer = spatial_block(buffer.reshape(32, -1, WIDE), hidden_one, low_two)
+        buffers = spatial_block(me_array, buffers, hidden_one, low_two)
         low_one, reduce_half = low_outer_block(*low_operands(), count)
         logit_grad, tokens_part = gate_back_block(*gate_back_operands())
         expand_half = run_outer(me_array, mixed_low, logit_grad)
         low_squeezed, kernel_grads = mixing_back_block(*mixing_back_operands())
-        few = few_of(run_stem_back(*stem_back_operands()), kernel_grads)
+        few = run_stem_back(*stem_back_operands())
         squeeze_half = run_outer(me_array, low_squeezed, tokens)
         tokens_grad = tokens_block(me_array, squeeze, tokens_part, low_squeezed)
         few = lax.psum(few, AXES)
-        sum_stem = few[:, :24].reshape(STEM, 3 * TILE)[:, : stem_weight.shape[0]].T
+        sum_stem = few[:, :24].reshape(8, 3, 8, TILE).swapaxes(1, 2).reshape(STEM, 3 * TILE)
+        sum_stem = sum_stem[:, : stem_weight.shape[0]].T
         sum_next, sum_scale = (
             few[:, 24:33, at : at + R // 8].swapaxes(0, 1).reshape(9, R) for at in (0, LANES)
         )
@@ -2039,15 +2125,12 @@
         sum_next = own_columns(sum_next, inner_width)
         sum_scale = own_columns(sum_scale, inner_width)
         sum_restore, sum_spatial, sum_reduce, sum_expand, sum_squeeze = reduced(
-            buffer, reduce_half, expand_half, squeeze_half
+            buffers, reduce_half, expand_half, squeeze_half
         )
     factors = factors.reshape(devices * view_count, outer_width + TILE)
     sum_class = product_left(
         factors[:, :outer_width], factors[:, outer_width : outer_width + CLASSES]
     )
-
-    stem_features = stem_out.reshape(STEM_SIDE, segments, STEM_LANES)
-    stem_features = stem_features.transpose(1, 0, 2).reshape(-1, STEM)
 
     def own_slice(values, width):
         return lax.dynamic_slice_in_dim(values, lax.axis_index("wide") * width, width)

time: 525 us -> 507 us (0.966)
  starting transfers between devices: 109 us -> 96.7 us
  waiting for transfers between devices: 62.6 us -> 57 us
    ppermute x74 -> x65, starting transfers between devices: 76.6 us -> 69.5 us  [exchange(): lax.ppermute(values, AXES, [(index, index ^ mask) for index in range(size)])]
    convert_element_type x0 -> x4, other arithmetic: none -> 6.66 us  [the longest x1 5.82 us: shards(): buffer = (keep.astype(f32) + came[0].astype(f32)).astype(bf16)]
    all_to_all x1 -> x0, starting transfers between devices: 6.51 us -> none  [shards(): lax.all_to_all(grads, 'wide', 0, 0, tiled=True)]
    ppermute x74 -> x65, waiting for transfers between devices: 43.2 us -> 37.8 us  [exchange(): lax.ppermute(values, AXES, [(index, index ^ mask) for index in range(size)])]
    pallas_call x27 -> x28, Pallas kernels: 252 us -> 255 us  [kernel_call(): return lambda *operands: call(*operands, *after)]
  transfers between devices with their start and end apart: 84 -> 74, of which waited for: 28 -> 28; matrix products, arithmetic and copies ran while one was open for 10% -> 10% of each run, Pallas kernels for 39% -> 41%
where the time goes in v2:
time: 507 us; the launch traced here: 497 us
  Pallas kernels  255 us (50%)
  starting transfers between devices  96.7 us (19%)
  waiting for transfers between devices  57 us (11%)
  local copies, waits for them, and re-layouts  39.9 us (8%)
  other arithmetic  29.7 us (6%)
  between operations  17.4 us (3%)
    pallas_call x28, Pallas kernels, kernel_call(): return lambda *operands: call(*operands, *after)  255 us
    ppermute x65, starting transfers between devices, exchange(): lax.ppermute(values, AXES, [(index, index ^ mask) for index in range(size)])  69.5 us
    ppermute x65, waiting for transfers between devices, exchange(): lax.ppermute(values, AXES, [(index, index ^ mask) for index in range(size)])  37.8 us
    all_to_all x4, starting transfers between devices, swap_total(): return jnp.sum(lax.all_to_all(copies, AXES, 0, 0, tiled=True), 0)  18.6 us
    all_to_all x4, waiting for transfers between devices, swap_total(): return jnp.sum(lax.all_to_all(copies, AXES, 0, 0, tiled=True), 0)  14.9 us
  transfers between devices with their start and end apart: 74, of which 28 were waited for; matrix products, arithmetic and copies ran while one was open for 10% of the time, Pallas kernels for 41%

profile of v2, /device:TPU:0, one launch (start us, length us, event | category | flops | bytes accessed | tf_op | source)
XLA Modules:
  0.0 496.9 jit_solution(2396331753438778800)
XLA Ops:
  8.5 2.1 shard_map.390
  10.6 3.0 collective-permute-start
  13.7 2.6 collective-permute-start.1
  16.6 1.8 fusion.3.refs_1_
  18.4 2.0 copy.108
  20.4 2.3 reshape.235
  22.7 2.8 copy.109
  26.1 1.8 collective-permute-start.3
  28.5 3.5 collective-permute-start.5
  34.7 7.8 %shard_map.392.refs_0_ = bf16[2,19,32,384]{3,2,1,0:T(8,128)(2,1)} custom-call(bf16[32,5,3,32,32]{4,3,2,1,0:T(8,128)(2,1)} %bitcast.232), custom_call_target="tpu_custom_call" | custom-call | flops 98304000 | bytes 16777216 | tf_op jit(solution)/shard_map/pallas_call | solution.py:359
  43.8 2.3 shard_map.395
  49.5 3.6 collective-permute-start.10
  53.3 9.2 %shard_map.397 = (f32[512,1024]{1,0:T(8,128)}, f32[2,1024]{1,0:T(2,128)}) custom-call(bf16[2,19,32,384]{3,2,1,0:T(8,128)(2,1)} %shard_map.392.refs_0_, bf16[8,384,256]{2,1,0:T(8,128)(2,1)} %fusion.3.refs_1_, bf16[7,256,128]{2,1,0:T(8,128)(2,1)} %get-tuple-element.372.refs_2_), custom_call_target="tpu_custom_call" | custom-call | flops 5637144576 | bytes 16777216 | tf_op jit(solution)/shard_map/pallas_call | solution.py:359
  67.8 15.1 %shard_map.400 = (f32[1568,512]{1,0:T(8,128)}, f32[1568,512]{1,0:T(8,128)}, bf16[1568,512]{1,0:T(8,128)(2,1)}) custom-call(s32[1]{0:T(128)} %bitcast.refs_0_, bf16[8,64,512]{2,1,0:T(8,128)(2,1)} %get-tuple-element.629.refs_1_, bf16[8,64,512]{2,1,0:T(8,128)(2,1)} %collective-permute-done.7.refs_2_, bf16[8,64,512]{2,1,0:T(8,128)(2,1)} %copy-done.31, ...), custom_call_target="tpu_custom_call" | custom-call | flops 6576668672 | bytes 16777216 | tf_op jit(solution)/shard_map/pallas_call | solution.py:359
  82.9 7.8 %collective-permute-done.14.refs_2_ = bf16[8,128,512]{2,1,0:T(8,128)(2,1)S(1)} collective-permute-done((bf16[8,128,512]{2,1,0:T(8,128)(2,1)S(1)}, bf16[8,128,512]{2,1,0:T(8,128)(2,1)S(1)}, u32[]{:S(2)}, u32[]{:S(2)}) %collective-permute-start.14) | collective-permute-done | bytes 1048608 | tf_op jit(solution)/shard_map/ppermute | solution.py:44
  91.2 2.9 collective-permute-done.16.refs_3_
  95.7 15.8 %shard_map.401 = (bf16[1568,2048]{1,0:T(8,128)(2,1)}, bf16[1568,2048]{1,0:T(8,128)(2,1)}, f32[1568,512]{1,0:T(8,128)}, f32[2,512]{1,0:T(2,128)}) custom-call(s32[1]{0:T(128)} %bitcast.refs_0_, bf16[8,128,512]{2,1,0:T(8,128)(2,1)} %copy-done, bf16[8,128,512]{2,1,0:T(8,128)(2,1)} %copy-done.8, bf16[8,128,512]{2,1,0:T(8,128)(2,1)} %copy-done.9, ...), custom_call_target="tpu_custom_call" | custom-call | flops 13153337344 | bytes 16777216 | tf_op jit(solution)/shard_map/pallas_call | solution.py:359
  113.0 1.7 collective-permute-start.19
  115.2 4.9 all-to-all-start
  121.0 14.1 %all-to-all-done = f32[32,3,512]{2,1,0:T(4,128)S(1)} async-done(((f32[32,3,512]{2,1,0:T(4,128)}), f32[32,3,512]{2,1,0:T(4,128)S(1)}, u32[]{:S(2)}, u32[]{:S(2)}) %all-to-all-start) | async-done | bytes 196640 | tf_op jit(solution)/shard_map/all_to_all | solution.py:79
  139.5 15.7 %shard_map.402 = (bf16[2,1008,1536]{2,1,0:T(8,128)(2,1)}, f32[1568,512]{1,0:T(8,128)}, f32[32,2,512]{2,1,0:T(2,128)}) custom-call(s32[1]{0:T(128)} %bitcast.refs_0_, bf16[4,144,512]{2,1,0:T(8,128)(2,1)} %copy-done.2, bf16[4,144,512]{2,1,0:T(8,128)(2,1)} %collective-permute-done.15.refs_2_, bf16[4,144,512]{2,1,0:T(8,128)(2,1)} %copy-done.25, ...), custom_call_target="tpu_custom_call" | custom-call | flops 14797504512 | bytes 16777216 | tf_op jit(solution)/shard_map/pallas_call | solution.py:359
  155.2 5.3 %all-to-all-start.1 = ((f32[32,2,512]{2,1,0:T(2,128)}), f32[32,2,512]{2,1,0:T(2,128)S(1)}, u32[]{:S(2)}, u32[]{:S(2)}) async-start(f32[32,2,512]{2,1,0:T(2,128)} %get-tuple-element.449), calls=%async_computation.1 | async-start | bytes 262144 | tf_op jit(solution)/shard_map/all_to_all | solution.py:79
  161.9 5.1 %shard_map.404 = (bf16[512,1024]{1,0:T(8,128)(2,1)}, f32[512,1024]{1,0:T(8,128)}, f32[2,1024]{1,0:T(2,128)}) custom-call(f32[512,1024]{1,0:T(8,128)} %get-tuple-element.612.refs_0_.refs_2_, f32[2,1024]{1,0:T(2,128)} %tile.22.refs_1_.refs_3_, f32[2,1024]{1,0:T(2,128)} %get-tuple-element.614.refs_2_.refs_4_, bf16[512,1024]{1,0:T(8,128)(2,1)} %bitcast.245), custom_call_target="tpu_custom_call" | custom-call | flops 4194304000 | bytes 16777216 | tf_op jit(solution)/shard_map/pallas_call | solution.py:359
  169.3 11.1 %shard_map.403 = (bf16[1568,512]{1,0:T(8,128)(2,1)}, bf16[1568,2048]{1,0:T(8,128)(2,1)}, f32[2,1,2048]{2,1,0:T(1,128)}, f32[2,2048]{1,0:T(2,128)}) custom-call(f32[1568,512]{1,0:T(8,128)} %get-tuple-element.499.refs_0_.refs_8_.refs_10_, f32[2,512]{1,0:T(2,128)} %reduce_sum.101.refs_1_.refs_9_.refs_11_, ...), custom_call_target="tpu_custom_call" | custom-call | flops 6576668672 | bytes 16777216 | tf_op jit(solution)/shard_map/pallas_call | solution.py:359
  183.2 2.1 collective-permute-start.27
  191.3 2.4 collective-permute-start.29
  196.9 2.5 collective-permute-done.30
  200.0 14.5 %shard_map.405 = (bf16[1568,2048]{1,0:T(8,128)(2,1)}, bf16[1568,2048]{1,0:T(8,128)(2,1)}, f32[2,8,2048]{2,1,0:T(8,128)}, f32[16,256]{1,0:T(8,128)}, bf16[16,2048]{1,0:T(8,128)(2,1)}) custom-call(bf16[1568,2048]{1,0:T(8,128)(2,1)} %get-tuple-element.452.refs_0_.refs_1_, f32[2,1,2048]{2,1,0:T(1,128)} %get-tuple-element.453.refs_1_.refs_2_, ...), custom_call_target="tpu_custom_call" | custom-call | flops 128450560 | bytes 16777216 | tf_op jit(solution)/shard_map/pallas_call | solution.py:359
  217.8 2.1 collective-permute-done.32.refs_2_
  220.5 3.2 shard_map.406
  223.8 2.5 collective-permute-start.33
  228.2 2.4 collective-permute-start.36
  230.5 2.5 collective-permute-start.35
  234.9 2.0 collective-permute-done.34
  237.8 3.6 collective-permute-start.37
  244.1 16.4 %shard_map.407 = (bf16[1568,2048]{1,0:T(8,128)(2,1)}, f32[1568,512]{1,0:T(8,128)}, f32[32,2,512]{2,1,0:T(2,128)}) custom-call(bf16[1568,2048]{1,0:T(8,128)(2,1)} %get-tuple-element.554.refs_0_.refs_6_, bf16[1568,2048]{1,0:T(8,128)(2,1)} %get-tuple-element.452.refs_0_.refs_1_, f32[2,1,2048]{2,1,0:T(1,128)} %get-tuple-element.453.refs_1_.refs_2_, ...), custom_call_target="tpu_custom_call" | custom-call | flops 6576668672 | bytes 16777216 | tf_op jit(solution)/shard_map/pallas_call | solution.py:359
  260.5 2.6 all-to-all-start.2
  263.1 8.5 %shard_map.408 = (bf16[16,208,512]{2,1,0:T(8,128)(2,1)}, bf16[16,208,512]{2,1,0:T(8,128)(2,1)}) custom-call(s32[1]{0:T(128)} %bitcast.refs_0_, bf16[1568,512]{1,0:T(8,128)(2,1)} %get-tuple-element.483.refs_1_, bf16[1568,2048]{1,0:T(8,128)(2,1)} %get-tuple-element.484.refs_2_), custom_call_target="tpu_custom_call" | custom-call | flops 6576668672 | bytes 16777216 | tf_op jit(solution)/shard_map/pallas_call | solution.py:359
  273.0 5.8 %all-to-all-start.3 = ((bf16[32,4,512]{2,1,0:T(4,128)(2,1)}), bf16[32,4,512]{2,1,0:T(4,128)(2,1)S(1)}, u32[]{:S(2)}, u32[]{:S(2)}) async-start(bf16[32,4,512]{2,1,0:T(4,128)(2,1)} %bitcast.40), calls=%async_computation.3 | async-start | bytes 262144 | tf_op jit(solution)/shard_map/all_to_all | solution.py:1963
  278.9 17.8 %shard_map.409 = (bf16[1568,512]{1,0:T(8,128)(2,1)}, f32[1568,512]{1,0:T(8,128)}, f32[32,2,512]{2,1,0:T(2,128)}) custom-call(s32[1]{0:T(128)} %bitcast.refs_0_, bf16[4,144,512]{2,1,0:T(8,128)(2,1)} %copy-done.2, bf16[4,144,512]{2,1,0:T(8,128)(2,1)} %collective-permute-done.15.refs_2_, bf16[4,144,512]{2,1,0:T(8,128)(2,1)} %copy-done.25, ...), custom_call_target="tpu_custom_call" | custom-call | flops 14797504512 | bytes 16777216 | tf_op jit(solution)/shard_map/pallas_call | solution.py:359
  296.7 5.8 %all-to-all-start.4 = ((f32[32,2,512]{2,1,0:T(2,128)}), f32[32,2,512]{2,1,0:T(2,128)S(1)}, u32[]{:S(2)}, u32[]{:S(2)}) async-start(f32[32,2,512]{2,1,0:T(2,128)} %get-tuple-element.523), calls=%async_computation.4 | async-start | bytes 262144 | tf_op jit(solution)/shard_map/all_to_all | solution.py:79
  302.6 18.7 %shard_map.410 = (bf16[16,208,512]{2,1,0:T(8,128)(2,1)}, bf16[16,208,512]{2,1,0:T(8,128)(2,1)}) custom-call(s32[1]{0:T(128)} %bitcast.refs_0_, bf16[16,208,512]{2,1,0:T(8,128)(2,1)} %get-tuple-element.517.refs_1_, bf16[16,208,512]{2,1,0:T(8,128)(2,1)} %get-tuple-element.518.refs_2_, ...), custom_call_target="tpu_custom_call", output_to_operand_aliasing={{0}: (1, {}), {1}: (2, {})} | custom-call | flops 14797504512 | bytes 16777216 | tf_op jit(solution)/shard_map/pallas_call | solution.py:359
  322.3 11.2 %shard_map.411 = (bf16[1568,512]{1,0:T(8,128)(2,1)}, bf16[8,256,256]{2,1,0:T(8,128)(2,1)}, bf16[8,256,256]{2,1,0:T(8,128)(2,1)}) custom-call(s32[1]{0:T(128)} %bitcast.refs_0_, f32[1568,512]{1,0:T(8,128)} %get-tuple-element.527.refs_1_, f32[1568,512]{1,0:T(8,128)} %get-tuple-element.528.refs_9_.refs_14_.refs_2_, ...), custom_call_target="tpu_custom_call" | custom-call | flops 6576668672 | bytes 16777216 | tf_op jit(solution)/shard_map/pallas_call | solution.py:359
  333.5 5.8 %add_convert_fusion = bf16[16,208,512]{2,1,0:T(8,128)(2,1)} fusion(bf16[16,208,512]{2,1,0:T(8,128)(2,1)} %collective-permute-done.40, bf16[16,208,512]{2,1,0:T(8,128)(2,1)} %get-tuple-element.538), kind=kLoop, calls=%fused_computation | loop fusion | flops 6815744 | bytes 10223616 | tf_op jit(solution)/shard_map/convert_element_type | solution.py:2021
  339.6 2.0 fusion.2.refs_1_
  346.8 1.8 collective-permute-start.42
  348.6 18.7 %shard_map.412 = (bf16[1568,2048]{1,0:T(8,128)(2,1)}, bf16[1568,2048]{1,0:T(8,128)(2,1)}) custom-call(s32[1]{0:T(128)} %bitcast.refs_0_, bf16[8,128,512]{2,1,0:T(8,128)(2,1)} %copy-done, bf16[8,128,512]{2,1,0:T(8,128)(2,1)} %copy-done.8, bf16[8,128,512]{2,1,0:T(8,128)(2,1)} %copy-done.9, bf16[8,128,512]{2,1,0:T(8,128)(2,1)} %collective-permute-done.17.refs_4_, ...), custom_call_target="tpu_custom_call" | custom-call | flops 6576668672 | bytes 16777216 | tf_op jit(solution)/shard_map/pallas_call | solution.py:359
  369.0 8.6 %shard_map.413 = (bf16[8,256,256]{2,1,0:T(8,128)(2,1)}, bf16[8,256,256]{2,1,0:T(8,128)(2,1)}) custom-call(s32[1]{0:T(128)} %bitcast.refs_0_, bf16[1568,512]{1,0:T(8,128)(2,1)} %get-tuple-element.565.refs_6_.refs_1_, bf16[1568,2048]{1,0:T(8,128)(2,1)} %get-tuple-element.583.refs_2_.refs_5_), custom_call_target="tpu_custom_call" | custom-call | flops 6576668672 | bytes 16777216 | tf_op jit(solution)/shard_map/pallas_call | solution.py:359
  377.6 2.1 collective-permute-done.43
  384.7 1.8 convert_add_fusion.1
  387.5 20.2 %shard_map.414 = (bf16[1568,512]{1,0:T(8,128)(2,1)}, f32[18,512]{1,0:T(8,128)}) custom-call(s32[1]{0:T(128)} %bitcast.refs_0_, bf16[8,128,512]{2,1,0:T(8,128)(2,1)} %copy-done, bf16[8,128,512]{2,1,0:T(8,128)(2,1)} %copy-done.8, bf16[8,128,512]{2,1,0:T(8,128)(2,1)} %copy-done.9, bf16[8,128,512]{2,1,0:T(8,128)(2,1)} %collective-permute-done.17.refs_4_, ...), custom_call_target="tpu_custom_call" | custom-call | flops 6576668672 | bytes 16777216 | tf_op jit(solution)/shard_map/pallas_call | solution.py:359
  407.8 2.3 bitcast_add_fusion.1
  412.1 8.5 %shard_map.415 = (bf16[8,256,256]{2,1,0:T(8,128)(2,1)}, bf16[8,256,256]{2,1,0:T(8,128)(2,1)}) custom-call(s32[1]{0:T(128)} %bitcast.refs_0_, bf16[1568,512]{1,0:T(8,128)(2,1)} %get-tuple-element.634.refs_1_.refs_6_, bf16[1568,2048]{1,0:T(8,128)(2,1)} %refs_2_.2), custom_call_target="tpu_custom_call" | custom-call | flops 6576668672 | bytes 16777216 | tf_op jit(solution)/shard_map/pallas_call | solution.py:359
  425.0 2.1 reduce-scatter.2.cloned.1.call-done
  428.7 2.4 collective-permute-start.48
  433.4 2.1 collective-permute-start.51
  435.5 10.6 %shard_map.416 = f32[8,40,256]{2,1,0:T(8,128)} custom-call(bf16[2,19,32,384]{3,2,1,0:T(8,128)(2,1)} %shard_map.392.refs_0_, bf16[8,256,384]{2,1,0:T(8,128)(2,1)} %fusion.2.refs_1_, f32[512,1024]{1,0:T(8,128)} %get-tuple-element.612.refs_0_.refs_2_, f32[2,1024]{1,0:T(2,128)} %tile.22.refs_1_.refs_3_, f32[2,1024]{1,0:T(2,128)} %get-tuple-element.614.refs_2_.refs_4_, ...), custom_call_target="tpu_custom_call" | custom-call | flops 5637144576 | bytes 16777216 | tf_op jit(solution)/shard_map/pallas_call | solution.py:359
  450.8 1.9 collective-permute-start.56
  452.8 10.0 %shard_map.417 = bf16[1568,2048]{1,0:T(8,128)(2,1)} custom-call(s32[1]{0:T(128)} %bitcast.refs_0_, bf16[8,64,512]{2,1,0:T(8,128)(2,1)} %get-tuple-element.629.refs_1_, bf16[8,64,512]{2,1,0:T(8,128)(2,1)} %collective-permute-done.7.refs_2_, bf16[8,64,512]{2,1,0:T(8,128)(2,1)} %copy-done.31, bf16[8,64,512]{2,1,0:T(8,128)(2,1)} %copy-done.32, ...), custom_call_target="tpu_custom_call" | custom-call | flops 6576668672 | bytes 16777216 | tf_op jit(solution)/shard_map/pallas_call | solution.py:359
  464.1 2.3 collective-permute-start.59
  467.6 1.7 collective-permute-start.62
  471.5 2.4 collective-permute-done.59
  475.6 3.8 collective-permute-done.63
  479.7 1.7 collective-permute-start.65
  (321 shorter events, 95.7 us)
Async XLA Ops:
  7.2 162.1 %all-gather.3.cloned.1.call-start = ((), (), s32[]{:S(2)}) async-start(), calls=%async_computation.7 | async-start | bytes 3244032 | tf_op jit(solution)/shard_map/all_gather | solution.py:1887
  10.6 14.8 %collective-permute-start = (bf16[96,512]{1,0:T(8,128)(2,1)}, bf16[96,512]{1,0:T(8,128)(2,1)S(1)}, u32[]{:S(2)}, u32[]{:S(2)}) collective-permute-start(bf16[96,512]{1,0:T(8,128)(2,1)} %get-tuple-element.349), channel_id=1, source_target_pairs={{0,8},{1,9},{2,10},{3,11},{4,12},{5,13},{6,14},{7,15},{8,0},{9,1},... | collective-permute-start | bytes 294920 | tf_op jit(solution)/shard_map/ppermute | solution.py:44
  13.7 11.8 %collective-permute-start.1 = (bf16[96,512]{1,0:T(8,128)(2,1)}, bf16[96,512]{1,0:T(8,128)(2,1)S(1)}, u32[]{:S(2)}, u32[]{:S(2)}) collective-permute-start(bf16[96,512]{1,0:T(8,128)(2,1)} %get-tuple-element.349), channel_id=1, source_target_pairs={{0,16},{1,17},{2,18},{3,19},{4,20},{5,21},{6,22},{7,23},{8,24},{9,... | collective-permute-start | bytes 294920 | tf_op jit(solution)/shard_map/ppermute | solution.py:44
  16.3 9.2 %collective-permute-start.2 = (bf16[96,512]{1,0:T(8,128)(2,1)}, bf16[96,512]{1,0:T(8,128)(2,1)S(1)}, u32[]{:S(2)}, u32[]{:S(2)}) collective-permute-start(bf16[96,512]{1,0:T(8,128)(2,1)} %get-tuple-element.349), channel_id=1, source_target_pairs={{0,24},{1,25},{2,26},{3,27},{4,28},{5,29},{6,30},{7,31},{8,16},{9,... | collective-permute-start | bytes 294920 | tf_op jit(solution)/shard_map/ppermute | solution.py:44
  26.1 16.4 %collective-permute-start.3 = (bf16[4,96,512]{2,1,0:T(8,128)(2,1)S(1)}, bf16[4,96,512]{2,1,0:T(8,128)(2,1)S(1)}, u32[]{:S(2)}, u32[]{:S(2)}) collective-permute-start(bf16[4,96,512]{2,1,0:T(8,128)(2,1)S(1)} %shard_map.391.refs_0_), channel_id=1, source_target_pairs={{0,4},{1,5},{2,6},{3,7},{4,0},{5,1},{6,2},{7,3},{8,12},{9,13},{10,... | collective-permute-start | bytes 1179656 | tf_op jit(solution)/shard_map/ppermute | solution.py:44
  27.9 14.6 %collective-permute-start.4 = (bf16[128,512]{1,0:T(8,128)(2,1)S(1)}, bf16[128,512]{1,0:T(8,128)(2,1)S(1)}, u32[]{:S(2)}, u32[]{:S(2)}) collective-permute-start(bf16[128,512]{1,0:T(8,128)(2,1)S(1)} %copy-done.4), channel_id=1, source_target_pairs={{0,8},{1,9},{2,10},{3,11},{4,12},{5,13},{6,14},{7,15},{8,0},{9,1},... | collective-permute-start | bytes 393224 | tf_op jit(solution)/shard_map/ppermute | solution.py:44
  28.5 14.0 %collective-permute-start.5 = (bf16[128,512]{1,0:T(8,128)(2,1)S(1)}, bf16[128,512]{1,0:T(8,128)(2,1)S(1)}, u32[]{:S(2)}, u32[]{:S(2)}) collective-permute-start(bf16[128,512]{1,0:T(8,128)(2,1)S(1)} %copy-done.4), channel_id=1, source_target_pairs={{0,16},{1,17},{2,18},{3,19},{4,20},{5,21},{6,22},{7,23},{8,24},{9,... | collective-permute-start | bytes 393224 | tf_op jit(solution)/shard_map/ppermute | solution.py:44
  32.0 10.5 %collective-permute-start.6 = (bf16[128,512]{1,0:T(8,128)(2,1)S(1)}, bf16[128,512]{1,0:T(8,128)(2,1)S(1)}, u32[]{:S(2)}, u32[]{:S(2)}) collective-permute-start(bf16[128,512]{1,0:T(8,128)(2,1)S(1)} %copy-done.4), channel_id=1, source_target_pairs={{0,24},{1,25},{2,26},{3,27},{4,28},{5,29},{6,30},{7,31},{8,16},{9,... | collective-permute-start | bytes 393224 | tf_op jit(solution)/shard_map/ppermute | solution.py:44
  46.9 15.6 %collective-permute-start.7 = (bf16[8,64,512]{2,1,0:T(8,128)(2,1)}, bf16[8,64,512]{2,1,0:T(8,128)(2,1)}, u32[]{:S(2)}, u32[]{:S(2)}) collective-permute-start(bf16[8,64,512]{2,1,0:T(8,128)(2,1)} %get-tuple-element.629.refs_1_), channel_id=1, source_target_pairs={{0,2},{1,3},{2,0},{3,1},{4,6},{5,7},{6,4},{7,5},{8,10},{9,11},{10,... | collective-permute-start | bytes 1572872 | tf_op jit(solution)/shard_map/ppermute | solution.py:44
  48.4 14.1 %collective-permute-start.8 = (bf16[4,128,512]{2,1,0:T(8,128)(2,1)S(1)}, bf16[4,128,512]{2,1,0:T(8,128)(2,1)S(1)}, u32[]{:S(2)}, u32[]{:S(2)}) collective-permute-start(bf16[4,128,512]{2,1,0:T(8,128)(2,1)S(1)} %shard_map.396.refs_0_), channel_id=1, source_target_pairs={{0,4},{1,5},{2,6},{3,7},{4,0},{5,1},{6,2},{7,3},{8,12},{9,13},{10,... | collective-permute-start | bytes 1572872 | tf_op jit(solution)/shard_map/ppermute | solution.py:44
  49.0 13.5 %collective-permute-start.9 = (bf16[144,512]{1,0:T(8,128)(2,1)S(1)}, bf16[144,512]{1,0:T(8,128)(2,1)S(1)}, u32[]{:S(2)}, u32[]{:S(2)}) collective-permute-start(bf16[144,512]{1,0:T(8,128)(2,1)S(1)} %copy-done.3), channel_id=1, source_target_pairs={{0,8},{1,9},{2,10},{3,11},{4,12},{5,13},{6,14},{7,15},{8,0},{9,1},... | collective-permute-start | bytes 442376 | tf_op jit(solution)/shard_map/ppermute | solution.py:44
  49.5 13.0 %collective-permute-start.10 = (bf16[144,512]{1,0:T(8,128)(2,1)S(1)}, bf16[144,512]{1,0:T(8,128)(2,1)S(1)}, u32[]{:S(2)}, u32[]{:S(2)}) collective-permute-start(bf16[144,512]{1,0:T(8,128)(2,1)S(1)} %copy-done.3), channel_id=1, source_target_pairs={{0,16},{1,17},{2,18},{3,19},{4,20},{5,21},{6,22},{7,23},{8,24},{9,... | collective-permute-start | bytes 442376 | tf_op jit(solution)/shard_map/ppermute | solution.py:44
  53.1 9.4 %collective-permute-start.11 = (bf16[144,512]{1,0:T(8,128)(2,1)S(1)}, bf16[144,512]{1,0:T(8,128)(2,1)S(1)}, u32[]{:S(2)}, u32[]{:S(2)}) collective-permute-start(bf16[144,512]{1,0:T(8,128)(2,1)S(1)} %copy-done.3), channel_id=1, source_target_pairs={{0,24},{1,25},{2,26},{3,27},{4,28},{5,29},{6,30},{7,31},{8,16},{9,... | collective-permute-start | bytes 442376 | tf_op jit(solution)/shard_map/ppermute | solution.py:44
  65.5 25.2 %collective-permute-start.14 = (bf16[8,128,512]{2,1,0:T(8,128)(2,1)S(1)}, bf16[8,128,512]{2,1,0:T(8,128)(2,1)S(1)}, u32[]{:S(2)}, u32[]{:S(2)}) collective-permute-start(bf16[8,128,512]{2,1,0:T(8,128)(2,1)S(1)} %shard_map.399.refs_1_), channel_id=1, source_target_pairs={{0,2},{1,3},{2,0},{3,1},{4,6},{5,7},{6,4},{7,5},{8,10},{9,11},{10,... | collective-permute-start | bytes 3145736 | tf_op jit(solution)/shard_map/ppermute | solution.py:44
  66.3 16.6 %collective-permute-start.15 = (bf16[4,144,512]{2,1,0:T(8,128)(2,1)S(1)}, bf16[4,144,512]{2,1,0:T(8,128)(2,1)}, u32[]{:S(2)}, u32[]{:S(2)}) collective-permute-start(bf16[4,144,512]{2,1,0:T(8,128)(2,1)S(1)} %shard_map.398.refs_1_), channel_id=1, source_target_pairs={{0,4},{1,5},{2,6},{3,7},{4,0},{5,1},{6,2},{7,3},{8,12},{9,13},{10,... | collective-permute-start | bytes 1769480 | tf_op jit(solution)/shard_map/ppermute | solution.py:44
  90.7 4.4 collective-permute-start.17
  95.3 16.2 %collective-permute-start.18 = (bf16[4,144,512]{2,1,0:T(8,128)(2,1)S(1)}, bf16[4,144,512]{2,1,0:T(8,128)(2,1)S(1)}, u32[]{:S(2)}, u32[]{:S(2)}) collective-permute-start(bf16[4,144,512]{2,1,0:T(8,128)(2,1)S(1)} %shard_map.398.refs_1_), channel_id=1, source_target_pairs={{0,2},{1,3},{2,0},{3,1},{4,6},{5,7},{6,4},{7,5},{8,10},{9,11},{10,... | collective-permute-start | bytes 1769480 | tf_op jit(solution)/shard_map/ppermute | solution.py:44
  113.0 22.7 %collective-permute-start.19 = (bf16[4,144,512]{2,1,0:T(8,128)(2,1)}, bf16[4,144,512]{2,1,0:T(8,128)(2,1)S(1)}, u32[]{:S(2)}, u32[]{:S(2)}) collective-permute-start(bf16[4,144,512]{2,1,0:T(8,128)(2,1)} %collective-permute-done.15.refs_2_), channel_id=1, source_target_pairs={{0,2},{1,3},{2,0},{3,1},{4,6},{5,7},{6,4},{7,5},{8,10},{9,11},{10,... | collective-permute-start | bytes 1769480 | tf_op jit(solution)/shard_map/ppermute | solution.py:44
  114.7 21.0 %collective-permute-start.20 = (bf16[4,144,512]{2,1,0:T(8,128)(2,1)S(1)}, bf16[4,144,512]{2,1,0:T(8,128)(2,1)S(1)}, u32[]{:S(2)}, u32[]{:S(2)}) collective-permute-start(bf16[4,144,512]{2,1,0:T(8,128)(2,1)S(1)} %shard_map.398.refs_1_), channel_id=1, source_target_pairs={{0,1},{1,0},{2,3},{3,2},{4,5},{5,4},{6,7},{7,6},{8,9},{9,8},{10,11... | collective-permute-start | bytes 1769480 | tf_op jit(solution)/shard_map/ppermute | solution.py:44
  114.7 21.1 %collective-permute-start.21 = (bf16[4,144,512]{2,1,0:T(8,128)(2,1)S(1)}, bf16[4,144,512]{2,1,0:T(8,128)(2,1)}, u32[]{:S(2)}, u32[]{:S(2)}) collective-permute-start(bf16[4,144,512]{2,1,0:T(8,128)(2,1)S(1)} %collective-permute-done.18.refs_3_), channel_id=1, source_target_pairs={{0,1},{1,0},{2,3},{3,2},{4,5},{5,4},{6,7},{7,6},{8,9},{9,8},{10,11... | collective-permute-start | bytes 1769480 | tf_op jit(solution)/shard_map/ppermute | solution.py:44
  115.2 19.9 %all-to-all-start = ((f32[32,3,512]{2,1,0:T(4,128)}), f32[32,3,512]{2,1,0:T(4,128)S(1)}, u32[]{:S(2)}, u32[]{:S(2)}) async-start(f32[32,3,512]{2,1,0:T(4,128)} %broadcast_in_dim.115), calls=%async_computation | async-start | bytes 524288 | tf_op jit(solution)/shard_map/all_to_all | solution.py:79
  155.2 13.5 %all-to-all-start.1 = ((f32[32,2,512]{2,1,0:T(2,128)}), f32[32,2,512]{2,1,0:T(2,128)S(1)}, u32[]{:S(2)}, u32[]{:S(2)}) async-start(f32[32,2,512]{2,1,0:T(2,128)} %get-tuple-element.449), calls=%async_computation.1 | async-start | bytes 262144 | tf_op jit(solution)/shard_map/all_to_all | solution.py:79
  183.2 4.9 collective-permute-start.27
  185.2 3.9 collective-permute-start.26
  185.8 3.9 collective-permute-start.25
  189.7 7.1 %collective-permute-start.28 = (f32[3,2048]{1,0:T(4,128)S(1)}, f32[3,2048]{1,0:T(4,128)S(1)}, u32[]{:S(2)}, u32[]{:S(2)}) collective-permute-start(f32[3,2048]{1,0:T(4,128)S(1)} %add_add_fusion.3), channel_id=1, source_target_pairs={{0,8},{1,9},{2,10},{3,11},{4,12},{5,13},{6,14},{7,15},{8,0},{9,1},... | collective-permute-start | bytes 73736 | tf_op jit(solution)/shard_map/ppermute | solution.py:44
  191.3 5.6 %collective-permute-start.29 = (f32[3,2048]{1,0:T(4,128)S(1)}, f32[3,2048]{1,0:T(4,128)S(1)}, u32[]{:S(2)}, u32[]{:S(2)}) collective-permute-start(f32[3,2048]{1,0:T(4,128)S(1)} %add_add_fusion.3), channel_id=1, source_target_pairs={{0,16},{1,17},{2,18},{3,19},{4,20},{5,21},{6,22},{7,23},{8,24},{9,... | collective-permute-start | bytes 73736 | tf_op jit(solution)/shard_map/ppermute | solution.py:44
  193.7 5.7 %collective-permute-start.30 = (f32[3,2048]{1,0:T(4,128)S(1)}, f32[3,2048]{1,0:T(4,128)S(1)}, u32[]{:S(2)}, u32[]{:S(2)}) collective-permute-start(f32[3,2048]{1,0:T(4,128)S(1)} %add_add_fusion.3), channel_id=1, source_target_pairs={{0,24},{1,25},{2,26},{3,27},{4,28},{5,29},{6,30},{7,31},{8,16},{9,... | collective-permute-start | bytes 73736 | tf_op jit(solution)/shard_map/ppermute | solution.py:44
  215.9 4.1 collective-permute-start.32
  228.2 6.3 %collective-permute-start.36 = (f32[3,2048]{1,0:T(4,128)S(1)}, f32[3,2048]{1,0:T(4,128)S(1)}, u32[]{:S(2)}, u32[]{:S(2)}) collective-permute-start(f32[3,2048]{1,0:T(4,128)S(1)} %add.249), channel_id=1, source_target_pairs={{0,6},{1,7},{2,4},{3,5},{4,2},{5,3},{6,0},{7,1},{8,14},{9,15},{10,... | collective-permute-start | bytes 73736 | tf_op jit(solution)/shard_map/ppermute | solution.py:44
  230.5 4.4 collective-permute-start.35
  236.9 5.9 %collective-permute-start.39 = (f32[3,2048]{1,0:T(4,128)S(1)}, f32[3,2048]{1,0:T(4,128)S(1)}, u32[]{:S(2)}, u32[]{:S(2)}) collective-permute-start(f32[3,2048]{1,0:T(4,128)S(1)} %add_add_fusion.1), channel_id=1, source_target_pairs={{0,24},{1,25},{2,26},{3,27},{4,28},{5,29},{6,30},{7,31},{8,16},{9,... | collective-permute-start | bytes 73736 | tf_op jit(solution)/shard_map/ppermute | solution.py:44
  237.8 5.6 %collective-permute-start.38 = (f32[3,2048]{1,0:T(4,128)S(1)}, f32[3,2048]{1,0:T(4,128)S(1)}, u32[]{:S(2)}, u32[]{:S(2)}) collective-permute-start(f32[3,2048]{1,0:T(4,128)S(1)} %add_add_fusion.1), channel_id=1, source_target_pairs={{0,16},{1,17},{2,18},{3,19},{4,20},{5,21},{6,22},{7,23},{8,24},{9,... | collective-permute-start | bytes 73736 | tf_op jit(solution)/shard_map/ppermute | solution.py:44
  237.8 5.6 %collective-permute-start.37 = (f32[3,2048]{1,0:T(4,128)S(1)}, f32[3,2048]{1,0:T(4,128)S(1)}, u32[]{:S(2)}, u32[]{:S(2)}) collective-permute-start(f32[3,2048]{1,0:T(4,128)S(1)} %add_add_fusion.1), channel_id=1, source_target_pairs={{0,8},{1,9},{2,10},{3,11},{4,12},{5,13},{6,14},{7,15},{8,0},{9,1},... | collective-permute-start | bytes 73736 | tf_op jit(solution)/shard_map/ppermute | solution.py:44
  260.5 11.2 %all-to-all-start.2 = ((f32[32,2,512]{2,1,0:T(2,128)}), f32[32,2,512]{2,1,0:T(2,128)S(1)}, u32[]{:S(2)}, u32[]{:S(2)}) async-start(f32[32,2,512]{2,1,0:T(2,128)} %get-tuple-element.487), calls=%async_computation.2 | async-start | bytes 262144 | tf_op jit(solution)/shard_map/all_to_all | solution.py:79
  273.0 23.7 %all-to-all-start.3 = ((bf16[32,4,512]{2,1,0:T(4,128)(2,1)}), bf16[32,4,512]{2,1,0:T(4,128)(2,1)S(1)}, u32[]{:S(2)}, u32[]{:S(2)}) async-start(bf16[32,4,512]{2,1,0:T(4,128)(2,1)} %bitcast.40), calls=%async_computation.3 | async-start | bytes 262144 | tf_op jit(solution)/shard_map/all_to_all | solution.py:1963
  296.7 24.6 %all-to-all-start.4 = ((f32[32,2,512]{2,1,0:T(2,128)}), f32[32,2,512]{2,1,0:T(2,128)S(1)}, u32[]{:S(2)}, u32[]{:S(2)}) async-start(f32[32,2,512]{2,1,0:T(2,128)} %get-tuple-element.523), calls=%async_computation.4 | async-start | bytes 262144 | tf_op jit(solution)/shard_map/all_to_all | solution.py:79
  302.6 124.5 %reduce-scatter.2.cloned.1.call-start = ((), (), s32[]{:S(2)}) async-start(), calls=%async_computation.6 | async-start | bytes 3833856 | tf_op jit(solution)/shard_map/reduce_scatter | solution.py:2026
  322.0 11.4 %collective-permute-start.40 = (bf16[16,208,512]{2,1,0:T(8,128)(2,1)}, bf16[16,208,512]{2,1,0:T(8,128)(2,1)}, u32[]{:S(2)}, u32[]{:S(2)}) collective-permute-start(bf16[16,208,512]{2,1,0:T(8,128)(2,1)} %get-tuple-element.536), channel_id=1, source_target_pairs={{0,1},{1,0},{2,3},{3,2},{4,5},{5,4},{6,7},{7,6},{8,9},{9,8},{10,11... | collective-permute-start | bytes 10223624 | tf_op jit(solution)/shard_map/ppermute | solution.py:44
  339.3 5.9 %collective-permute-start.41 = (bf16[8,256,256]{2,1,0:T(8,128)(2,1)}, bf16[8,256,256]{2,1,0:T(8,128)(2,1)}, u32[]{:S(2)}, u32[]{:S(2)}) collective-permute-start(bf16[8,256,256]{2,1,0:T(8,128)(2,1)} %get-tuple-element.543), channel_id=1, source_target_pairs={{0,1},{1,0},{2,3},{3,2},{4,5},{5,4},{6,7},{7,6},{8,9},{9,8},{10,11... | collective-permute-start | bytes 3145736 | tf_op jit(solution)/shard_map/ppermute | solution.py:44
  346.8 20.5 %collective-permute-start.42 = (bf16[4,2,128,256]{3,2,0,1:T(8,128)(2,1)S(1)}, bf16[4,2,128,256]{3,2,0,1:T(8,128)(2,1)S(1)}, u32[]{:S(2)}, u32[]{:S(2)}) collective-permute-start(bf16[4,2,128,256]{3,2,0,1:T(8,128)(2,1)S(1)} %fusion.8), channel_id=1, source_target_pairs={{0,2},{1,3},{2,0},{3,1},{4,6},{5,7},{6,4},{7,5},{8,10},{9,11},{10,... | collective-permute-start | bytes 1572872 | tf_op jit(solution)/shard_map/ppermute | solution.py:44
  367.5 12.2 %collective-permute-start.43 = (bf16[4,128,256]{2,1,0:T(8,128)(2,1)S(1)}, bf16[4,128,256]{2,1,0:T(8,128)(2,1)S(1)}, u32[]{:S(2)}, u32[]{:S(2)}) collective-permute-start(bf16[4,128,256]{2,1,0:T(8,128)(2,1)S(1)} %fusion.12), channel_id=1, source_target_pairs={{0,4},{1,5},{2,6},{3,7},{4,0},{5,1},{6,2},{7,3},{8,12},{9,13},{10,... | collective-permute-start | bytes 786440 | tf_op jit(solution)/shard_map/ppermute | solution.py:44
  379.6 5.1 %collective-permute-start.44 = (bf16[8,256,256]{2,1,0:T(8,128)(2,1)}, bf16[8,256,256]{2,1,0:T(8,128)(2,1)}, u32[]{:S(2)}, u32[]{:S(2)}) collective-permute-start(bf16[8,256,256]{2,1,0:T(8,128)(2,1)} %get-tuple-element.572), channel_id=1, source_target_pairs={{0,1},{1,0},{2,3},{3,2},{4,5},{5,4},{6,7},{7,6},{8,9},{9,8},{10,11... | collective-permute-start | bytes 3145736 | tf_op jit(solution)/shard_map/ppermute | solution.py:44
  386.6 21.2 %collective-permute-start.45 = (bf16[4,2,128,256]{3,2,1,0:T(8,128)(2,1)S(1)}, bf16[4,2,128,256]{3,2,1,0:T(8,128)(2,1)}, u32[]{:S(2)}, u32[]{:S(2)}) collective-permute-start(bf16[4,2,128,256]{3,2,1,0:T(8,128)(2,1)S(1)} %fusion.6), channel_id=1, source_target_pairs={{0,2},{1,3},{2,0},{3,1},{4,6},{5,7},{6,4},{7,5},{8,10},{9,11},{10,... | collective-permute-start | bytes 1572872 | tf_op jit(solution)/shard_map/ppermute | solution.py:44
  411.2 9.6 %collective-permute-start.46 = (bf16[4,128,256]{2,1,0:T(8,128)(2,1)S(1)}, bf16[4,128,256]{2,1,0:T(8,128)(2,1)S(1)}, u32[]{:S(2)}, u32[]{:S(2)}) collective-permute-start(bf16[4,128,256]{2,1,0:T(8,128)(2,1)S(1)} %fusion.13), channel_id=1, source_target_pairs={{0,4},{1,5},{2,6},{3,7},{4,0},{5,1},{6,2},{7,3},{8,12},{9,13},{10,... | collective-permute-start | bytes 786440 | tf_op jit(solution)/shard_map/ppermute | solution.py:44
  428.7 17.5 %collective-permute-start.48 = (bf16[4,2,128,256]{3,2,1,0:T(8,128)(2,1)}, bf16[4,2,128,256]{3,2,1,0:T(8,128)(2,1)S(1)}, u32[]{:S(2)}, u32[]{:S(2)}) collective-permute-start(bf16[4,2,128,256]{3,2,1,0:T(8,128)(2,1)} %fusion.7), channel_id=1, source_target_pairs={{0,2},{1,3},{2,0},{3,1},{4,6},{5,7},{6,4},{7,5},{8,10},{9,11},{10,... | collective-permute-start | bytes 1572872 | tf_op jit(solution)/shard_map/ppermute | solution.py:44
  431.1 15.0 %collective-permute-start.49 = (bf16[2,128,256]{2,1,0:T(8,128)(2,1)}, bf16[2,128,256]{2,1,0:T(8,128)(2,1)}, u32[]{:S(2)}, u32[]{:S(2)}) collective-permute-start(bf16[2,128,256]{2,1,0:T(8,128)(2,1)} %get-tuple-element.619), channel_id=1, source_target_pairs={{0,8},{1,9},{2,10},{3,11},{4,12},{5,13},{6,14},{7,15},{8,0},{9,1},... | collective-permute-start | bytes 393224 | tf_op jit(solution)/shard_map/ppermute | solution.py:44
  432.0 14.1 %collective-permute-start.50 = (bf16[2,128,256]{2,1,0:T(8,128)(2,1)}, bf16[2,128,256]{2,1,0:T(8,128)(2,1)}, u32[]{:S(2)}, u32[]{:S(2)}) collective-permute-start(bf16[2,128,256]{2,1,0:T(8,128)(2,1)} %get-tuple-element.620), channel_id=1, source_target_pairs={{0,16},{1,17},{2,18},{3,19},{4,20},{5,21},{6,22},{7,23},{8,24},{9,... | collective-permute-start | bytes 393224 | tf_op jit(solution)/shard_map/ppermute | solution.py:44
  433.4 12.7 %collective-permute-start.51 = (bf16[2,128,256]{2,1,0:T(8,128)(2,1)S(1)}, bf16[2,128,256]{2,1,0:T(8,128)(2,1)}, u32[]{:S(2)}, u32[]{:S(2)}) collective-permute-start(bf16[2,128,256]{2,1,0:T(8,128)(2,1)S(1)} %get-tuple-element.621), channel_id=1, source_target_pairs={{0,24},{1,25},{2,26},{3,27},{4,28},{5,29},{6,30},{7,31},{8,16},{9,... | collective-permute-start | bytes 393224 | tf_op jit(solution)/shard_map/ppermute | solution.py:44
  435.5 10.7 %collective-permute-start.52 = (bf16[208,512]{1,0:T(8,128)(2,1)}, bf16[208,512]{1,0:T(8,128)(2,1)S(1)}, u32[]{:S(2)}, u32[]{:S(2)}) collective-permute-start(bf16[208,512]{1,0:T(8,128)(2,1)} %dynamic-slice_bitcast_fusion), channel_id=1, source_target_pairs={{0,2},{1,3},{2,0},{3,1},{4,6},{5,7},{6,4},{7,5},{8,10},{9,11},{10,... | collective-permute-start | bytes 638984 | tf_op jit(solution)/shard_map/ppermute | solution.py:44
  448.7 14.3 %collective-permute-start.53 = (bf16[4,128,256]{2,1,0:T(8,128)(2,1)S(1)}, bf16[4,128,256]{2,1,0:T(8,128)(2,1)S(1)}, u32[]{:S(2)}, u32[]{:S(2)}) collective-permute-start(bf16[4,128,256]{2,1,0:T(8,128)(2,1)S(1)} %fusion.14), channel_id=1, source_target_pairs={{0,4},{1,5},{2,6},{3,7},{4,0},{5,1},{6,2},{7,3},{8,12},{9,13},{10,... | collective-permute-start | bytes 786440 | tf_op jit(solution)/shard_map/ppermute | solution.py:44
  449.7 13.2 %collective-permute-start.54 = (bf16[4,40,256]{2,1,0:T(8,128)(2,1)S(1)}, bf16[4,40,256]{2,1,0:T(8,128)(2,1)S(1)}, u32[]{:S(2)}, u32[]{:S(2)}) collective-permute-start(bf16[4,40,256]{2,1,0:T(8,128)(2,1)S(1)} %fusion.48), channel_id=1, source_target_pairs={{0,4},{1,5},{2,6},{3,7},{4,0},{5,1},{6,2},{7,3},{8,12},{9,13},{10,... | collective-permute-start | bytes 245768 | tf_op jit(solution)/shard_map/ppermute | solution.py:44
  450.8 12.2 %collective-permute-start.55 = (bf16[2,128,256]{2,1,0:T(8,128)(2,1)S(1)}, bf16[2,128,256]{2,1,0:T(8,128)(2,1)S(1)}, u32[]{:S(2)}, u32[]{:S(2)}) collective-permute-start(bf16[2,128,256]{2,1,0:T(8,128)(2,1)S(1)} %fusion.20), channel_id=1, source_target_pairs={{0,1},{1,0},{2,3},{3,2},{4,5},{5,4},{6,7},{7,6},{8,9},{9,8},{10,11... | collective-permute-start | bytes 393224 | tf_op jit(solution)/shard_map/ppermute | solution.py:44
  450.8 12.2 %collective-permute-start.56 = (bf16[2,128,256]{2,1,0:T(8,128)(2,1)S(1)}, bf16[2,128,256]{2,1,0:T(8,128)(2,1)S(1)}, u32[]{:S(2)}, u32[]{:S(2)}) collective-permute-start(bf16[2,128,256]{2,1,0:T(8,128)(2,1)S(1)} %fusion.20), channel_id=1, source_target_pairs={{0,2},{1,3},{2,0},{3,1},{4,6},{5,7},{6,4},{7,5},{8,10},{9,11},{10,... | collective-permute-start | bytes 393224 | tf_op jit(solution)/shard_map/ppermute | solution.py:44
  452.7 10.2 %collective-permute-start.57 = (bf16[2,128,256]{2,1,0:T(8,128)(2,1)S(1)}, bf16[2,128,256]{2,1,0:T(8,128)(2,1)S(1)}, u32[]{:S(2)}, u32[]{:S(2)}) collective-permute-start(bf16[2,128,256]{2,1,0:T(8,128)(2,1)S(1)} %fusion.20), channel_id=1, source_target_pairs={{0,3},{1,2},{2,1},{3,0},{4,7},{5,6},{6,5},{7,4},{8,11},{9,10},{10,... | collective-permute-start | bytes 393224 | tf_op jit(solution)/shard_map/ppermute | solution.py:44
  463.1 6.3 %collective-permute-start.58 = (bf16[168,256]{1,0:T(8,128)(2,1)S(1)}, bf16[168,256]{1,0:T(8,128)(2,1)S(1)}, u32[]{:S(2)}, u32[]{:S(2)}) collective-permute-start(bf16[168,256]{1,0:T(8,128)(2,1)S(1)} %get-tuple-element.644), channel_id=1, source_target_pairs={{0,8},{1,9},{2,10},{3,11},{4,12},{5,13},{6,14},{7,15},{8,0},{9,1},... | collective-permute-start | bytes 258056 | tf_op jit(solution)/shard_map/ppermute | solution.py:44
  464.1 9.9 %collective-permute-start.59 = (bf16[168,256]{1,0:T(8,128)(2,1)S(1)}, bf16[168,256]{1,0:T(8,128)(2,1)S(1)}, u32[]{:S(2)}, u32[]{:S(2)}) collective-permute-start(bf16[168,256]{1,0:T(8,128)(2,1)S(1)} %get-tuple-element.645), channel_id=1, source_target_pairs={{0,16},{1,17},{2,18},{3,19},{4,20},{5,21},{6,22},{7,23},{8,24},{9,... | collective-permute-start | bytes 258056 | tf_op jit(solution)/shard_map/ppermute | solution.py:44
  466.4 7.6 %collective-permute-start.60 = (bf16[168,256]{1,0:T(8,128)(2,1)S(1)}, bf16[168,256]{1,0:T(8,128)(2,1)S(1)}, u32[]{:S(2)}, u32[]{:S(2)}) collective-permute-start(bf16[168,256]{1,0:T(8,128)(2,1)S(1)} %get-tuple-element.646), channel_id=1, source_target_pairs={{0,24},{1,25},{2,26},{3,27},{4,28},{5,29},{6,30},{7,31},{8,16},{9,... | collective-permute-start | bytes 258056 | tf_op jit(solution)/shard_map/ppermute | solution.py:44
  467.6 6.4 %collective-permute-start.61 = (bf16[208,512]{1,0:T(8,128)(2,1)S(1)}, bf16[208,512]{1,0:T(8,128)(2,1)S(1)}, u32[]{:S(2)}, u32[]{:S(2)}) collective-permute-start(bf16[208,512]{1,0:T(8,128)(2,1)S(1)} %fusion.11), channel_id=1, source_target_pairs={{0,1},{1,0},{2,3},{3,2},{4,5},{5,4},{6,7},{7,6},{8,9},{9,8},{10,11... | collective-permute-start | bytes 638984 | tf_op jit(solution)/shard_map/ppermute | solution.py:44
  467.6 8.0 %collective-permute-start.62 = (bf16[208,512]{1,0:T(8,128)(2,1)S(1)}, bf16[208,512]{1,0:T(8,128)(2,1)S(1)}, u32[]{:S(2)}, u32[]{:S(2)}) collective-permute-start(bf16[208,512]{1,0:T(8,128)(2,1)S(1)} %fusion.11), channel_id=1, source_target_pairs={{0,2},{1,3},{2,0},{3,1},{4,6},{5,7},{6,4},{7,5},{8,10},{9,11},{10,... | collective-permute-start | bytes 638984 | tf_op jit(solution)/shard_map/ppermute | solution.py:44
  469.5 9.9 %collective-permute-start.63 = (bf16[208,512]{1,0:T(8,128)(2,1)S(1)}, bf16[208,512]{1,0:T(8,128)(2,1)S(1)}, u32[]{:S(2)}, u32[]{:S(2)}) collective-permute-start(bf16[208,512]{1,0:T(8,128)(2,1)S(1)} %fusion.11), channel_id=1, source_target_pairs={{0,3},{1,2},{2,1},{3,0},{4,7},{5,6},{6,5},{7,4},{8,11},{9,10},{10,... | collective-permute-start | bytes 638984 | tf_op jit(solution)/shard_map/ppermute | solution.py:44
  479.5 4.9 collective-permute-start.64
  479.7 4.7 collective-permute-start.65
  481.5 4.7 collective-permute-start.66
  (44 other events, 428.2 us)
Sparse Core Ops, SparseCore 0:
  95.3 63.0 all-gather.2
  345.4 81.7 reduce-scatter.1
